TPU v7x, 32 devices: a whole 2x2x4 slice. The times are simulated.
32 devices in a mesh: seq: 8 (over y, x, core), res: 4 (over z).
Axes of the slice: x: 2, y: 2, z: 4, core: 2. Of those that a mesh axis runs over, the one named last changes fastest.
Arguments:
- coupled_embedding: float32 [192, 192, 128], P(('res', 'seq')), may hold values from -6 to 6
- aligned_embedding: float32 [16, 192, 256], P('seq', 'res'), may hold values from -6 to 6
- coupled_change_adjoint: float32 [192, 192, 128], P(('res', 'seq')), may hold values from -6 to 6
- aligned_change_adjoint: float32 [16, 192, 256], P('seq', 'res'), may hold values from -6 to 6
- coupled_scaler: float32 [128], replicated, may hold values from 0.25 to 1.75
- coupled_asking_matrix: float32 [128, 128], replicated, may hold values from -24 to 24
- coupled_lookup_matrix: float32 [128, 128], replicated, may hold values from -1 to 1
- coupled_content_matrix: float32 [128, 128], replicated, may hold values from -0.5 to 0.5
- coupled_sigmoid_matrix: float32 [128, 128], replicated, may hold values from -0.5 to 0.5
- coupled_offset_matrix: float32 [128, 4], replicated, may hold values from -1 to 1
- coupled_result_matrix: float32 [128, 128], replicated, may hold values from -0.5 to 0.5
- aligned_scaler: float32 [256], replicated, may hold values from 0.25 to 1.75
- coupled_scaler_for_offset: float32 [128], replicated, may hold values from 0.25 to 1.75
- aligned_asking_matrix: float32 [256, 256], replicated, may hold values from -24 to 24
- aligned_lookup_matrix: float32 [256, 256], replicated, may hold values from -1 to 1
- aligned_content_matrix: float32 [256, 256], replicated, may hold values from -0.375 to 0.375
- aligned_sigmoid_matrix: float32 [256, 256], replicated, may hold values from -0.375 to 0.375
- aligned_offset_matrix: float32 [128, 8], replicated, may hold values from -1 to 1
- aligned_result_matrix: float32 [256, 256], replicated, may hold values from -0.375 to 0.375
Outputs:
- coupled_embedding_sensitivity: float32 [192, 192, 128], P(('res', 'seq'))
- aligned_embedding_sensitivity: float32 [16, 192, 256], P('seq', 'res')
All inputs are finite; a program needn't handle non-finite values.
Results may differ from a plain program's by a relative error of at most 0.0003.
Values sent between devices are 32-bit elements; how exact they have to be, the bound alone decides.
No kernel may reach another device: no remote copies, remote signals or barrier semaphores. Data moves between devices by JAX's collectives and lax.ppermute only.
A program may use at most 192 MiB of HBM per device.

v0:
```python
import math

import jax
import jax.numpy as jnp
from jax import lax
from jax.sharding import PartitionSpec as P

HP = 4
ALIGNED_SPLITS = 8


EXACT_MATMUL = lax.Precision.HIGHEST
EPSILON = 1e-05


def standardize_features(values, norm_gain):
    center = values - jnp.mean(values, axis=-1, keepdims=True)
    spread = jnp.mean(center * center, axis=-1, keepdims=True)
    return center * lax.rsqrt(spread + EPSILON) * norm_gain


def affine_map(values, weight):
    return jnp.einsum("...c,ce->...e", values, weight, precision=EXACT_MATMUL)


def sigmoid_mixing(query_vectors, key_rows, value_rows, gate_preact, softmax_offset, head_count):
    query_shape = query_vectors.shape
    head_width = query_shape[-1] // head_count
    query_heads = query_vectors.reshape(query_shape[:-1] + (head_count, head_width))
    key_heads = key_rows.reshape(key_rows.shape[:-1] + (head_count, head_width))
    value_heads = value_rows.reshape(value_rows.shape[:-1] + (head_count, head_width))
    logits = (
        jnp.einsum("...qhd,...khd->...qhk", query_heads, key_heads, precision=EXACT_MATMUL)
        / math.sqrt(head_width)
        + softmax_offset
    )
    largest = lax.stop_gradient(jnp.max(logits, axis=-1, keepdims=True))
    weights = jnp.exp(logits - largest)
    weights = weights / jnp.sum(weights, axis=-1, keepdims=True)
    mixed_contents = jnp.einsum(
        "...qhk,...khd->...qhd", weights, value_heads, precision=EXACT_MATMUL
    )
    return mixed_contents.reshape(query_shape) * jax.nn.sigmoid(gate_preact)


def on_device(
    coupled_embedding,
    aligned_embedding,
    coupled_change_adjoint,
    aligned_change_adjoint,
    coupled_scaler,
    coupled_asking_matrix,
    coupled_lookup_matrix,
    coupled_content_matrix,
    coupled_sigmoid_matrix,
    coupled_offset_matrix,
    coupled_result_matrix,
    aligned_scaler,
    coupled_scaler_for_offset,
    aligned_asking_matrix,
    aligned_lookup_matrix,
    aligned_content_matrix,
    aligned_sigmoid_matrix,
    aligned_offset_matrix,
    aligned_result_matrix,
):

    def pair_local(entering_lines):
        standardized_source = standardize_features(entering_lines, coupled_scaler)
        return (
            affine_map(standardized_source, coupled_asking_matrix),
            affine_map(standardized_source, coupled_lookup_matrix),
            affine_map(standardized_source, coupled_content_matrix),
            affine_map(standardized_source, coupled_sigmoid_matrix),
            jnp.einsum(
                "jkc,ch->jhk", standardized_source, coupled_offset_matrix, precision=EXACT_MATMUL
            ),
        )

    (row_queries, row_keys, row_values, row_gates, bias_rows), pair_back = jax.vjp(
        pair_local, coupled_embedding
    )
    by_seq = lax.all_gather(bias_rows, "seq", axis=0, tiled=True)
    full_bias = lax.all_gather(by_seq, "res", axis=0, tiled=True)

    def row_output(one_query, one_key, one_value, one_gate, softmax_offset):
        return affine_map(
            sigmoid_mixing(one_query, one_key, one_value, one_gate, softmax_offset, HP),
            coupled_result_matrix,
        )

    def row_step(bias_sum, row_items):
        one_query, one_key, one_value, one_gate, one_cotan = row_items
        discarded_entry, row_back = jax.vjp(
            row_output, one_query, one_key, one_value, one_gate, full_bias
        )
        grad_query, grad_key, grad_value, grad_gate, grad_bias = row_back(one_cotan)
        return (bias_sum + grad_bias, (grad_query, grad_key, grad_value, grad_gate))

    bias_total, row_grads = lax.scan(
        row_step,
        jnp.zeros_like(full_bias),
        (row_queries, row_keys, row_values, row_gates, coupled_change_adjoint),
    )
    by_res = lax.psum_scatter(bias_total, "res", scatter_dimension=0, tiled=True)
    bias_grad_rows = lax.psum_scatter(by_res, "seq", scatter_dimension=0, tiled=True)
    (mixed_result_sensitivity,) = pair_back(row_grads + (bias_grad_rows,))

    def aligned_offset_portion(entering_lines):
        return jnp.einsum(
            "gys,sj->gjy",
            standardize_features(entering_lines, coupled_scaler_for_offset),
            aligned_offset_matrix,
            precision=EXACT_MATMUL,
        )

    aligned_offset_part, aligned_offset_reverse = jax.vjp(aligned_offset_portion, coupled_embedding)
    tile_softmax_offset = lax.all_gather(aligned_offset_part, "seq", axis=0, tiled=True)

    def sequence_output(query_vectors, full_key_rows, full_value_rows, gate_preact, softmax_offset):
        return affine_map(
            sigmoid_mixing(
                query_vectors,
                full_key_rows,
                full_value_rows,
                gate_preact,
                softmax_offset,
                ALIGNED_SPLITS,
            ),
            aligned_result_matrix,
        )

    state_all = lax.all_gather(aligned_embedding, "res", axis=1, tiled=True)

    def near_local(carry_pile):
        standardized_source = standardize_features(carry_pile, aligned_scaler)
        return (
            affine_map(standardized_source, aligned_asking_matrix),
            affine_map(standardized_source, aligned_sigmoid_matrix),
        )

    def keys_local(carry_pile):
        standardized_source = standardize_features(carry_pile, aligned_scaler)
        return (
            affine_map(standardized_source, aligned_lookup_matrix),
            affine_map(standardized_source, aligned_content_matrix),
        )

    (aligned_asking_lines, aligned_sigmoid_factors), near_back = jax.vjp(
        near_local, aligned_embedding
    )
    (full_key_rows, full_value_rows), keys_back = jax.vjp(keys_local, state_all)
    discarded_entry, sigmoid_mixing_reverse = jax.vjp(
        sequence_output,
        aligned_asking_lines,
        full_key_rows,
        full_value_rows,
        aligned_sigmoid_factors,
        tile_softmax_offset,
    )
    query_gradient, full_key_gradient, full_value_gradient, gate_gradient, block_bias_gradient = (
        sigmoid_mixing_reverse(aligned_change_adjoint)
    )
    (state_term,) = keys_back((full_key_gradient, full_value_gradient))
    spread_grad = lax.psum_scatter(state_term, "res", scatter_dimension=1, tiled=True)
    (near_grad,) = near_back((query_gradient, gate_gradient))
    aligned_embedding_sensitivity = near_grad + spread_grad
    offset_line_sensitivity = lax.psum_scatter(
        block_bias_gradient, "seq", scatter_dimension=0, tiled=True
    )
    (coupled_sensitivity_via_offset,) = aligned_offset_reverse(offset_line_sensitivity)
    return (
        mixed_result_sensitivity + coupled_sensitivity_via_offset,
        aligned_embedding_sensitivity,
    )


def solution(mesh):
    in_specs = (
        P(("res", "seq"), None, None),
        P("seq", "res", None),
        P(("res", "seq"), None, None),
        P("seq", "res", None),
        P(),
        P(),
        P(),
        P(),
        P(),
        P(),
        P(),
        P(),
        P(),
        P(),
        P(),
        P(),
        P(),
        P(),
        P(),
    )
    out_specs = (P(("res", "seq"), None, None), P("seq", "res", None))
    return jax.shard_map(
        on_device, mesh=mesh, in_specs=in_specs, out_specs=out_specs, check_vma=False
    )
```

profile of v0, /device:TPU:0, one launch (start us, length us, event | category | flops | bytes accessed | tf_op | source)
XLA Modules:
  0.0 319.2 jit_solution(9007783397290859417)
XLA Ops:
  12.6 10.7 %all_gather.12 = f32[48,4,192]{2,1,0:T(4,128)S(1)} all-gather(f32[6,4,192]{2,1,0:T(4,128)S(1)} %convolution_bitcast_fusion.1), channel_id=1, replica_groups=mesh['seq'=8,'res'=4] {'seq'}, dimensions={0}, use_global_device_ids=true | all-gather | bytes 165888 | tf_op jit(solution)/shard_map/all_gather | solution.py:83
  23.3 20.0 %all_gather.13 = f32[192,4,192]{2,1,0:T(4,128)S(1)} all-gather(f32[48,4,192]{2,1,0:T(4,128)S(1)} %all_gather.12), channel_id=1, replica_groups=mesh['seq'=8,'res'=4] {'res'}, dimensions={0}, use_global_device_ids=true | all-gather | bytes 737280 | tf_op jit(solution)/shard_map/all_gather | solution.py:84
  45.7 2.4 fusion.70
  48.1 2.4 fusion.71
  50.5 1.6 fusion.72
  52.2 99.2 %while.19 = (s32[]{:T(128)}, f32[192,4,192]{0,2,1:T(8,128)}, f32[6,192,128]{1,2,0:T(8,128)}, f32[6,192,128]{1,2,0:T(8,128)}, f32[6,192,128]{1,2,0:T(8,128)}, /*i...) while((s32[]{:T(128)}, f32[192,4,192]{0,2,1:T(8,128)}, ...), condition=%wide.region_6.0_spmd.clone, body=%wide.region_2.6_spmd.clone.sunk | while | flops 381444096 | bytes 21477280 | solution.py:100
  59.6 1.6 fusion.192
  75.2 1.6 fusion.192
  82.2 2.3 fusion.186
  91.9 1.6 fusion.192
  98.9 2.3 fusion.186
  108.6 1.6 fusion.192
  115.6 2.3 fusion.186
  125.3 1.6 fusion.192
  132.3 2.3 fusion.186
  142.1 1.6 fusion.192
  149.1 2.3 fusion.186
  151.4 2.4 copy.107
  154.7 18.0 %all_gather.14 = f32[2,192,256]{2,1,0:T(8,128)S(1)} all-gather(f32[2,48,256]{2,1,0:T(8,128)S(1)} %copy-done.13), channel_id=1, replica_groups=mesh['seq'=8,'res'=4] {'res'}, dimensions={1}, use_global_device_ids=true | all-gather | bytes 491520 | tf_op jit(solution)/shard_map/all_gather | solution.py:133
  175.1 10.0 %all_gather.15 = f32[48,8,192]{2,1,0:T(8,128)S(1)} all-gather(f32[6,8,192]{2,1,0:T(8,128)S(1)} %convolution_bitcast_fusion), channel_id=1, replica_groups=mesh['seq'=8,'res'=4] {'seq'}, dimensions={0}, use_global_device_ids=true | all-gather | bytes 331776 | tf_op jit(solution)/shard_map/all_gather | solution.py:118
  190.4 1.6 fusion.42
  195.0 2.1 fusion.36
  204.8 1.8 multiply_reduce_fusion.3
  210.0 1.6 constant_dynamic-slice_fusion.3
  211.9 2.0 broadcast_add_fusion
  227.7 4.1 %reduce-scatter.3.cloned.1.call-done = f32[6,8,192]{2,1,0:T(8,128)} async-done(((f32[48,8,192]{2,1,0:T(8,128)}), f32[6,8,192]{2,1,0:T(8,128)}) %reduce-scatter.3.cloned.1.call-update) | async-done | bytes 36880 | tf_op jit(solution)/shard_map/reduce_scatter | solution.py:168
  231.8 1.9 convolution_multiply_fusion.2
  233.7 54.0 %all-reduce.7.cloned.1.call-done = f32[48,4,192]{2,1,0:T(4,128)} async-done(((f32[48,4,192]{2,1,0:T(4,128)}), f32[48,4,192]{2,1,0:T(4,128)}) %all-reduce.7.cloned.1.call-update) | async-done | bytes 147472
  287.7 2.8 multiply_reduce_fusion.1
  291.9 2.1 add_add_fusion.3
  294.0 15.9 %reduce-scatter.5.cloned.1.call-done = f32[2,48,256]{2,1,0:T(8,128)} async-done(((f32[2,192,256]{2,1,0:T(8,128)}), f32[2,48,256]{2,1,0:T(8,128)}) %reduce-scatter.5.cloned.1.call-update) | async-done | bytes 98320 | tf_op jit(solution)/shard_map/reduce_scatter | solution.py:165
  309.9 1.7 add_add_fusion.5
  (399 shorter events, 120.1 us)
Async XLA Ops:
  8.0 178.6 %copy-start = (f32[256,256]{1,0:T(8,128)S(1)}, f32[256,256]{1,0:T(8,128)}, u32[]{:S(2)}) copy-start(f32[256,256]{1,0:T(8,128)} %param.35) | copy-start | bytes 786436
  8.0 201.9 %all-reduce.5.cloned.1.call-start = ((), (), s32[]{:S(2)}) async-start(), calls=%async_computation.4 | async-start | bytes 1572864
  11.4 39.2 %copy-start.30 = (f32[6,192]{1,0:T(8,128)}, f32[6,192]{1,0:T(8,128)S(1)}, u32[]{:S(2)}) copy-start(f32[6,192]{1,0:T(8,128)S(1)} %fusion.102) | copy-start | bytes 13828
  45.7 2.5 copy-start.46
  48.1 2.4 copy-start.37
  59.6 1.6 copy-start.6
  59.6 1.6 copy-start.8
  75.1 1.6 copy-start.6
  75.1 1.6 copy-start.8
  82.1 2.3 copy-start.17
  91.9 1.6 copy-start.6
  98.9 2.3 copy-start.17
  108.6 1.6 copy-start.6
  115.6 2.3 copy-start.17
  125.3 1.6 copy-start.6
  132.3 2.3 copy-start.17
  142.1 1.6 copy-start.6
  149.1 2.3 copy-start.17
  153.8 19.4 %copy-start.2 = (f32[6,192,128]{2,1,0:T(8,128)S(1)}, f32[6,192,128]{2,1,0:T(8,128)}, u32[]{:S(2)}) copy-start(f32[6,192,128]{2,1,0:T(8,128)} %param.21) | copy-start | bytes 1769476
  153.8 78.0 %reduce-scatter.3.cloned.1.call-start = ((), (), s32[]{:S(2)}) async-start(), calls=%async_computation.2 | async-start | bytes 442368 | tf_op jit(solution)/shard_map/reduce_scatter | solution.py:168
  154.7 18.5 %copy-start.31 = (f32[6,192]{1,0:T(8,128)S(1)}, f32[6,192]{1,0:T(8,128)}, u32[]{:S(2)}) copy-start(f32[6,192]{1,0:T(8,128)} %copy-done.30) | copy-start | bytes 13828
  154.7 18.5 %copy-start.62 = (f32[128]{0:T(128)S(1)}, f32[128]{0:T(128)}, u32[]{:S(2)}) copy-start(f32[128]{0:T(128)} %param.33) | copy-start | bytes 1540
  186.7 5.3 %copy-start.56 = (f32[2,48]{1,0:T(2,128)}, f32[2,48]{1,0:T(2,128)S(1)}, u32[]{:S(2)}) copy-start(f32[2,48]{1,0:T(2,128)S(1)} %fusion.109) | copy-start | bytes 1156
  199.1 1.7 copy-start.15
  199.1 88.7 %all-reduce.7.cloned.1.call-start = ((), (), s32[]{:S(2)}) async-start(), calls=%async_computation.5 | async-start | bytes 393216
  211.6 98.3 %reduce-scatter.5.cloned.1.call-start = ((), (), s32[]{:S(2)}) async-start(), calls=%async_computation.3 | async-start | bytes 491520 | tf_op jit(solution)/shard_map/reduce_scatter | solution.py:165
  216.4 4.2 %copy-start.43 = (f32[128,128]{1,0:T(8,128)S(1)}, f32[128,128]{1,0:T(8,128)}, u32[]{:S(2)}) copy-start(f32[128,128]{1,0:T(8,128)} %param.26) | copy-start | bytes 196612
  217.4 3.2 %copy-start.27 = (f32[6,192,128]{1,2,0:T(8,128)S(1)}, f32[6,192,128]{1,2,0:T(8,128)}, u32[]{:S(2)}) copy-start(f32[6,192,128]{1,2,0:T(8,128)} %get-tuple-element.77) | copy-start | bytes 1769476
  227.0 4.8 %copy-start.63 = (f32[128]{0:T(128)S(1)}, f32[128]{0:T(128)}, u32[]{:S(2)}) copy-start(f32[128]{0:T(128)} %param.33) | copy-start | bytes 1540
  227.7 60.1 %copy-start.54 = (f32[128]{0:T(128)S(1)}, f32[128]{0:T(128)}, u32[]{:S(2)}) copy-start(f32[128]{0:T(128)} %param.25) | copy-start | bytes 1540
  227.7 60.1 %copy-start.61 = (f32[128,4]{0,1:T(4,128)S(1)}, f32[128,4]{0,1:T(4,128)}, u32[]{:S(2)}) copy-start(f32[128,4]{0,1:T(4,128)} %param.30) | copy-start | bytes 6148
  287.7 2.8 copy-start.50
  (83 other events, 80.8 us)
Sparse Core Ops, SparseCore 0:
  153.9 46.4 all-reduce.4
Sparse Core Ops, SparseCore 1:
  199.1 32.6 reduce-scatter.2
  234.7 52.9 all-reduce.6
  289.9 20.0 reduce-scatter.4
where the time goes:
time: 321 us; the launch traced here: 319 us
  waiting for transfers between devices  74.1 us (23%)
  matrix products  72.6 us (23%)
  blocking collectives  58.7 us (18%)
  local copies, waits for them, and re-layouts  54.3 us (17%)
  other arithmetic  40.4 us (13%)
  between operations  17.7 us (6%)
    unnamed x6, waiting for transfers between devices  54.1 us
    dot_general x22, matrix products, affine_map(): return jnp.einsum('...c,ce->...e', values, weight, precision=EXACT_MATMUL)  28.6 us
    all_gather x1, blocking collectives, on_device(): full_bias = lax.all_gather(by_seq, 'res', axis=0, tiled=True)  20 us
    dot_general x21, matrix products, sigmoid_mixing(): jnp.einsum('...qhk,...khd->...qhd', weights, value_heads, precision=EXACT...  18.9 us
    all_gather x1, blocking collectives, on_device(): state_all = lax.all_gather(aligned_embedding, 'res', axis=1, tiled=True)  18 us
    dot_general x21, matrix products, sigmoid_mixing(): jnp.einsum('...qhd,...khd->...qhk', query_heads, key_heads, precision=EXA...  17.3 us
    unnamed x118, local copies, waits for them, and re-layouts  16.2 us
    reduce_scatter x1, waiting for transfers between devices, on_device(): lax.psum_scatter(state_term, 'res', scatter_dimension=1, tiled=True)  15.9 us
  transfers between devices with their start and end apart: 4, of which 3 were waited for; matrix products, arithmetic and copies ran while one was open for 13% of the time, Pallas kernels for 0%

commit v1 on v0

--- a/solution.py
+++ b/solution.py
@@ -1,8 +1,11 @@
+import functools
 import math
 
 import jax
 import jax.numpy as jnp
 from jax import lax
+from jax.experimental import pallas as pl
+from jax.experimental.pallas import tpu as pltpu
 from jax.sharding import PartitionSpec as P
 
 HP = 4
@@ -43,7 +46,7 @@
     return mixed_contents.reshape(query_shape) * jax.nn.sigmoid(gate_preact)
 
 
-def on_device(
+def scanned_on_device(
     coupled_embedding,
     aligned_embedding,
     coupled_change_adjoint,
@@ -175,6 +178,460 @@
     )
 
 
+F32 = jnp.float32
+BF16 = jnp.bfloat16
+HEAD = 32
+LANES = 128
+
+
+def split2(a):
+    top = a.astype(BF16)
+    return top, (a - top.astype(F32)).astype(BF16)
+
+
+def split3(a):
+    top = a.astype(BF16)
+    rest = a - top.astype(F32)
+    mid = rest.astype(BF16)
+    return top, mid, (rest - mid.astype(F32)).astype(BF16)
+
+
+def left6(parts):
+    a, b, c = parts
+    return [a, a, b, b, a, c]
+
+
+def right6(parts):
+    a, b, c = parts
+    return [a, b, a, b, c, a]
+
+
+def left3(parts):
+    return [parts[0], parts[0], parts[1]]
+
+
+def right3(parts):
+    return [parts[0], parts[1], parts[0]]
+
+
+def nn(a, b):
+    return lax.dot_general(a, b, (((1,), (0,)), ((), ())), preferred_element_type=F32)
+
+
+def nt(a, b):
+    return lax.dot_general(a, b, (((1,), (1,)), ((), ())), preferred_element_type=F32)
+
+
+def cat(parts, axis):
+    return jnp.concatenate(parts, axis=axis)
+
+
+def normed(v):
+    center = v - jnp.mean(v, axis=-1, keepdims=True)
+    spread = jnp.mean(center * center, axis=-1, keepdims=True)
+    scale = lax.rsqrt(spread + EPSILON)
+    return center * scale, scale
+
+
+def normed_back(n, scale, dn):
+    return scale * (
+        dn - jnp.mean(dn, axis=-1, keepdims=True) - n * jnp.mean(dn * n, axis=-1, keepdims=True)
+    )
+
+
+def head_mask(h, dtype):
+    lane = lax.broadcasted_iota(jnp.int32, (1, LANES), 1)
+    return jnp.where((lane // HEAD) == h, 1.0, 0.0).astype(dtype)
+
+
+def bias_kernel(rows, x_ref, g_ref, wp_ref, g2_ref, wm_ref, bp_ref, bm_ref):
+    hp, hm = wp_ref.shape[0], wm_ref.shape[0]
+    w = cat([wp_ref[...] * g_ref[...], wm_ref[...] * g2_ref[...]], 0)
+    wcat = cat(left6(split3(w)), 1)
+    for j in range(rows):
+        n, _ = normed(x_ref[j])
+        res = nt(wcat, cat(right6(split3(n)), 1))
+        for h in range(hp):
+            bp_ref[h * rows + j : h * rows + j + 1, :] = res[h : h + 1]
+        for h in range(hm):
+            bm_ref[h * rows + j : h * rows + j + 1, :] = res[hp + h : hp + h + 1]
+
+
+def place(axis_sizes):
+    seq_n, res_n = axis_sizes
+    return lax.axis_index("seq"), lax.axis_index("res")
+
+
+def pair_kernel(
+    dims,
+    x_ref, adj_ref, own_ref, other_ref,
+    g_ref, wq_ref, wk_ref, wv_ref, wg_ref, wo_ref,
+    dn_ref, near_ref, far_ref,
+    bt, dbt, w6, w3, wo3, wb,
+):
+    rows, heads, seq_n, res_n = dims
+    step = pl.program_id(0)
+    seq, res = lax.axis_index("seq"), lax.axis_index("res")
+    core, chip = lax.rem(seq, 2), lax.div(seq, 2)
+    n_keys = x_ref.shape[1]
+
+    @pl.when(step == 0)
+    def _():
+        g = g_ref[...]
+        wq = wq_ref[...] * g * (1.0 / math.sqrt(HEAD))
+        wk = wk_ref[...] * g
+        wv = wv_ref[...] * g
+        wg = wg_ref[...] * g
+        w6[...] = cat(right6(split3(cat([wq, wk], 1))), 0)
+        w3[...] = cat(right3(split2(cat([wv, wg], 1))), 0)
+        wo3[...] = cat(right3(split2(wo_ref[...])), 1)
+        top, low = split2(cat([wq, wk, wv, wg], 1))
+        wb[0] = top
+        wb[1] = low
+        for z in range(res_n):
+            zi = lax.bitwise_xor(res, z)
+            for s in range(seq_n):
+                ci = lax.bitwise_xor(chip, s // 2)
+                block = jnp.where(core == s % 2, own_ref[ci, zi], other_ref[ci, zi])
+                d = z * seq_n + s
+                for h in range(heads):
+                    dbt[h, d * rows : (d + 1) * rows, :] = block[h * rows : (h + 1) * rows]
+        for h in range(heads):
+            bt[h] = dbt[h].T
+        dbt[...] = jnp.zeros_like(dbt)
+
+    n, _ = normed(x_ref[0])
+    parts = split3(n)
+    qk = nn(cat(left6(parts), 1), w6[...])
+    vg = nn(cat(left3(parts), 1), w3[...])
+    q, k, v, gate = qk[:, :LANES], qk[:, LANES:], vg[:, :LANES], vg[:, LANES:]
+    d_out = nt(cat(left3(split2(adj_ref[0])), 1), wo3[...])
+    sig = jax.nn.sigmoid(gate)
+    d_mix = d_out * sig
+    q1, q2, q3 = split3(q)
+    ks = split3(k)
+    kcat = cat(left6(ks), 1)
+    vs = split2(v)
+    vcat = cat(left3(vs), 1)
+    kt1, kt2 = split2(k.T)
+    vt1, vt2 = split2(v.T)
+    m1, m2 = split2(d_mix)
+    mixed, dq = [], []
+    dk = jnp.zeros((n_keys, LANES), F32)
+    dv = jnp.zeros((n_keys, LANES), F32)
+    for h in range(heads):
+        mask = head_mask(h, BF16)
+        qh = (q1 * mask, q2 * mask, q3 * mask)
+        mh = (m1 * mask, m2 * mask)
+        band = slice(h * HEAD, (h + 1) * HEAD)
+        s = nt(kcat, cat(right6(qh), 1)) + bt[h]
+        e = jnp.exp(s - jnp.max(s, axis=0, keepdims=True))
+        p = e * (1.0 / jnp.sum(e, axis=0, keepdims=True))
+        p1, p2 = split2(p)
+        both = nn(cat([vt1[band], vt2[band]], 0), p1)
+        mixed.append(both[:HEAD] + both[HEAD:] + nn(vt1[band], p2))
+        dp = nt(vcat, cat(right3(mh), 1))
+        ds = p * (dp - jnp.sum(p * dp, axis=0, keepdims=True))
+        dbt[h] = dbt[h] + ds
+        s1, s2 = split2(ds)
+        both = nn(cat([kt1[band], kt2[band]], 0), s1)
+        dq.append(both[:HEAD] + both[HEAD:] + nn(kt1[band], s2))
+        both = nn(s1, cat(qh[:2], 1))
+        dk = dk + both[:, :LANES] + both[:, LANES:] + nn(s2, qh[0])
+        both = nn(p1, cat(mh, 1))
+        dv = dv + both[:, :LANES] + both[:, LANES:] + nn(p2, mh[0])
+    o = cat(mixed, 0).T
+    d_gate = d_out * o * sig * (1.0 - sig)
+    t1, t2 = split2(cat([cat(dq, 0).T, dk, dv, d_gate], 1))
+    dn_ref[0] = nt(t1, wb[0]) + nt(t1, wb[1]) + nt(t2, wb[0])
+
+    @pl.when(step == rows - 1)
+    def _():
+        for h in range(heads):
+            bt[h] = dbt[h].T
+        for z in range(res_n):
+            zi = lax.bitwise_xor(res, z)
+            for s in range(seq_n):
+                ci = lax.bitwise_xor(chip, s // 2)
+                d = z * seq_n + s
+                block = cat([bt[h, d * rows : (d + 1) * rows, :] for h in range(heads)], 0)
+
+                @pl.when(core == s % 2)
+                def _():
+                    near_ref[ci, zi] = block
+
+                @pl.when(core != s % 2)
+                def _():
+                    far_ref[ci, zi] = block
+
+
+def msa_kernel(
+    dims,
+    y0_ref, y1_ref, y2_ref, y3_ref, adj_ref, own_ref, other_ref,
+    g_ref, wq_ref, wk_ref, wv_ref, wg_ref, wo_ref,
+    dy_ref, r0_ref, r1_ref, r2_ref, r3_ref, near_ref, far_ref,
+    bias, dbias, yall, dyall,
+):
+    rows, heads, seq_n, res_n = dims
+    seq, res = lax.axis_index("seq"), lax.axis_index("res")
+    core, chip = lax.rem(seq, 2), lax.div(seq, 2)
+    n_seqs, own, feats = y0_ref.shape
+    n_keys = own * res_n
+    tiles = feats // LANES
+    g = g_ref[...]
+    wq = wq_ref[...] * g * (1.0 / math.sqrt(HEAD))
+    wk = wk_ref[...] * g
+    wv = wv_ref[...] * g
+    wg = wg_ref[...] * g
+
+    for t, ref in enumerate((y0_ref, y1_ref, y2_ref, y3_ref)):
+        at = pl.multiple_of(lax.bitwise_xor(res, t) * own, own)
+        for b in range(n_seqs):
+            yall[b, pl.ds(at, own), :] = ref[b]
+    for s in range(seq_n):
+        ci = lax.bitwise_xor(chip, s // 2)
+        block = jnp.where(core == s % 2, own_ref[ci], other_ref[ci])
+        for h in range(heads):
+            bias[h, s * rows : (s + 1) * rows, :] = block[h * rows : (h + 1) * rows]
+
+    n_own, _ = normed(y0_ref[...].reshape(n_seqs * own, feats))
+    n_all, _ = normed(yall[...].reshape(n_seqs * n_keys, feats))
+    own_parts, all_parts = split3(n_own), split3(n_all)
+    q = nn(cat(left6(own_parts), 1), cat(right6(split3(wq)), 0))
+    gate = nn(cat(left3(own_parts), 1), cat(right3(split2(wg)), 0))
+    k = nn(cat(left6(all_parts), 1), cat(right6(split3(wk)), 0))
+    v = nn(cat(left3(all_parts), 1), cat(right3(split2(wv)), 0))
+    adj = adj_ref[...].reshape(n_seqs * own, feats)
+    d_out = nt(cat(left3(split2(adj)), 1), cat(right3(split2(wo_ref[...])), 1))
+    sig = jax.nn.sigmoid(gate)
+    d_mix = d_out * sig
+    mixes, dqs = [], []
+    for b in range(n_seqs):
+        near = slice(b * own, (b + 1) * own)
+        wide = slice(b * n_keys, (b + 1) * n_keys)
+        mix_tiles, dq_tiles, dkt, dvt = [], [], [], []
+        for t in range(tiles):
+            cols = slice(t * LANES, (t + 1) * LANES)
+            q_t, k_t, v_t, m_t = q[near, cols], k[wide, cols], v[wide, cols], d_mix[near, cols]
+            qp = split3(q_t)
+            kp = split3(k_t)
+            vp = split2(v_t)
+            mp = split2(m_t)
+            qt1, qt2 = split2(q_t.T)
+            mt1, mt2 = split2(m_t.T)
+            kcat = cat(right6(kp), 1)
+            vcat = cat(right3(vp), 1)
+            mix = jnp.zeros((own, LANES), F32)
+            dq = jnp.zeros((own, LANES), F32)
+            for u in range(LANES // HEAD):
+                h = t * (LANES // HEAD) + u
+                mask = head_mask(u, BF16)
+                fmask = head_mask(u, F32)
+                band = slice(u * HEAD, (u + 1) * HEAD)
+                s = nt(cat(left6([a * mask for a in qp]), 1), kcat) + bias[h]
+                e = jnp.exp(s - jnp.max(s, axis=1, keepdims=True))
+                p = e * (1.0 / jnp.sum(e, axis=1, keepdims=True))
+                p1, p2 = split2(p)
+                both = nn(p1, cat(vp, 1))
+                mix = mix + fmask * (both[:, :LANES] + both[:, LANES:] + nn(p2, vp[0]))
+                dp = nt(cat(left3([a * mask for a in mp]), 1), vcat)
+                ds = p * (dp - jnp.sum(p * dp, axis=1, keepdims=True))
+                dbias[h] = ds if b == 0 else dbias[h] + ds
+                s1, s2 = split2(ds)
+                both = nn(s1, cat(kp[:2], 1))
+                dq = dq + fmask * (both[:, :LANES] + both[:, LANES:] + nn(s2, kp[0]))
+                both = nn(cat([qt1[band], qt2[band]], 0), s1)
+                dkt.append(both[:HEAD] + both[HEAD:] + nn(qt1[band], s2))
+                both = nn(cat([mt1[band], mt2[band]], 0), p1)
+                dvt.append(both[:HEAD] + both[HEAD:] + nn(mt1[band], p2))
+            mix_tiles.append(mix)
+            dq_tiles.append(dq)
+        mixes.append(cat(mix_tiles, 1))
+        dqs.append(cat(dq_tiles, 1))
+        t1, t2 = split2(cat([cat(dkt, 0).T, cat(dvt, 0).T], 1))
+        b1, b2 = split2(cat([wk, wv], 1))
+        dyall[b] = nt(t1, b1) + nt(t1, b2) + nt(t2, b1)
+    o = cat(mixes, 0)
+    d_gate = d_out * o * sig * (1.0 - sig)
+    t1, t2 = split2(cat([cat(dqs, 0), d_gate], 1))
+    b1, b2 = split2(cat([wq, wg], 1))
+    dy_ref[...] = (nt(t1, b1) + nt(t1, b2) + nt(t2, b1)).reshape(n_seqs, own, feats)
+    for t, ref in enumerate((r0_ref, r1_ref, r2_ref, r3_ref)):
+        at = pl.multiple_of(lax.bitwise_xor(res, t) * own, own)
+        for b in range(n_seqs):
+            ref[b] = dyall[b, pl.ds(at, own), :]
+    for s in range(seq_n):
+        ci = lax.bitwise_xor(chip, s // 2)
+        block = cat([dbias[h, s * rows : (s + 1) * rows, :] for h in range(heads)], 0)
+
+        @pl.when(core == s % 2)
+        def _():
+            near_ref[ci] = block
+
+        @pl.when(core != s % 2)
+        def _():
+            far_ref[ci] = block
+
+
+def aligned_end_kernel(y_ref, dy_ref, r0_ref, r1_ref, r2_ref, r3_ref, out_ref):
+    n, scale = normed(y_ref[...])
+    dn = dy_ref[...] + r0_ref[...] + r1_ref[...] + r2_ref[...] + r3_ref[...]
+    out_ref[...] = normed_back(n, scale, dn)
+
+
+def pair_end_kernel(
+    rows,
+    x_ref, dn_ref, p0_ref, p1_ref, p2_ref, p3_ref, m0_ref, m1_ref, m2_ref, m3_ref,
+    g_ref, wp_ref, g2_ref, wm_ref, out_ref,
+):
+    hp, hm = wp_ref.shape[0], wm_ref.shape[0]
+    w = cat([wp_ref[...] * g_ref[...], wm_ref[...] * g2_ref[...]], 0)
+    w = cat([w, jnp.zeros((16 - hp - hm, w.shape[1]), F32)], 0)
+    wcat = cat(right3(split2(w)), 0)
+    pair = p0_ref[...] + p1_ref[...] + p2_ref[...] + p3_ref[...]
+    msa = m0_ref[...] + m1_ref[...] + m2_ref[...] + m3_ref[...]
+    for j in range(rows):
+        lines = [pair[h * rows + j : h * rows + j + 1] for h in range(hp)]
+        lines += [msa[h * rows + j : h * rows + j + 1] for h in range(hm)]
+        lines += [jnp.zeros((16 - hp - hm, pair.shape[1]), F32)]
+        b = cat(lines, 0).T
+        dn = dn_ref[j] + nn(cat(left3(split2(b)), 1), wcat)
+        n, scale = normed(x_ref[j])
+        out_ref[j] = normed_back(n, scale, dn)
+
+
+MIB = 1 << 20
+
+
+def params(mib, **more):
+    return pltpu.CompilerParams(vmem_limit_bytes=mib * MIB, **more)
+
+
+def swap(values, axis, size, offset):
+    return lax.ppermute(values, axis, [(i, i ^ offset) for i in range(size)])
+
+
+def fused_on_device(
+    seq_n,
+    res_n,
+    coupled_embedding,
+    aligned_embedding,
+    coupled_change_adjoint,
+    aligned_change_adjoint,
+    coupled_scaler,
+    coupled_asking_matrix,
+    coupled_lookup_matrix,
+    coupled_content_matrix,
+    coupled_sigmoid_matrix,
+    coupled_offset_matrix,
+    coupled_result_matrix,
+    aligned_scaler,
+    coupled_scaler_for_offset,
+    aligned_asking_matrix,
+    aligned_lookup_matrix,
+    aligned_content_matrix,
+    aligned_sigmoid_matrix,
+    aligned_offset_matrix,
+    aligned_result_matrix,
+):
+    rows, length, feats = coupled_embedding.shape
+    n_seqs, own, wide = aligned_embedding.shape
+    hp, hm = HP, ALIGNED_SPLITS
+    chips = seq_n // 2
+    shape = lambda *s: jax.ShapeDtypeStruct(s, F32)
+    wp_t, wm_t = coupled_offset_matrix.T, aligned_offset_matrix.T
+    gain = coupled_scaler.reshape(1, feats)
+    gain2 = coupled_scaler_for_offset.reshape(1, feats)
+
+    others = [swap(aligned_embedding, "res", res_n, t) for t in range(1, res_n)]
+    pair_rows, msa_rows = pl.pallas_call(
+        functools.partial(bias_kernel, rows),
+        out_shape=(shape(hp * rows, length), shape(hm * rows, length)),
+        compiler_params=params(16),
+        name="bias_rows",
+    )(coupled_embedding, gain, wp_t, gain2, wm_t)
+    column = jnp.stack([pair_rows] + [swap(pair_rows, "res", res_n, t) for t in range(1, res_n)])
+    own_pair = jnp.stack([column] + [swap(column, "seq", seq_n, 2 * t) for t in range(1, chips)])
+    own_msa = jnp.stack([msa_rows] + [swap(msa_rows, "seq", seq_n, 2 * t) for t in range(1, chips)])
+    other_pair = swap(own_pair, "seq", seq_n, 1)
+    other_msa = swap(own_msa, "seq", seq_n, 1)
+
+    msa = pl.pallas_call(
+        functools.partial(msa_kernel, (rows, hm, seq_n, res_n)),
+        out_shape=(shape(n_seqs, own, wide),) * 5 + (shape(chips, hm * rows, length),) * 2,
+        scratch_shapes=[
+            pltpu.VMEM((hm, own, length), F32),
+            pltpu.VMEM((hm, own, length), F32),
+            pltpu.VMEM((n_seqs, length, wide), F32),
+            pltpu.VMEM((n_seqs, length, wide), F32),
+        ],
+        compiler_params=params(48),
+        name="msa_attention",
+        cost_estimate=pl.CostEstimate(flops=2 * 10**9, bytes_accessed=4 * 10**6, transcendentals=0),
+    )(
+        aligned_embedding, *others, aligned_change_adjoint, own_msa, other_msa,
+        aligned_scaler.reshape(wide, 1), aligned_asking_matrix, aligned_lookup_matrix,
+        aligned_content_matrix, aligned_sigmoid_matrix, aligned_result_matrix,
+    )
+    dy, kept, sent, msa_near, msa_far = msa[0], msa[1], msa[2:5], msa[5], msa[6]
+    arrived = [swap(a, "res", res_n, t + 1) for t, a in enumerate(sent)]
+    msa_half = msa_near + swap(msa_far, "seq", seq_n, 1)
+    msa_parts = [msa_half[0]] + [swap(msa_half[t], "seq", seq_n, 2 * t) for t in range(1, chips)]
+
+    whole = lambda *s: pl.BlockSpec(s, lambda i: (0,) * len(s))
+    row = pl.BlockSpec((1, length, feats), lambda i: (i, 0, 0))
+    quarter = (chips, res_n, hp * rows, length)
+    dn, near, far = pl.pallas_call(
+        functools.partial(pair_kernel, (rows, hp, seq_n, res_n)),
+        grid=(rows,),
+        in_specs=[row, row, whole(*quarter), whole(*quarter), whole(feats, 1)]
+        + [whole(feats, feats)] * 5,
+        out_specs=(row, whole(*quarter), whole(*quarter)),
+        out_shape=(shape(rows, length, feats), shape(*quarter), shape(*quarter)),
+        scratch_shapes=[
+            pltpu.VMEM((hp, length, length), F32),
+            pltpu.VMEM((hp, length, length), F32),
+            pltpu.VMEM((6 * feats, 2 * feats), BF16),
+            pltpu.VMEM((3 * feats, 2 * feats), BF16),
+            pltpu.VMEM((feats, 3 * feats), BF16),
+            pltpu.VMEM((2, feats, 4 * feats), BF16),
+        ],
+        compiler_params=params(48),
+        name="pair_attention",
+        cost_estimate=pl.CostEstimate(flops=2 * 10**10, bytes_accessed=6 * 10**6, transcendentals=0),
+    )(
+        coupled_embedding, coupled_change_adjoint, own_pair, other_pair,
+        coupled_scaler.reshape(feats, 1), coupled_asking_matrix, coupled_lookup_matrix,
+        coupled_content_matrix, coupled_sigmoid_matrix, coupled_result_matrix,
+    )
+    half = near + swap(far, "seq", seq_n, 1)
+    column = half[0]
+    for t in range(1, chips):
+        column = column + swap(half[t], "seq", seq_n, 2 * t)
+    parts = [column[0]] + [swap(column[t], "res", res_n, t) for t in range(1, res_n)]
+
+    aligned_out = pl.pallas_call(
+        aligned_end_kernel,
+        out_shape=shape(n_seqs, own, wide),
+        compiler_params=params(16),
+        name="aligned_end",
+    )(aligned_embedding, dy, kept, *arrived)
+    coupled_out = pl.pallas_call(
+        functools.partial(pair_end_kernel, rows),
+        out_shape=shape(rows, length, feats),
+        compiler_params=params(16),
+        name="pair_end",
+    )(coupled_embedding, dn, *parts, *msa_parts, gain, wp_t, gain2, wm_t)
+    return coupled_out, aligned_out
+
+
+def on_device(seq_n, res_n, *arrays):
+    length = arrays[0].shape[1]
+    if length <= 2 * LANES and seq_n == 8 and res_n == 4:
+        return fused_on_device(seq_n, res_n, *arrays)
+    return scanned_on_device(*arrays)
+
+
 def solution(mesh):
     in_specs = (
         P(("res", "seq"), None, None),
@@ -199,5 +656,6 @@
     )
     out_specs = (P(("res", "seq"), None, None), P("seq", "res", None))
     return jax.shard_map(
-        on_device, mesh=mesh, in_specs=in_specs, out_specs=out_specs, check_vma=False
-    )
+        functools.partial(on_device, mesh.shape["seq"], mesh.shape["res"]),
+        mesh=mesh, in_specs=in_specs, out_specs=out_specs, check_vma=False
+    )

time: 321 us -> 98 us (0.31)
  matrix products: 72.6 us -> 0 us
  blocking collectives: 58.7 us -> 0 us
  waiting for transfers between devices: 74.1 us -> 17.8 us
  local copies, waits for them, and re-layouts: 54.3 us -> 2.69 us
  Pallas kernels: 0 us -> 45.3 us
  other arithmetic: 40.4 us -> 0.16 us
  starting transfers between devices: 0.43 us -> 30.8 us
  between operations: 17.7 us -> 1.02 us
    dot_general x68 -> x0, matrix products: 71.9 us -> none  [the longest x22 28.6 us: affine_map(): return jnp.einsum('...c,ce->...e', values, weight, precision=EXACT_MATMUL)]
    all_gather x4 -> x0, blocking collectives: 58.7 us -> none  [the longest x1 20 us: on_device(): full_bias = lax.all_gather(by_seq, 'res', axis=0, tiled=True)]
    unnamed x6 -> x0, waiting for transfers between devices: 54.1 us -> none
    pallas_call x0 -> x5, Pallas kernels: none -> 45.3 us  [the longest x1 26 us: fused_on_device(): pl.pallas_call(functools.partial(pair_kernel, (rows, hp, seq_n, res_n)),...]
    ppermute x0 -> x28, starting transfers between devices: none -> 30.8 us  [swap(): return lax.ppermute(values, axis, [(i, i ^ offset) for i in range(size)])]
    reduce_scatter x2 -> x0, waiting for transfers between devices: 20 us -> none  [the longest x1 15.9 us: on_device(): lax.psum_scatter(state_term, 'res', scatter_dimension=1, tiled=True)]
    ppermute x0 -> x28, waiting for transfers between devices: none -> 17.8 us  [swap(): return lax.ppermute(values, axis, [(i, i ^ offset) for i in range(size)])]
    add x8 -> x3, other arithmetic: 16.4 us -> 0.1 us  [the longest x1 0.05 us: fused_on_device(): half = near + swap(far, 'seq', seq_n, 1)]
  transfers between devices with their start and end apart: 4 -> 28, of which waited for: 3 -> 10; matrix products, arithmetic and copies ran while one was open for 13% -> 0% of each run, Pallas kernels for 0% -> 43%
where the time goes in v1:
time: 98 us; the launch traced here: 97.8 us
  Pallas kernels  45.3 us (46%)
  starting transfers between devices  30.8 us (31%)
  waiting for transfers between devices  17.8 us (18%)
  local copies, waits for them, and re-layouts  2.69 us (3%)
  between operations  1.02 us (1%)
    ppermute x28, starting transfers between devices, swap(): return lax.ppermute(values, axis, [(i, i ^ offset) for i in range(size)])  30.8 us
    pallas_call x1, Pallas kernels, fused_on_device(): pl.pallas_call(functools.partial(pair_kernel, (rows, hp, seq_n, res_n)),...  26 us
    ppermute x28, waiting for transfers between devices, swap(): return lax.ppermute(values, axis, [(i, i ^ offset) for i in range(size)])  17.8 us
    pallas_call x1, Pallas kernels, fused_on_device(): pl.pallas_call(functools.partial(msa_kernel, (rows, hm, seq_n, res_n)), o...  14.9 us
    pallas_call x1, Pallas kernels, fused_on_device(): pl.pallas_call(functools.partial(pair_end_kernel, rows), out_shape=shape(...  2.63 us
    unnamed x40, local copies, waits for them, and re-layouts  2.41 us
  transfers between devices with their start and end apart: 28, of which 10 were waited for; matrix products, arithmetic and copies ran while one was open for 0% of the time, Pallas kernels for 43%

profile of v1, /device:TPU:0, one launch (start us, length us, event | category | flops | bytes accessed | tf_op | source)
XLA Modules:
  0.0 97.8 jit_solution(15484866022903696032)
XLA Ops:
  0.7 0.6 copy-done.3
  1.3 1.1 %copy-done = f32[6,192,128]{2,1,0:T(8,128)S(1)} copy-done((f32[6,192,128]{2,1,0:T(8,128)S(1)}, f32[6,192,128]{2,1,0:T(8,128)}, u32[]{:S(2)}) %copy-start) | copy-done | bytes 589848
  2.4 0.8 bias_rows.1
  3.2 5.1 %collective-permute-start.2 = (f32[24,192]{1,0:T(8,128)S(1)}, f32[24,192]{1,0:T(8,128)S(1)}, u32[]{:S(2)}, u32[]{:S(2)}) collective-permute-start(f32[24,192]{1,0:T(8,128)S(1)} %get-tuple-element.14), channel_id=1, source_target_pairs={{0,3},{1,2},{2,1},{3,0},{4,7},{5,6},{6,5},{7,4},{8,11},{9,10},{10,... | collective-permute-start | bytes 55304 | tf_op jit(solution)/shard_map/ppermute | solution.py:511
  8.3 0.6 collective-permute-start
  9.0 1.2 %collective-permute-done.2 = f32[24,192]{1,0:T(8,128)S(1)} collective-permute-done((f32[24,192]{1,0:T(8,128)S(1)}, f32[24,192]{1,0:T(8,128)S(1)}, u32[]{:S(2)}, u32[]{:S(2)}) %collective-permute-start.2) | collective-permute-done | bytes 18464 | tf_op jit(solution)/shard_map/ppermute | solution.py:511
  10.1 2.9 %collective-permute-done.1 = f32[24,192]{1,0:T(8,128)S(1)} collective-permute-done((f32[24,192]{1,0:T(8,128)S(1)}, f32[24,192]{1,0:T(8,128)S(1)}, u32[]{:S(2)}, u32[]{:S(2)}) %collective-permute-start.1) | collective-permute-done | bytes 18464 | tf_op jit(solution)/shard_map/ppermute | solution.py:511
  13.1 2.5 %collective-permute-start.5 = (f32[4,24,192]{2,1,0:T(8,128)S(1)}, f32[4,24,192]{2,1,0:T(8,128)S(1)}, u32[]{:S(2)}, u32[]{:S(2)}) collective-permute-start(f32[4,24,192]{2,1,0:T(8,128)S(1)} %get-tuple-element.38), channel_id=1, source_target_pairs={{0,24},{4,28},{8,16},{12,20},{16,8},{20,12},{24,0},{28,4},{1,25},{... | collective-permute-start | bytes 221192 | tf_op jit(solution)/shard_map/ppermute | solution.py:511
  16.7 3.1 %collective-permute-done.5 = f32[4,24,192]{2,1,0:T(8,128)S(1)} collective-permute-done((f32[4,24,192]{2,1,0:T(8,128)S(1)}, f32[4,24,192]{2,1,0:T(8,128)S(1)}, u32[]{:S(2)}, u32[]{:S(2)}) %collective-permute-start.5) | collective-permute-done | bytes 73760 | tf_op jit(solution)/shard_map/ppermute | solution.py:511
  19.7 0.8 collective-permute-done.4
  20.9 1.6 %collective-permute-start.19 = (f32[48,192]{1,0:T(8,128)S(1)}, f32[48,192]{1,0:T(8,128)S(1)}, u32[]{:S(2)}, u32[]{:S(2)}) collective-permute-start(f32[48,192]{1,0:T(8,128)S(1)} %get-tuple-element.18), channel_id=1, source_target_pairs={{0,24},{4,28},{8,16},{12,20},{16,8},{20,12},{24,0},{28,4},{1,25},{... | collective-permute-start | bytes 110600 | tf_op jit(solution)/shard_map/ppermute | solution.py:511
  23.0 1.4 %collective-permute-start.17 = (f32[48,192]{1,0:T(8,128)S(1)}, f32[48,192]{1,0:T(8,128)S(1)}, u32[]{:S(2)}, u32[]{:S(2)}) collective-permute-start(f32[48,192]{1,0:T(8,128)S(1)} %get-tuple-element.18), channel_id=1, source_target_pairs={{0,8},{4,12},{8,0},{12,4},{16,24},{20,28},{24,16},{28,20},{1,9},{5... | collective-permute-start | bytes 110600 | tf_op jit(solution)/shard_map/ppermute | solution.py:511
  24.7 1.3 %collective-permute-done.19 = f32[48,192]{1,0:T(8,128)S(1)} collective-permute-done((f32[48,192]{1,0:T(8,128)S(1)}, f32[48,192]{1,0:T(8,128)S(1)}, u32[]{:S(2)}, u32[]{:S(2)}) %collective-permute-start.19) | collective-permute-done | bytes 36896 | tf_op jit(solution)/shard_map/ppermute | solution.py:511
  26.0 2.0 %collective-permute-start.15 = (f32[2,48,256]{2,1,0:T(8,128)S(1)}, f32[2,48,256]{2,1,0:T(8,128)S(1)}, u32[]{:S(2)}, u32[]{:S(2)}) collective-permute-start(f32[2,48,256]{2,1,0:T(8,128)S(1)} %copy-done.2), channel_id=1, source_target_pairs={{0,2},{1,3},{2,0},{3,1},{4,6},{5,7},{6,4},{7,5},{8,10},{9,11},{10,... | collective-permute-start | bytes 294920 | tf_op jit(solution)/shard_map/ppermute | solution.py:511
  28.0 1.1 %collective-permute-start.16 = (f32[2,48,256]{2,1,0:T(8,128)S(1)}, f32[2,48,256]{2,1,0:T(8,128)S(1)}, u32[]{:S(2)}, u32[]{:S(2)}) collective-permute-start(f32[2,48,256]{2,1,0:T(8,128)S(1)} %copy-done.2), channel_id=1, source_target_pairs={{0,3},{1,2},{2,1},{3,0},{4,7},{5,6},{6,5},{7,4},{8,11},{9,10},{10,... | collective-permute-start | bytes 294920 | tf_op jit(solution)/shard_map/ppermute | solution.py:511
  30.0 26.0 %pair_attention.1 = (f32[6,192,128]{2,1,0:T(8,128)S(1)}, f32[4,4,24,192]{3,2,1,0:T(8,128)S(1)}, f32[4,4,24,192]{3,2,1,0:T(8,128)S(1)}) custom-call(f32[6,192,128]{2,1,0:T(8,128)S(1)} %copy-done.1, f32[6,192,128]{2,1,0:T(8,128)S(1)} %copy-done.7, f32[4,4,24,192]{3,2,1,0:T(8,128)S(1)} %pad_maximum_fusion.own_ref, ...), custom_call_target="tpu_custom_call" | custom-call | flops 20000000000 | bytes 6000000 | tf_op jit(solution)/shard_map/pair_attention/pallas_call | solution.py:584
  56.2 14.9 %msa_attention.1 = (f32[2,48,256]{2,1,0:T(8,128)S(1)}, f32[2,48,256]{2,1,0:T(8,128)S(1)}, f32[2,48,256]{2,1,0:T(8,128)S(1)}, f32[2,48,256]{2,1,0:T(8,128)S(1)}, ...) custom-call(f32[2,48,256]{2,1,0:T(8,128)S(1)} %copy-done.2, ...), custom_call_target="tpu_custom_call" | custom-call | flops 2000000000 | bytes 4000000 | tf_op jit(solution)/shard_map/msa_attention/pallas_call | solution.py:559
  72.1 2.9 %collective-permute-start.26 = (f32[2,48,256]{2,1,0:T(8,128)S(1)}, f32[2,48,256]{2,1,0:T(8,128)S(1)}, u32[]{:S(2)}, u32[]{:S(2)}) collective-permute-start(f32[2,48,256]{2,1,0:T(8,128)S(1)} %get-tuple-element.24), channel_id=1, source_target_pairs={{0,2},{1,3},{2,0},{3,1},{4,6},{5,7},{6,4},{7,5},{8,10},{9,11},{10,... | collective-permute-start | bytes 294920 | tf_op jit(solution)/shard_map/ppermute | solution.py:511
  75.1 1.6 %collective-permute-start.10 = (f32[4,24,192]{2,1,0:T(8,128)S(1)}, f32[4,24,192]{2,1,0:T(8,128)S(1)}, u32[]{:S(2)}, u32[]{:S(2)}) collective-permute-start(f32[4,24,192]{2,1,0:T(8,128)S(1)} %get-tuple-element.27), channel_id=1, source_target_pairs={{0,24},{4,28},{8,16},{12,20},{16,8},{20,12},{24,0},{28,4},{1,25},{... | collective-permute-start | bytes 221192 | tf_op jit(solution)/shard_map/ppermute | solution.py:511
  77.2 1.5 %collective-permute-start.8 = (f32[4,24,192]{2,1,0:T(8,128)S(1)}, f32[4,24,192]{2,1,0:T(8,128)S(1)}, u32[]{:S(2)}, u32[]{:S(2)}) collective-permute-start(f32[4,24,192]{2,1,0:T(8,128)S(1)} %get-tuple-element.26), channel_id=1, source_target_pairs={{0,8},{4,12},{8,0},{12,4},{16,24},{20,28},{24,16},{28,20},{1,9},{5... | collective-permute-start | bytes 221192 | tf_op jit(solution)/shard_map/ppermute | solution.py:511
  78.6 2.8 %collective-permute-done.10 = f32[4,24,192]{2,1,0:T(8,128)S(1)} collective-permute-done((f32[4,24,192]{2,1,0:T(8,128)S(1)}, f32[4,24,192]{2,1,0:T(8,128)S(1)}, u32[]{:S(2)}, u32[]{:S(2)}) %collective-permute-start.10) | collective-permute-done | bytes 73760 | tf_op jit(solution)/shard_map/ppermute | solution.py:511
  81.5 1.0 %collective-permute-start.27 = (f32[2,48,256]{2,1,0:T(8,128)S(1)}, f32[2,48,256]{2,1,0:T(8,128)S(1)}, u32[]{:S(2)}, u32[]{:S(2)}) collective-permute-start(f32[2,48,256]{2,1,0:T(8,128)S(1)} %get-tuple-element.25), channel_id=1, source_target_pairs={{0,3},{1,2},{2,1},{3,0},{4,7},{5,6},{6,5},{7,4},{8,11},{9,10},{10,... | collective-permute-start | bytes 294920 | tf_op jit(solution)/shard_map/ppermute | solution.py:511
  82.5 0.8 collective-permute-start.22
  83.3 1.3 %collective-permute-start.23 = (f32[48,192]{1,0:T(8,128)S(1)}, f32[48,192]{1,0:T(8,128)S(1)}, u32[]{:S(2)}, u32[]{:S(2)}) collective-permute-start(f32[48,192]{1,0:T(8,128)S(1)} %get-tuple-element.30), channel_id=1, source_target_pairs={{0,16},{4,20},{8,24},{12,28},{16,0},{20,4},{24,8},{28,12},{1,17},{... | collective-permute-start | bytes 110600 | tf_op jit(solution)/shard_map/ppermute | solution.py:511
  84.6 1.5 %collective-permute-start.24 = (f32[48,192]{1,0:T(8,128)S(1)}, f32[48,192]{1,0:T(8,128)S(1)}, u32[]{:S(2)}, u32[]{:S(2)}) collective-permute-start(f32[48,192]{1,0:T(8,128)S(1)} %get-tuple-element.29), channel_id=1, source_target_pairs={{0,24},{4,28},{8,16},{12,20},{16,8},{20,12},{24,0},{28,4},{1,25},{... | collective-permute-start | bytes 110600 | tf_op jit(solution)/shard_map/ppermute | solution.py:511
  86.4 1.8 %collective-permute-done.27.r3_ref = f32[2,48,256]{2,1,0:T(8,128)S(1)} collective-permute-done((f32[2,48,256]{2,1,0:T(8,128)S(1)}, f32[2,48,256]{2,1,0:T(8,128)S(1)}, u32[]{:S(2)}, u32[]{:S(2)}) %collective-permute-start.27) | collective-permute-done | bytes 98336 | tf_op jit(solution)/shard_map/ppermute | solution.py:511
  88.2 1.4 %collective-permute-start.12 = (f32[24,192]{1,0:T(8,128)S(1)}, f32[24,192]{1,0:T(8,128)S(1)}, u32[]{:S(2)}, u32[]{:S(2)}) collective-permute-start(f32[24,192]{1,0:T(8,128)S(1)} %get-tuple-element.34), channel_id=1, source_target_pairs={{0,2},{1,3},{2,0},{3,1},{4,6},{5,7},{6,4},{7,5},{8,10},{9,11},{10,... | collective-permute-start | bytes 55304 | tf_op jit(solution)/shard_map/ppermute | solution.py:511
  89.6 1.0 %collective-permute-start.13 = (f32[24,192]{1,0:T(8,128)S(1)}, f32[24,192]{1,0:T(8,128)S(1)}, u32[]{:S(2)}, u32[]{:S(2)}) collective-permute-start(f32[24,192]{1,0:T(8,128)S(1)} %get-tuple-element.33), channel_id=1, source_target_pairs={{0,3},{1,2},{2,1},{3,0},{4,7},{5,6},{6,5},{7,4},{8,11},{9,10},{10,... | collective-permute-start | bytes 55304 | tf_op jit(solution)/shard_map/ppermute | solution.py:511
  90.5 0.9 aligned_end.1
  91.5 1.4 %collective-permute-done.12.p2_ref = f32[24,192]{1,0:T(8,128)S(1)} collective-permute-done((f32[24,192]{1,0:T(8,128)S(1)}, f32[24,192]{1,0:T(8,128)S(1)}, u32[]{:S(2)}, u32[]{:S(2)}) %collective-permute-start.12) | collective-permute-done | bytes 18464 | tf_op jit(solution)/shard_map/ppermute | solution.py:511
  92.9 2.3 %collective-permute-done.13.p3_ref = f32[24,192]{1,0:T(8,128)S(1)} collective-permute-done((f32[24,192]{1,0:T(8,128)S(1)}, f32[24,192]{1,0:T(8,128)S(1)}, u32[]{:S(2)}, u32[]{:S(2)}) %collective-permute-start.13) | collective-permute-done | bytes 18464 | tf_op jit(solution)/shard_map/ppermute | solution.py:511
  95.2 2.6 %pair_end.1 = f32[6,192,128]{2,1,0:T(8,128)} custom-call(f32[6,192,128]{2,1,0:T(8,128)S(1)} %copy-done.1, f32[6,192,128]{2,1,0:T(8,128)S(1)} %get-tuple-element.15.dn_ref, f32[24,192]{1,0:T(8,128)S(1)} %get-tuple-element.36.p0_ref, f32[24,192]{1,0:T(8,128)S(1)} %collective-permute-done.11.p1_ref, f32[24,192]{1,0:T(8,128)S(1)} %collective-permute-done.12.p2_ref, ...), custom_call_target="tpu_custom_call" | custom-call | tf_op jit(solution)/shard_map/pair_end/pallas_call | solution.py:619
  (80 shorter events, 5.0 us)
Async XLA Ops:
  3.2 6.9 %collective-permute-start.2 = (f32[24,192]{1,0:T(8,128)S(1)}, f32[24,192]{1,0:T(8,128)S(1)}, u32[]{:S(2)}, u32[]{:S(2)}) collective-permute-start(f32[24,192]{1,0:T(8,128)S(1)} %get-tuple-element.14), channel_id=1, source_target_pairs={{0,3},{1,2},{2,1},{3,0},{4,7},{5,6},{6,5},{7,4},{8,11},{9,10},{10,... | collective-permute-start | bytes 55304 | tf_op jit(solution)/shard_map/ppermute | solution.py:511
  8.3 4.7 %collective-permute-start.1 = (f32[24,192]{1,0:T(8,128)S(1)}, f32[24,192]{1,0:T(8,128)S(1)}, u32[]{:S(2)}, u32[]{:S(2)}) collective-permute-start(f32[24,192]{1,0:T(8,128)S(1)} %get-tuple-element.14), channel_id=1, source_target_pairs={{0,2},{1,3},{2,0},{3,1},{4,6},{5,7},{6,4},{7,5},{8,10},{9,11},{10,... | collective-permute-start | bytes 55304 | tf_op jit(solution)/shard_map/ppermute | solution.py:511
  8.3 4.7 %collective-permute-start = (f32[24,192]{1,0:T(8,128)S(1)}, f32[24,192]{1,0:T(8,128)S(1)}, u32[]{:S(2)}, u32[]{:S(2)}) collective-permute-start(f32[24,192]{1,0:T(8,128)S(1)} %get-tuple-element.14), channel_id=1, source_target_pairs={{0,1},{1,0},{2,3},{3,2},{4,5},{5,4},{6,7},{7,6},{8,9},{9,8},{10,11... | collective-permute-start | bytes 55304 | tf_op jit(solution)/shard_map/ppermute | solution.py:511
  13.1 6.6 %collective-permute-start.5 = (f32[4,24,192]{2,1,0:T(8,128)S(1)}, f32[4,24,192]{2,1,0:T(8,128)S(1)}, u32[]{:S(2)}, u32[]{:S(2)}) collective-permute-start(f32[4,24,192]{2,1,0:T(8,128)S(1)} %get-tuple-element.38), channel_id=1, source_target_pairs={{0,24},{4,28},{8,16},{12,20},{16,8},{20,12},{24,0},{28,4},{1,25},{... | collective-permute-start | bytes 221192 | tf_op jit(solution)/shard_map/ppermute | solution.py:511
  15.6 4.9 %collective-permute-start.4 = (f32[4,24,192]{2,1,0:T(8,128)S(1)}, f32[4,24,192]{2,1,0:T(8,128)S(1)}, u32[]{:S(2)}, u32[]{:S(2)}) collective-permute-start(f32[4,24,192]{2,1,0:T(8,128)S(1)} %get-tuple-element.38), channel_id=1, source_target_pairs={{0,16},{4,20},{8,24},{12,28},{16,0},{20,4},{24,8},{28,12},{1,17},{... | collective-permute-start | bytes 221192 | tf_op jit(solution)/shard_map/ppermute | solution.py:511
  16.1 4.6 %collective-permute-start.3 = (f32[4,24,192]{2,1,0:T(8,128)S(1)}, f32[4,24,192]{2,1,0:T(8,128)S(1)}, u32[]{:S(2)}, u32[]{:S(2)}) collective-permute-start(f32[4,24,192]{2,1,0:T(8,128)S(1)} %get-tuple-element.38), channel_id=1, source_target_pairs={{0,8},{4,12},{8,0},{12,4},{16,24},{20,28},{24,16},{28,20},{1,9},{5... | collective-permute-start | bytes 221192 | tf_op jit(solution)/shard_map/ppermute | solution.py:511
  20.8 8.5 %collective-permute-start.6 = (f32[4,4,24,192]{3,2,1,0:T(8,128)S(1)}, f32[4,4,24,192]{3,2,1,0:T(8,128)S(1)}, u32[]{:S(2)}, u32[]{:S(2)}) collective-permute-start(f32[4,4,24,192]{3,2,1,0:T(8,128)S(1)} %pad_maximum_fusion.own_ref), channel_id=1, source_target_pairs={{0,4},{4,0},{8,12},{12,8},{16,20},{20,16},{24,28},{28,24},{1,5},{5... | collective-permute-start | bytes 884744 | tf_op jit(solution)/shard_map/ppermute | solution.py:511
  20.9 5.1 %collective-permute-start.19 = (f32[48,192]{1,0:T(8,128)S(1)}, f32[48,192]{1,0:T(8,128)S(1)}, u32[]{:S(2)}, u32[]{:S(2)}) collective-permute-start(f32[48,192]{1,0:T(8,128)S(1)} %get-tuple-element.18), channel_id=1, source_target_pairs={{0,24},{4,28},{8,16},{12,20},{16,8},{20,12},{24,0},{28,4},{1,25},{... | collective-permute-start | bytes 110600 | tf_op jit(solution)/shard_map/ppermute | solution.py:511
  22.4 5.6 %collective-permute-start.18 = (f32[48,192]{1,0:T(8,128)S(1)}, f32[48,192]{1,0:T(8,128)S(1)}, u32[]{:S(2)}, u32[]{:S(2)}) collective-permute-start(f32[48,192]{1,0:T(8,128)S(1)} %get-tuple-element.18), channel_id=1, source_target_pairs={{0,16},{4,20},{8,24},{12,28},{16,0},{20,4},{24,8},{28,12},{1,17},{... | collective-permute-start | bytes 110600 | tf_op jit(solution)/shard_map/ppermute | solution.py:511
  23.0 6.2 %collective-permute-start.17 = (f32[48,192]{1,0:T(8,128)S(1)}, f32[48,192]{1,0:T(8,128)S(1)}, u32[]{:S(2)}, u32[]{:S(2)}) collective-permute-start(f32[48,192]{1,0:T(8,128)S(1)} %get-tuple-element.18), channel_id=1, source_target_pairs={{0,8},{4,12},{8,0},{12,4},{16,24},{20,28},{24,16},{28,20},{1,9},{5... | collective-permute-start | bytes 110600 | tf_op jit(solution)/shard_map/ppermute | solution.py:511
  24.4 31.7 %collective-permute-start.14 = (f32[2,48,256]{2,1,0:T(8,128)S(1)}, f32[2,48,256]{2,1,0:T(8,128)S(1)}, u32[]{:S(2)}, u32[]{:S(2)}) collective-permute-start(f32[2,48,256]{2,1,0:T(8,128)S(1)} %copy-done.2), channel_id=1, source_target_pairs={{0,1},{1,0},{2,3},{3,2},{4,5},{5,4},{6,7},{7,6},{8,9},{9,8},{10,11... | collective-permute-start | bytes 294920 | tf_op jit(solution)/shard_map/ppermute | solution.py:511
  26.0 30.1 %collective-permute-start.15 = (f32[2,48,256]{2,1,0:T(8,128)S(1)}, f32[2,48,256]{2,1,0:T(8,128)S(1)}, u32[]{:S(2)}, u32[]{:S(2)}) collective-permute-start(f32[2,48,256]{2,1,0:T(8,128)S(1)} %copy-done.2), channel_id=1, source_target_pairs={{0,2},{1,3},{2,0},{3,1},{4,6},{5,7},{6,4},{7,5},{8,10},{9,11},{10,... | collective-permute-start | bytes 294920 | tf_op jit(solution)/shard_map/ppermute | solution.py:511
  28.0 28.1 %collective-permute-start.16 = (f32[2,48,256]{2,1,0:T(8,128)S(1)}, f32[2,48,256]{2,1,0:T(8,128)S(1)}, u32[]{:S(2)}, u32[]{:S(2)}) collective-permute-start(f32[2,48,256]{2,1,0:T(8,128)S(1)} %copy-done.2), channel_id=1, source_target_pairs={{0,3},{1,2},{2,1},{3,0},{4,7},{5,6},{6,5},{7,4},{8,11},{9,10},{10,... | collective-permute-start | bytes 294920 | tf_op jit(solution)/shard_map/ppermute | solution.py:511
  29.2 27.0 %copy-start.8 = (f32[256,256]{1,0:T(8,128)S(1)}, f32[256,256]{1,0:T(8,128)}, u32[]{:S(2)}) copy-start(f32[256,256]{1,0:T(8,128)} %wq_ref.3) | copy-start | bytes 786436
  29.2 27.0 %copy-start.9 = (f32[256,256]{1,0:T(8,128)S(1)}, f32[256,256]{1,0:T(8,128)}, u32[]{:S(2)}) copy-start(f32[256,256]{1,0:T(8,128)} %wk_ref.3) | copy-start | bytes 786436
  29.2 27.0 %copy-start.10 = (f32[256,256]{1,0:T(8,128)S(1)}, f32[256,256]{1,0:T(8,128)}, u32[]{:S(2)}) copy-start(f32[256,256]{1,0:T(8,128)} %wv_ref.3) | copy-start | bytes 786436
  29.2 27.0 %copy-start.11 = (f32[256,256]{1,0:T(8,128)S(1)}, f32[256,256]{1,0:T(8,128)}, u32[]{:S(2)}) copy-start(f32[256,256]{1,0:T(8,128)} %wg_ref.3) | copy-start | bytes 786436
  29.2 26.9 %collective-permute-start.20 = (f32[4,48,192]{2,1,0:T(8,128)S(1)}, f32[4,48,192]{2,1,0:T(8,128)S(1)}, u32[]{:S(2)}, u32[]{:S(2)}) collective-permute-start(f32[4,48,192]{2,1,0:T(8,128)S(1)} %pad_maximum_fusion.1.own_ref), channel_id=1, source_target_pairs={{0,4},{4,0},{8,12},{12,8},{16,20},{20,16},{24,28},{28,24},{1,5},{5... | collective-permute-start | bytes 442376 | tf_op jit(solution)/shard_map/ppermute | solution.py:511
  56.0 19.0 %collective-permute-start.7 = (f32[4,4,24,192]{3,2,1,0:T(8,128)S(1)}, f32[4,4,24,192]{3,2,1,0:T(8,128)S(1)}, u32[]{:S(2)}, u32[]{:S(2)}) collective-permute-start(f32[4,4,24,192]{3,2,1,0:T(8,128)S(1)} %get-tuple-element.17), channel_id=1, source_target_pairs={{0,4},{4,0},{8,12},{12,8},{16,20},{20,16},{24,28},{28,24},{1,5},{5... | collective-permute-start | bytes 884744 | tf_op jit(solution)/shard_map/ppermute | solution.py:511
  71.1 3.8 %collective-permute-start.21 = (f32[4,48,192]{2,1,0:T(8,128)S(1)}, f32[4,48,192]{2,1,0:T(8,128)S(1)}, u32[]{:S(2)}, u32[]{:S(2)}) collective-permute-start(f32[4,48,192]{2,1,0:T(8,128)S(1)} %get-tuple-element.20), channel_id=1, source_target_pairs={{0,4},{4,0},{8,12},{12,8},{16,20},{20,16},{24,28},{28,24},{1,5},{5... | collective-permute-start | bytes 442376 | tf_op jit(solution)/shard_map/ppermute | solution.py:511
  71.7 12.9 %collective-permute-start.25 = (f32[2,48,256]{2,1,0:T(8,128)S(1)}, f32[2,48,256]{2,1,0:T(8,128)S(1)}, u32[]{:S(2)}, u32[]{:S(2)}) collective-permute-start(f32[2,48,256]{2,1,0:T(8,128)S(1)} %get-tuple-element.23), channel_id=1, source_target_pairs={{0,1},{1,0},{2,3},{3,2},{4,5},{5,4},{6,7},{7,6},{8,9},{9,8},{10,11... | collective-permute-start | bytes 294920 | tf_op jit(solution)/shard_map/ppermute | solution.py:511
  72.1 14.0 %collective-permute-start.26 = (f32[2,48,256]{2,1,0:T(8,128)S(1)}, f32[2,48,256]{2,1,0:T(8,128)S(1)}, u32[]{:S(2)}, u32[]{:S(2)}) collective-permute-start(f32[2,48,256]{2,1,0:T(8,128)S(1)} %get-tuple-element.24), channel_id=1, source_target_pairs={{0,2},{1,3},{2,0},{3,1},{4,6},{5,7},{6,4},{7,5},{8,10},{9,11},{10,... | collective-permute-start | bytes 294920 | tf_op jit(solution)/shard_map/ppermute | solution.py:511
  75.1 6.4 %collective-permute-start.10 = (f32[4,24,192]{2,1,0:T(8,128)S(1)}, f32[4,24,192]{2,1,0:T(8,128)S(1)}, u32[]{:S(2)}, u32[]{:S(2)}) collective-permute-start(f32[4,24,192]{2,1,0:T(8,128)S(1)} %get-tuple-element.27), channel_id=1, source_target_pairs={{0,24},{4,28},{8,16},{12,20},{16,8},{20,12},{24,0},{28,4},{1,25},{... | collective-permute-start | bytes 221192 | tf_op jit(solution)/shard_map/ppermute | solution.py:511
  76.6 5.8 %collective-permute-start.9 = (f32[4,24,192]{2,1,0:T(8,128)S(1)}, f32[4,24,192]{2,1,0:T(8,128)S(1)}, u32[]{:S(2)}, u32[]{:S(2)}) collective-permute-start(f32[4,24,192]{2,1,0:T(8,128)S(1)} %get-tuple-element.28), channel_id=1, source_target_pairs={{0,16},{4,20},{8,24},{12,28},{16,0},{20,4},{24,8},{28,12},{1,17},{... | collective-permute-start | bytes 221192 | tf_op jit(solution)/shard_map/ppermute | solution.py:511
  77.2 6.1 %collective-permute-start.8 = (f32[4,24,192]{2,1,0:T(8,128)S(1)}, f32[4,24,192]{2,1,0:T(8,128)S(1)}, u32[]{:S(2)}, u32[]{:S(2)}) collective-permute-start(f32[4,24,192]{2,1,0:T(8,128)S(1)} %get-tuple-element.26), channel_id=1, source_target_pairs={{0,8},{4,12},{8,0},{12,4},{16,24},{20,28},{24,16},{28,20},{1,9},{5... | collective-permute-start | bytes 221192 | tf_op jit(solution)/shard_map/ppermute | solution.py:511
  81.5 6.7 %collective-permute-start.27 = (f32[2,48,256]{2,1,0:T(8,128)S(1)}, f32[2,48,256]{2,1,0:T(8,128)S(1)}, u32[]{:S(2)}, u32[]{:S(2)}) collective-permute-start(f32[2,48,256]{2,1,0:T(8,128)S(1)} %get-tuple-element.25), channel_id=1, source_target_pairs={{0,3},{1,2},{2,1},{3,0},{4,7},{5,6},{6,5},{7,4},{8,11},{9,10},{10,... | collective-permute-start | bytes 294920 | tf_op jit(solution)/shard_map/ppermute | solution.py:511
  82.5 7.1 %collective-permute-start.22 = (f32[48,192]{1,0:T(8,128)S(1)}, f32[48,192]{1,0:T(8,128)S(1)}, u32[]{:S(2)}, u32[]{:S(2)}) collective-permute-start(f32[48,192]{1,0:T(8,128)S(1)} %get-tuple-element.31), channel_id=1, source_target_pairs={{0,8},{4,12},{8,0},{12,4},{16,24},{20,28},{24,16},{28,20},{1,9},{5... | collective-permute-start | bytes 110600 | tf_op jit(solution)/shard_map/ppermute | solution.py:511
  83.3 8.2 %collective-permute-start.23 = (f32[48,192]{1,0:T(8,128)S(1)}, f32[48,192]{1,0:T(8,128)S(1)}, u32[]{:S(2)}, u32[]{:S(2)}) collective-permute-start(f32[48,192]{1,0:T(8,128)S(1)} %get-tuple-element.30), channel_id=1, source_target_pairs={{0,16},{4,20},{8,24},{12,28},{16,0},{20,4},{24,8},{28,12},{1,17},{... | collective-permute-start | bytes 110600 | tf_op jit(solution)/shard_map/ppermute | solution.py:511
  84.6 6.9 %collective-permute-start.24 = (f32[48,192]{1,0:T(8,128)S(1)}, f32[48,192]{1,0:T(8,128)S(1)}, u32[]{:S(2)}, u32[]{:S(2)}) collective-permute-start(f32[48,192]{1,0:T(8,128)S(1)} %get-tuple-element.29), channel_id=1, source_target_pairs={{0,24},{4,28},{8,16},{12,20},{16,8},{20,12},{24,0},{28,4},{1,25},{... | collective-permute-start | bytes 110600 | tf_op jit(solution)/shard_map/ppermute | solution.py:511
  86.1 5.4 %collective-permute-start.11 = (f32[24,192]{1,0:T(8,128)S(1)}, f32[24,192]{1,0:T(8,128)S(1)}, u32[]{:S(2)}, u32[]{:S(2)}) collective-permute-start(f32[24,192]{1,0:T(8,128)S(1)} %get-tuple-element.35), channel_id=1, source_target_pairs={{0,1},{1,0},{2,3},{3,2},{4,5},{5,4},{6,7},{7,6},{8,9},{9,8},{10,11... | collective-permute-start | bytes 55304 | tf_op jit(solution)/shard_map/ppermute | solution.py:511
  88.2 4.7 %collective-permute-start.12 = (f32[24,192]{1,0:T(8,128)S(1)}, f32[24,192]{1,0:T(8,128)S(1)}, u32[]{:S(2)}, u32[]{:S(2)}) collective-permute-start(f32[24,192]{1,0:T(8,128)S(1)} %get-tuple-element.34), channel_id=1, source_target_pairs={{0,2},{1,3},{2,0},{3,1},{4,6},{5,7},{6,4},{7,5},{8,10},{9,11},{10,... | collective-permute-start | bytes 55304 | tf_op jit(solution)/shard_map/ppermute | solution.py:511
  89.6 5.6 %collective-permute-start.13 = (f32[24,192]{1,0:T(8,128)S(1)}, f32[24,192]{1,0:T(8,128)S(1)}, u32[]{:S(2)}, u32[]{:S(2)}) collective-permute-start(f32[24,192]{1,0:T(8,128)S(1)} %get-tuple-element.33), channel_id=1, source_target_pairs={{0,3},{1,2},{2,1},{3,0},{4,7},{5,6},{6,5},{7,4},{8,11},{9,10},{10,... | collective-permute-start | bytes 55304 | tf_op jit(solution)/shard_map/ppermute | solution.py:511
  (16 other events, 156.2 us)

commit v2 on v0

--- a/solution.py
+++ b/solution.py
@@ -1,8 +1,11 @@
+import functools
 import math
 
 import jax
 import jax.numpy as jnp
 from jax import lax
+from jax.experimental import pallas as pl
+from jax.experimental.pallas import tpu as pltpu
 from jax.sharding import PartitionSpec as P
 
 HP = 4
@@ -43,7 +46,7 @@
     return mixed_contents.reshape(query_shape) * jax.nn.sigmoid(gate_preact)
 
 
-def on_device(
+def scanned_on_device(
     coupled_embedding,
     aligned_embedding,
     coupled_change_adjoint,
@@ -175,6 +178,633 @@
     )
 
 
+F32 = jnp.float32
+BF16 = jnp.bfloat16
+HEAD = 32
+LANES = 128
+TILE = 256
+
+
+def split2(a):
+    top = a.astype(BF16)
+    return top, (a - top.astype(F32)).astype(BF16)
+
+
+def split3(a):
+    top = a.astype(BF16)
+    rest = a - top.astype(F32)
+    mid = rest.astype(BF16)
+    return top, mid, (rest - mid.astype(F32)).astype(BF16)
+
+
+def left6(parts):
+    a, b, c = parts
+    return [a, a, b, b, a, c]
+
+
+def right6(parts):
+    a, b, c = parts
+    return [a, b, a, b, c, a]
+
+
+def left3(parts):
+    return [parts[0], parts[0], parts[1]]
+
+
+def right3(parts):
+    return [parts[0], parts[1], parts[0]]
+
+
+def nn(a, b):
+    return lax.dot_general(a, b, (((1,), (0,)), ((), ())), preferred_element_type=F32)
+
+
+def nt(a, b):
+    return lax.dot_general(a, b, (((1,), (1,)), ((), ())), preferred_element_type=F32)
+
+
+def cat(parts, axis):
+    return jnp.concatenate(parts, axis=axis)
+
+
+def normed(v):
+    center = v - jnp.mean(v, axis=-1, keepdims=True)
+    spread = jnp.mean(center * center, axis=-1, keepdims=True)
+    scale = lax.rsqrt(spread + EPSILON)
+    return center * scale, scale
+
+
+def normed_back(n, scale, dn):
+    return scale * (
+        dn - jnp.mean(dn, axis=-1, keepdims=True) - n * jnp.mean(dn * n, axis=-1, keepdims=True)
+    )
+
+
+def head_mask(h, dtype):
+    lane = lax.broadcasted_iota(jnp.int32, (1, LANES), 1)
+    return jnp.where((lane // HEAD) == h, 1.0, 0.0).astype(dtype)
+
+
+def bias_kernel(rows, x_ref, g_ref, wp_ref, g2_ref, wm_ref, bp_ref, bm_ref):
+    hp, hm = wp_ref.shape[0], wm_ref.shape[0]
+    w = cat([wp_ref[...] * g_ref[...], wm_ref[...] * g2_ref[...]], 0)
+    wcat = cat(left6(split3(w)), 1)
+    for j in range(rows):
+        n, _ = normed(x_ref[j])
+        res = nt(wcat, cat(right6(split3(n)), 1))
+        for h in range(hp):
+            bp_ref[h * rows + j : h * rows + j + 1, :] = res[h : h + 1]
+        for h in range(hm):
+            bm_ref[h * rows + j : h * rows + j + 1, :] = res[hp + h : hp + h + 1]
+
+
+def pair_project_kernel(
+    x_ref, adj_ref, g_ref, wq_ref, wk_ref, wv_ref, wg_ref, wo_ref, gl_ref, wp_ref, gl2_ref, wm_ref,
+    q_ref, k_ref, v_ref, m_ref, kt_ref, vt_ref, dout_ref, sig_ref, n_ref, scale_ref, wj_ref,
+):
+    rows, length, feats = x_ref.shape
+    g = g_ref[...]
+    wq = wq_ref[...] * g * (1.0 / math.sqrt(HEAD))
+    wk = wk_ref[...] * g
+    wv = wv_ref[...] * g
+    wg = wg_ref[...] * g
+    w6 = cat(right6(split3(cat([wq, wk], 1))), 0)
+    w3 = cat(right3(split2(cat([wv, wg], 1))), 0)
+    wo3 = cat(right3(split2(wo_ref[...])), 1)
+    for i in range(rows):
+        n, scale = normed(x_ref[i])
+        n_ref[i] = n
+        scale_ref[i] = jnp.broadcast_to(scale, n.shape)
+        parts = split3(n)
+        qk = nn(cat(left6(parts), 1), w6)
+        vg = nn(cat(left3(parts), 1), w3)
+        d_out = nt(cat(left3(split2(adj_ref[i])), 1), wo3)
+        sig = jax.nn.sigmoid(vg[:, feats:])
+        dout_ref[i] = d_out
+        sig_ref[i] = sig
+        q, k, v = qk[:, :feats], qk[:, feats:], vg[:, :feats]
+        q_ref[i] = cat(split3(q), 1)
+        k_ref[i] = cat(split3(k), 1)
+        v_ref[i] = cat(split2(v), 1)
+        m_ref[i] = cat(split2(d_out * sig), 1)
+        kt_ref[i] = cat(split2(k.T), 0)
+        vt_ref[i] = cat(split2(v.T), 0)
+    hp, hm = wp_ref.shape[0], wm_ref.shape[0]
+    w = cat([wp_ref[...] * gl_ref[...], wm_ref[...] * gl2_ref[...]], 0)
+    lines = [jnp.broadcast_to(w[h : h + 1], (rows, feats)) for h in range(hp + hm)]
+    lines += [jnp.zeros((LANES - rows * (hp + hm), feats), F32)]
+    spread = cat(lines, 0)
+    at = lax.broadcasted_iota(jnp.int32, (LANES, 1), 0)
+    for j in range(rows):
+        mine = jnp.where(lax.rem(at, rows) == j, spread, 0.0)
+        wj_ref[:, j * feats : (j + 1) * feats] = cat(right3(split2(mine)), 0)
+
+
+def gather_chips(natural, refs, core, chip):
+    half = len(refs) // 2
+    for t in range(half):
+        at = lax.bitwise_xor(chip, t) * 2
+        natural[at + core] = refs[t][...]
+        natural[at + 1 - core] = refs[half + t][...]
+
+
+def pair_kernel(
+    dims,
+    q_ref, k_ref, v_ref, m_ref, kt_ref, vt_ref,
+    b0_ref, b1_ref, b2_ref, b3_ref, b4_ref, b5_ref, b6_ref, b7_ref,
+    ot_ref, dqt_ref, dk_ref, dv_ref, near_ref, far_ref,
+    bt, dbt, stack, natural,
+):
+    rows, heads, seq_n, res_n = dims
+    step = pl.program_id(0)
+    seq, res = lax.axis_index("seq"), lax.axis_index("res")
+    core, chip = lax.rem(seq, 2), lax.div(seq, 2)
+    n_keys = q_ref.shape[1]
+
+    @pl.when(step == 0)
+    def _():
+        blocks = (b0_ref, b1_ref, b2_ref, b3_ref, b4_ref, b5_ref, b6_ref, b7_ref)
+        gather_chips(natural, blocks, core, chip)
+        for z in range(res_n):
+            zi = lax.bitwise_xor(res, z)
+            for s in range(seq_n):
+                block = natural[s, zi]
+                d = z * seq_n + s
+                for h in range(heads):
+                    at = h * n_keys + d * rows
+                    stack[at : at + rows, :] = block[h * rows : (h + 1) * rows]
+        bt[...] = stack[...].T
+        dbt[...] = jnp.zeros_like(dbt)
+
+    def pieces(ref, count):
+        return [ref[0, :, t * LANES : (t + 1) * LANES] for t in range(count)]
+
+    masks = [head_mask(h, BF16) for h in range(heads)]
+    qs = [cat([a * mask for mask in masks], 0) for a in pieces(q_ref, 3)]
+    ms = [cat([a * mask for mask in masks], 0) for a in pieces(m_ref, 2)]
+    kcat = cat(left6(pieces(k_ref, 3)), 1)
+    vcat = cat(left3(pieces(v_ref, 2)), 1)
+    kt1, kt2 = kt_ref[0, :LANES], kt_ref[0, LANES:]
+    vt1, vt2 = vt_ref[0, :LANES], vt_ref[0, LANES:]
+    dk = jnp.zeros((n_keys, LANES), F32)
+    dv = jnp.zeros((n_keys, LANES), F32)
+    for c in range(heads * n_keys // TILE):
+        cols = slice(c * TILE, (c + 1) * TILE)
+        first, last = c * TILE // n_keys, ((c + 1) * TILE - 1) // n_keys
+        band = slice(first * HEAD, (last + 1) * HEAD)
+        lane = lax.broadcasted_iota(jnp.int32, (1, TILE), 1) + c * TILE
+
+        def of_heads(top, low, a1, a2):
+            both = nn(cat([top[band], low[band]], 0), a1)
+            half = both.shape[0] // 2
+            total = both[:half] + both[half:] + nn(top[band], a2)
+            picked = total[:HEAD]
+            for h in range(first + 1, last + 1):
+                rest = total[(h - first) * HEAD : (h - first + 1) * HEAD]
+                picked = jnp.where(lane >= h * n_keys, rest, picked)
+            return picked
+
+        qc = [a[cols] for a in qs]
+        mc = [a[cols] for a in ms]
+        s = nt(kcat, cat(right6(qc), 1)) + bt[:, cols]
+        dp = nt(vcat, cat(right3(mc), 1))
+        e = jnp.exp(s - jnp.max(s, axis=0, keepdims=True))
+        p = e * (1.0 / jnp.sum(e, axis=0, keepdims=True))
+        p1, p2 = split2(p)
+        ot_ref[0, :, cols] = of_heads(vt1, vt2, p1, p2)
+        ds = p * (dp - jnp.sum(p * dp, axis=0, keepdims=True))
+        dbt[:, cols] = dbt[:, cols] + ds
+        s1, s2 = split2(ds)
+        dqt_ref[0, :, cols] = of_heads(kt1, kt2, s1, s2)
+        both = nn(s1, cat(qc[:2], 1))
+        dk = dk + both[:, :LANES] + both[:, LANES:] + nn(s2, qc[0])
+        both = nn(p1, cat(mc, 1))
+        dv = dv + both[:, :LANES] + both[:, LANES:] + nn(p2, mc[0])
+    dk_ref[0] = dk
+    dv_ref[0] = dv
+
+    @pl.when(step == rows - 1)
+    def _():
+        stack[...] = dbt[...].T
+        for z in range(res_n):
+            zi = lax.bitwise_xor(res, z)
+            for s in range(seq_n):
+                ci = lax.bitwise_xor(chip, s // 2)
+                d = z * seq_n + s
+                at = [h * n_keys + d * rows for h in range(heads)]
+                block = cat([stack[a : a + rows, :] for a in at], 0)
+
+                @pl.when(core == s % 2)
+                def _():
+                    near_ref[ci, zi] = block
+
+                @pl.when(core != s % 2)
+                def _():
+                    far_ref[ci, zi] = block
+
+
+def pair_back_kernel(
+    ot_ref, dqt_ref, dk_ref, dv_ref, dout_ref, sig_ref,
+    g_ref, wq_ref, wk_ref, wv_ref, wg_ref, dn_ref,
+):
+    rows, length, feats = dk_ref.shape
+    g = g_ref[...]
+    wq = wq_ref[...] * g * (1.0 / math.sqrt(HEAD))
+    w1, w2 = split2(cat([wq, wk_ref[...] * g, wv_ref[...] * g, wg_ref[...] * g], 1))
+
+    def lines(flat):
+        heads = flat.shape[1] // length
+        return cat([flat[:, h * length : (h + 1) * length] for h in range(heads)], 0).T
+
+    for i in range(rows):
+        o, sig = lines(ot_ref[i]), sig_ref[i]
+        d_gate = dout_ref[i] * o * sig * (1.0 - sig)
+        t1, t2 = split2(cat([lines(dqt_ref[i]), dk_ref[i], dv_ref[i], d_gate], 1))
+        dn_ref[i] = nt(t1, w1) + nt(t1, w2) + nt(t2, w1)
+
+
+def msa_project_kernel(
+    y0_ref, y1_ref, y2_ref, y3_ref, adj_ref,
+    g_ref, wq_ref, wk_ref, wv_ref, wg_ref, wo_ref,
+    q_ref, m_ref, dout_ref, sig_ref, k_ref, v_ref,
+    yall,
+):
+    res = lax.axis_index("res")
+    n_seqs, own, feats = y0_ref.shape
+    n_keys = yall.shape[1]
+    g = g_ref[...]
+    for t, ref in enumerate((y0_ref, y1_ref, y2_ref, y3_ref)):
+        at = pl.multiple_of(lax.bitwise_xor(res, t) * own, own)
+        for b in range(n_seqs):
+            yall[b, pl.ds(at, own), :] = ref[b]
+    n_own, _ = normed(y0_ref[...].reshape(n_seqs * own, feats))
+    n_all, _ = normed(yall[...].reshape(n_seqs * n_keys, feats))
+    own_parts, all_parts = split3(n_own), split3(n_all)
+    wq = wq_ref[...] * g * (1.0 / math.sqrt(HEAD))
+    q = nn(cat(left6(own_parts), 1), cat(right6(split3(wq)), 0))
+    gate = nn(cat(left3(own_parts), 1), cat(right3(split2(wg_ref[...] * g)), 0))
+    k = nn(cat(left6(all_parts), 1), cat(right6(split3(wk_ref[...] * g)), 0))
+    v = nn(cat(left3(all_parts), 1), cat(right3(split2(wv_ref[...] * g)), 0))
+    adj = adj_ref[...].reshape(n_seqs * own, feats)
+    d_out = nt(cat(left3(split2(adj)), 1), cat(right3(split2(wo_ref[...])), 1))
+    sig = jax.nn.sigmoid(gate)
+    q_ref[...] = q
+    m_ref[...] = d_out * sig
+    dout_ref[...] = d_out
+    sig_ref[...] = sig
+    k_ref[...] = k
+    v_ref[...] = v
+
+
+def msa_kernel(
+    dims,
+    q_ref, m_ref, k_ref, v_ref,
+    b0_ref, b1_ref, b2_ref, b3_ref, b4_ref, b5_ref, b6_ref, b7_ref,
+    g_ref, wk_ref, wv_ref, after_ref,
+    o_ref, dq_ref, r0_ref, r1_ref, r2_ref, r3_ref, near_ref, far_ref,
+    bias, dbias, dyall, natural,
+):
+    rows, heads, seq_n, res_n = dims
+    seq, res = lax.axis_index("seq"), lax.axis_index("res")
+    core, chip = lax.rem(seq, 2), lax.div(seq, 2)
+    n_seqs, own, feats = r0_ref.shape
+    n_keys = own * res_n
+    tiles, group = feats // LANES, LANES // HEAD
+    blocks = (b0_ref, b1_ref, b2_ref, b3_ref, b4_ref, b5_ref, b6_ref, b7_ref)
+    gather_chips(natural, blocks, core, chip)
+    for s in range(seq_n):
+        block = cat([natural[s, res_n], natural[s, res_n + 1]], 0)
+        for h in range(heads):
+            at = h * own + s * rows
+            bias[at : at + rows, :] = block[h * rows : (h + 1) * rows]
+    masks = [head_mask(u, BF16) for u in range(group)]
+    fmasks = [head_mask(u, F32) for u in range(group)]
+
+    def stacked(a, by):
+        return cat([a * mask for mask in by], 0)
+
+    def own_rows(full):
+        total = fmasks[0] * full[:own]
+        for u in range(1, group):
+            total = total + fmasks[u] * full[u * own : (u + 1) * own]
+        return total
+
+    b1, b2 = split2(cat([wk_ref[...] * g_ref[...], wv_ref[...] * g_ref[...]], 1))
+    for b in range(n_seqs):
+        near = slice(b * own, (b + 1) * own)
+        wide = slice(b * n_keys, (b + 1) * n_keys)
+        dkt, dvt = [], []
+        for t in range(tiles):
+            cols = slice(t * LANES, (t + 1) * LANES)
+            lines = slice(t * group * own, (t + 1) * group * own)
+            q_t, m_t = q_ref[near, cols], m_ref[near, cols]
+            qs = [stacked(a, masks) for a in split3(q_t)]
+            ms = [stacked(a, masks) for a in split2(m_t)]
+            qt1, qt2 = split2(stacked(q_t, fmasks).T)
+            mt1, mt2 = split2(stacked(m_t, fmasks).T)
+            kp = split3(k_ref[wide, cols])
+            vp = split2(v_ref[wide, cols])
+            s = nt(cat(left6(qs), 1), cat(right6(kp), 1)) + bias[lines]
+            dp = nt(cat(left3(ms), 1), cat(right3(vp), 1))
+            e = jnp.exp(s - jnp.max(s, axis=1, keepdims=True))
+            p = e * (1.0 / jnp.sum(e, axis=1, keepdims=True))
+            p1, p2 = split2(p)
+            both = nn(p1, cat(vp, 1))
+            o_ref[near, cols] = own_rows(both[:, :LANES] + both[:, LANES:] + nn(p2, vp[0]))
+            ds = p * (dp - jnp.sum(p * dp, axis=1, keepdims=True))
+            dbias[lines] = ds if b == 0 else dbias[lines] + ds
+            s1, s2 = split2(ds)
+            both = nn(s1, cat(kp[:2], 1))
+            dq_ref[near, cols] = own_rows(both[:, :LANES] + both[:, LANES:] + nn(s2, kp[0]))
+            both = nn(cat([qt1, qt2], 0), s1)
+            dkt.append(both[:LANES] + both[LANES:] + nn(qt1, s2))
+            both = nn(cat([mt1, mt2], 0), p1)
+            dvt.append(both[:LANES] + both[LANES:] + nn(mt1, p2))
+        t1, t2 = split2(cat([a.T for a in dkt + dvt], 1))
+        dyall[b] = nt(t1, b1) + nt(t1, b2) + nt(t2, b1)
+    for t, ref in enumerate((r0_ref, r1_ref, r2_ref, r3_ref)):
+        at = pl.multiple_of(lax.bitwise_xor(res, t) * own, own)
+        for b in range(n_seqs):
+            ref[b] = dyall[b, pl.ds(at, own), :]
+    for s in range(seq_n):
+        ci = lax.bitwise_xor(chip, s // 2)
+        at = [h * own + s * rows for h in range(heads)]
+        block = cat([dbias[a : a + rows, :] for a in at], 0)
+
+        @pl.when(core == s % 2)
+        def _():
+            near_ref[ci] = block
+
+        @pl.when(core != s % 2)
+        def _():
+            far_ref[ci] = block
+
+
+def aligned_back_kernel(
+    o_ref, dq_ref, dout_ref, sig_ref, g_ref, wq_ref, wg_ref, r0_ref, dy_ref
+):
+    n_seqs, own, feats = r0_ref.shape
+    sig = sig_ref[...]
+    d_gate = dout_ref[...] * o_ref[...] * sig * (1.0 - sig)
+    t1, t2 = split2(cat([dq_ref[...], d_gate], 1))
+    wq = wq_ref[...] * g_ref[...] * (1.0 / math.sqrt(HEAD))
+    b1, b2 = split2(cat([wq, wg_ref[...] * g_ref[...]], 1))
+    dy = nt(t1, b1) + nt(t1, b2) + nt(t2, b1)
+    dy_ref[...] = dy.reshape(n_seqs, own, feats) + r0_ref[...]
+
+
+def aligned_end_kernel(y_ref, dy_ref, r1_ref, r2_ref, r3_ref, out_ref):
+    n, scale = normed(y_ref[...])
+    out_ref[...] = normed_back(n, scale, dy_ref[...] + r1_ref[...] + r2_ref[...] + r3_ref[...])
+
+
+def stack_kernel(p0_ref, p1_ref, p2_ref, p3_ref, m_ref, after_ref, out_ref):
+    lines = p0_ref.shape[0]
+    for t, ref in enumerate((p0_ref, p1_ref, p2_ref, p3_ref)):
+        out_ref[t] = ref[...]
+    out_ref[4] = m_ref[:lines]
+    out_ref[5] = m_ref[lines:]
+
+
+def core_sum_kernel(p0_ref, p1_ref, m0_ref, m1_ref, after_ref, s0_ref, s1_ref, s2_ref, s3_ref):
+    res_n, lines = p0_ref.shape[1:3]
+    for t, ref in enumerate((s0_ref, s1_ref, s2_ref, s3_ref)):
+        ref[:res_n] = p0_ref[t] + p1_ref[t]
+        ref[res_n] = m0_ref[t, :lines] + m1_ref[t, :lines]
+        ref[res_n + 1] = m0_ref[t, lines:] + m1_ref[t, lines:]
+
+
+def chip_sum_kernel(
+    s0_ref, s1_ref, s2_ref, s3_ref, after_ref, c0_ref, c1_ref, c2_ref, c3_ref, m_ref
+):
+    lines = c0_ref.shape[0]
+    for t, ref in enumerate((c0_ref, c1_ref, c2_ref, c3_ref)):
+        ref[...] = s0_ref[t] + s1_ref[t] + s2_ref[t] + s3_ref[t]
+    for t in range(2):
+        total = s0_ref[4 + t] + s1_ref[4 + t] + s2_ref[4 + t] + s3_ref[4 + t]
+        m_ref[t * lines : (t + 1) * lines] = total
+
+
+def pair_end_kernel(
+    n_ref, scale_ref, dn_ref, p0_ref, p1_ref, p2_ref, p3_ref, m_ref, wj_ref, out_ref
+):
+    rows, length, feats = n_ref.shape
+    pair = p0_ref[...] + p1_ref[...] + p2_ref[...] + p3_ref[...]
+    msa = m_ref[...]
+    pad = jnp.zeros((LANES - pair.shape[0] - msa.shape[0], length), F32)
+    b = cat([pair, msa, pad], 0).T
+    more = nn(cat(left3(split2(b)), 1), wj_ref[...])
+    for j in range(rows):
+        dn = dn_ref[j] + more[:, j * feats : (j + 1) * feats]
+        out_ref[j] = normed_back(n_ref[j], scale_ref[j], dn)
+
+
+MIB = 1 << 20
+
+
+def params(mib, **more):
+    return pltpu.CompilerParams(vmem_limit_bytes=mib * MIB, **more)
+
+
+def swap(values, axis, size, offset):
+    return lax.ppermute(values, axis, [(i, i ^ offset) for i in range(size)])
+
+
+def fused_on_device(
+    seq_n,
+    res_n,
+    coupled_embedding,
+    aligned_embedding,
+    coupled_change_adjoint,
+    aligned_change_adjoint,
+    coupled_scaler,
+    coupled_asking_matrix,
+    coupled_lookup_matrix,
+    coupled_content_matrix,
+    coupled_sigmoid_matrix,
+    coupled_offset_matrix,
+    coupled_result_matrix,
+    aligned_scaler,
+    coupled_scaler_for_offset,
+    aligned_asking_matrix,
+    aligned_lookup_matrix,
+    aligned_content_matrix,
+    aligned_sigmoid_matrix,
+    aligned_offset_matrix,
+    aligned_result_matrix,
+):
+    rows, length, feats = coupled_embedding.shape
+    n_seqs, own, wide = aligned_embedding.shape
+    hp, hm = HP, ALIGNED_SPLITS
+    chips = seq_n // 2
+    shape = lambda *s: jax.ShapeDtypeStruct(s, F32)
+    wp_t, wm_t = coupled_offset_matrix.T, aligned_offset_matrix.T
+    gain = coupled_scaler.reshape(1, feats)
+    gain2 = coupled_scaler_for_offset.reshape(1, feats)
+
+    others = [swap(aligned_embedding, "res", res_n, t) for t in range(1, res_n)]
+    pair_rows, msa_rows = pl.pallas_call(
+        functools.partial(bias_kernel, rows),
+        out_shape=(shape(hp * rows, length), shape(hm * rows, length)),
+        compiler_params=params(16),
+        name="bias_rows",
+    )(coupled_embedding, gain, wp_t, gain2, wm_t)
+    bf = lambda *s: jax.ShapeDtypeStruct(s, BF16)
+    gain_in = coupled_scaler.reshape(feats, 1)
+    q, k, v, m, kt, vt, d_out, sig, n, scale, wj = pl.pallas_call(
+        pair_project_kernel,
+        out_shape=(
+            bf(rows, length, 3 * feats), bf(rows, length, 3 * feats),
+            bf(rows, length, 2 * feats), bf(rows, length, 2 * feats),
+            bf(rows, 2 * feats, length), bf(rows, 2 * feats, length),
+        ) + (shape(rows, length, feats),) * 4 + (bf(3 * LANES, rows * feats),),
+        compiler_params=params(63),
+        name="pair_project",
+        cost_estimate=pl.CostEstimate(flops=2 * 10**9, bytes_accessed=10**7, transcendentals=0),
+    )(
+        coupled_embedding, coupled_change_adjoint, gain_in, coupled_asking_matrix,
+        coupled_lookup_matrix, coupled_content_matrix, coupled_sigmoid_matrix,
+        coupled_result_matrix, gain, wp_t, gain2, wm_t,
+    )
+
+    lines = hp * rows
+    joint = (res_n + 2, lines, length)
+    vmem = lambda count: [pl.BlockSpec(memory_space=pltpu.VMEM)] * count
+    after = [pl.BlockSpec(memory_space=pl.ANY)]
+    first = pl.pallas_call(
+        stack_kernel,
+        in_specs=vmem(5) + after,
+        out_shape=shape(*joint),
+        compiler_params=params(16),
+        name="stack_rows",
+    )(pair_rows, *[swap(pair_rows, "res", res_n, t) for t in range(1, res_n)], msa_rows, n)
+    blocks = [first] + [swap(first, "seq", seq_n, 2 * t) for t in range(1, chips)]
+    blocks = blocks + [swap(a, "seq", seq_n, 1) for a in blocks]
+
+    wide_gain = aligned_scaler.reshape(wide, 1)
+    flat = lambda count: shape(n_seqs * count, wide)
+    mq, mm, m_out, m_sig, mk, mv = pl.pallas_call(
+        msa_project_kernel,
+        out_shape=(flat(own),) * 4 + (flat(length),) * 2,
+        scratch_shapes=[pltpu.VMEM((n_seqs, length, wide), F32)],
+        compiler_params=params(63),
+        name="msa_project",
+        cost_estimate=pl.CostEstimate(flops=10**9, bytes_accessed=10**7, transcendentals=0),
+    )(
+        aligned_embedding, *others, aligned_change_adjoint, wide_gain, aligned_asking_matrix,
+        aligned_lookup_matrix, aligned_content_matrix, aligned_sigmoid_matrix,
+        aligned_result_matrix,
+    )
+
+    piece = lambda *s: pl.BlockSpec((1,) + s, lambda i: (i, 0, 0))
+    whole = lambda *s: pl.BlockSpec(s, lambda i: (0,) * len(s))
+    quarter = (chips, res_n, lines, length)
+    ot, dqt, dk, dv, near, far = pl.pallas_call(
+        functools.partial(pair_kernel, (rows, hp, seq_n, res_n)),
+        grid=(rows,),
+        in_specs=[
+            piece(length, 3 * feats), piece(length, 3 * feats),
+            piece(length, 2 * feats), piece(length, 2 * feats),
+            piece(2 * feats, length), piece(2 * feats, length),
+        ] + [whole(*joint)] * seq_n,
+        out_specs=(
+            piece(HEAD, hp * length), piece(HEAD, hp * length),
+            piece(length, feats), piece(length, feats), whole(*quarter), whole(*quarter),
+        ),
+        out_shape=(
+            shape(rows, HEAD, hp * length), shape(rows, HEAD, hp * length),
+            shape(rows, length, feats), shape(rows, length, feats),
+            shape(*quarter), shape(*quarter),
+        ),
+        scratch_shapes=[
+            pltpu.VMEM((length, hp * length), F32),
+            pltpu.VMEM((length, hp * length), F32),
+            pltpu.VMEM((hp * length, length), F32),
+            pltpu.VMEM((seq_n,) + joint, F32),
+        ],
+        compiler_params=params(48),
+        name="pair_attention",
+        cost_estimate=pl.CostEstimate(flops=10**10, bytes_accessed=10**7, transcendentals=0),
+    )(q, k, v, m, kt, vt, *blocks)
+    far_pair = swap(far, "seq", seq_n, 1)
+    dn = pl.pallas_call(
+        pair_back_kernel,
+        out_shape=shape(rows, length, feats),
+        compiler_params=params(32),
+        name="pair_back",
+        cost_estimate=pl.CostEstimate(flops=10**9, bytes_accessed=10**7, transcendentals=0),
+    )(
+        ot, dqt, dk, dv, d_out, sig, gain_in, coupled_asking_matrix,
+        coupled_lookup_matrix, coupled_content_matrix, coupled_sigmoid_matrix,
+    )
+    stretch = pltpu.VMEM((hm * own, length), F32)
+    o, dq, kept, r1, r2, r3, msa_near, msa_far = pl.pallas_call(
+        functools.partial(msa_kernel, (rows, hm, seq_n, res_n)),
+        out_shape=(flat(own),) * 2 + (shape(n_seqs, own, wide),) * 4
+        + (shape(chips, hm * rows, length),) * 2,
+        in_specs=vmem(15) + after,
+        scratch_shapes=[
+            stretch, stretch, pltpu.VMEM((n_seqs, length, wide), F32),
+            pltpu.VMEM((seq_n,) + joint, F32),
+        ],
+        compiler_params=params(48),
+        name="msa_attention",
+        cost_estimate=pl.CostEstimate(flops=4 * 10**9, bytes_accessed=10**7, transcendentals=0),
+    )(
+        mq, mm, mk, mv, *blocks, wide_gain,
+        aligned_lookup_matrix, aligned_content_matrix, near,
+    )
+    far_msa = swap(msa_far, "seq", seq_n, 1)
+    arrived = [swap(a, "res", res_n, t + 1) for t, a in enumerate((r1, r2, r3))]
+    sums = pl.pallas_call(
+        core_sum_kernel,
+        in_specs=vmem(4) + after,
+        out_shape=(shape(*joint),) * chips,
+        compiler_params=params(16),
+        name="core_sum",
+    )(near, far_pair, msa_near, far_msa, dn)
+    dy = pl.pallas_call(
+        aligned_back_kernel,
+        out_shape=shape(n_seqs, own, wide),
+        compiler_params=params(16),
+        name="aligned_back",
+        cost_estimate=pl.CostEstimate(flops=10**9, bytes_accessed=10**6, transcendentals=0),
+    )(o, dq, m_out, m_sig, wide_gain, aligned_asking_matrix, aligned_sigmoid_matrix, kept)
+    *column, msa_sum = pl.pallas_call(
+        chip_sum_kernel,
+        in_specs=vmem(4) + after,
+        out_shape=(shape(lines, length),) * res_n + (shape(hm * rows, length),),
+        compiler_params=params(16),
+        name="chip_sum",
+    )(sums[0], *[swap(sums[t], "seq", seq_n, 2 * t) for t in range(1, chips)], dy)
+    parts = [column[0]] + [swap(column[t], "res", res_n, t) for t in range(1, res_n)]
+
+    aligned_out = pl.pallas_call(
+        aligned_end_kernel,
+        out_shape=shape(n_seqs, own, wide),
+        compiler_params=params(16),
+        name="aligned_end",
+    )(aligned_embedding, dy, *arrived)
+    coupled_out = pl.pallas_call(
+        pair_end_kernel,
+        out_shape=shape(rows, length, feats),
+        compiler_params=params(16),
+        name="pair_end",
+    )(n, scale, dn, *parts, msa_sum, wj)
+    return coupled_out, aligned_out
+
+
+def on_device(seq_n, res_n, *arrays):
+    length = arrays[0].shape[1]
+    rows = arrays[0].shape[0]
+    narrow = length <= 2 * LANES and HP * length % TILE == 0
+    narrow = narrow and rows * (HP + ALIGNED_SPLITS) <= LANES
+    narrow = narrow and ALIGNED_SPLITS == 2 * HP
+    if narrow and seq_n == 8 and res_n == 4:
+        return fused_on_device(seq_n, res_n, *arrays)
+    return scanned_on_device(*arrays)
+
+
 def solution(mesh):
     in_specs = (
         P(("res", "seq"), None, None),
@@ -199,5 +829,6 @@
     )
     out_specs = (P(("res", "seq"), None, None), P("seq", "res", None))
     return jax.shard_map(
-        on_device, mesh=mesh, in_specs=in_specs, out_specs=out_specs, check_vma=False
-    )
+        functools.partial(on_device, mesh.shape["seq"], mesh.shape["res"]),
+        mesh=mesh, in_specs=in_specs, out_specs=out_specs, check_vma=False
+    )

time: 321 us -> 81.3 us (0.25)
  matrix products: 72.6 us -> 0 us
  waiting for transfers between devices: 74.1 us -> 8.47 us
  blocking collectives: 58.7 us -> 0 us
  local copies, waits for them, and re-layouts: 54.3 us -> 7.21 us
  other arithmetic: 40.4 us -> 0 us
  Pallas kernels: 0 us -> 34.3 us
  starting transfers between devices: 0.43 us -> 29.8 us
  between operations: 17.7 us -> 1.06 us
    dot_general x68 -> x0, matrix products: 71.9 us -> none  [the longest x22 28.6 us: affine_map(): return jnp.einsum('...c,ce->...e', values, weight, precision=EXACT_MATMUL)]
    all_gather x4 -> x0, blocking collectives: 58.7 us -> none  [the longest x1 20 us: on_device(): full_bias = lax.all_gather(by_seq, 'res', axis=0, tiled=True)]
    unnamed x6 -> x0, waiting for transfers between devices: 54.1 us -> none
    pallas_call x0 -> x12, Pallas kernels: none -> 34.3 us  [the longest x1 14.6 us: fused_on_device(): pl.pallas_call(functools.partial(pair_kernel, (rows, hp, seq_n, res_n)),...]
    ppermute x0 -> x24, starting transfers between devices: none -> 29.8 us  [swap(): return lax.ppermute(values, axis, [(i, i ^ offset) for i in range(size)])]
    reduce_scatter x2 -> x0, waiting for transfers between devices: 20 us -> none  [the longest x1 15.9 us: on_device(): lax.psum_scatter(state_term, 'res', scatter_dimension=1, tiled=True)]
    add x8 -> x0, other arithmetic: 16.4 us -> none  [the longest x6 12.6 us: row_step(): return (bias_sum + grad_bias, (grad_query, grad_key, grad_value, grad_gate))]
    while x109 -> x0, local copies, waits for them, and re-layouts: 14.4 us -> none
  transfers between devices with their start and end apart: 4 -> 24, of which waited for: 3 -> 3; matrix products, arithmetic and copies ran while one was open for 13% -> 2% of each run, Pallas kernels for 0% -> 22%
where the time goes in v2:
time: 81.3 us; the launch traced here: 80.8 us
  Pallas kernels  34.3 us (42%)
  starting transfers between devices  29.8 us (37%)
  waiting for transfers between devices  8.47 us (10%)
  local copies, waits for them, and re-layouts  7.21 us (9%)
  between operations  1.06 us (1%)
    ppermute x24, starting transfers between devices, swap(): return lax.ppermute(values, axis, [(i, i ^ offset) for i in range(size)])  29.8 us
    pallas_call x1, Pallas kernels, fused_on_device(): pl.pallas_call(functools.partial(pair_kernel, (rows, hp, seq_n, res_n)),...  14.6 us
    ppermute x24, waiting for transfers between devices, swap(): return lax.ppermute(values, axis, [(i, i ^ offset) for i in range(size)])  8.47 us
    pallas_call x1, Pallas kernels, fused_on_device(): pl.pallas_call(pair_project_kernel, out_shape=(bf(rows, length, 3 * feats...  5.86 us
    unnamed x68, local copies, waits for them, and re-layouts  5.67 us
    pallas_call x1, Pallas kernels, fused_on_device(): pl.pallas_call(functools.partial(msa_kernel, (rows, hm, seq_n, res_n)), o...  5.24 us
    pallas_call x1, Pallas kernels, fused_on_device(): pl.pallas_call(msa_project_kernel, out_shape=(flat(own),) * 4 + (flat(len...  3.71 us
  transfers between devices with their start and end apart: 24, of which 3 were waited for; matrix products, arithmetic and copies ran while one was open for 2% of the time, Pallas kernels for 22%

profile of v2, /device:TPU:0, one launch (start us, length us, event | category | flops | bytes accessed | tf_op | source)
XLA Modules:
  0.0 80.8 jit_solution(10465608907884610291)
XLA Ops:
  0.7 0.6 copy-done.15
  1.3 1.1 %copy-done.4 = f32[6,192,128]{2,1,0:T(8,128)S(1)} copy-done((f32[6,192,128]{2,1,0:T(8,128)S(1)}, f32[6,192,128]{2,1,0:T(8,128)}, u32[]{:S(2)}) %copy-start.4) | copy-done | bytes 589848
  2.4 0.8 bias_rows.1
  3.2 3.1 %collective-permute-start = (f32[24,192]{1,0:T(8,128)S(1)}, f32[24,192]{1,0:T(8,128)S(1)}, u32[]{:S(2)}, u32[]{:S(2)}) collective-permute-start(f32[24,192]{1,0:T(8,128)S(1)} %get-tuple-element.52.p0_ref), channel_id=1, source_target_pairs={{0,1},{1,0},{2,3},{3,2},{4,5},{5,4},{6,7},{7,6},{8,9},{9,8},{10,11... | collective-permute-start | bytes 55304 | tf_op jit(solution)/shard_map/ppermute | solution.py:610
  6.3 2.6 %collective-permute-start.1 = (f32[24,192]{1,0:T(8,128)S(1)}, f32[24,192]{1,0:T(8,128)S(1)}, u32[]{:S(2)}, u32[]{:S(2)}) collective-permute-start(f32[24,192]{1,0:T(8,128)S(1)} %get-tuple-element.52.p0_ref), channel_id=1, source_target_pairs={{0,2},{1,3},{2,0},{3,1},{4,6},{5,7},{6,4},{7,5},{8,10},{9,11},{10,... | collective-permute-start | bytes 55304 | tf_op jit(solution)/shard_map/ppermute | solution.py:610
  8.9 0.9 %collective-permute-start.11 = (f32[2,48,256]{2,1,0:T(8,128)S(1)}, f32[2,48,256]{2,1,0:T(8,128)S(1)}, u32[]{:S(2)}, u32[]{:S(2)}) collective-permute-start(f32[2,48,256]{2,1,0:T(8,128)S(1)} %copy-done.9), channel_id=1, source_target_pairs={{0,1},{1,0},{2,3},{3,2},{4,5},{5,4},{6,7},{7,6},{8,9},{9,8},{10,11... | collective-permute-start | bytes 294920 | tf_op jit(solution)/shard_map/ppermute | solution.py:610
  9.8 0.7 copy.23.g_ref
  10.5 5.9 %pair_project.1 = (bf16[6,192,384]{2,1,0:T(8,128)(2,1)}, bf16[6,192,384]{2,1,0:T(8,128)(2,1)}, bf16[6,192,256]{2,1,0:T(8,128)(2,1)}, bf16[6,192,256]{2,1,0:T(8,1...) custom-call(f32[6,192,128]{2,1,0:T(8,128)} %x_ref.3, ...), custom_call_target="tpu_custom_call" | custom-call | flops 2000000000 | bytes 10000000 | tf_op jit(solution)/shard_map/pair_project/pallas_call | solution.py:654
  16.4 1.1 %copy-done = f32[6,192,128]{2,1,0:T(8,128)S(1)} copy-done((f32[6,192,128]{2,1,0:T(8,128)S(1)}, f32[6,192,128]{2,1,0:T(8,128)}, u32[]{:S(2)}) %copy-start) | copy-done | bytes 589848
  17.5 1.6 %collective-permute-start.3 = (f32[6,24,192]{2,1,0:T(8,128)S(1)}, f32[6,24,192]{2,1,0:T(8,128)S(1)}, u32[]{:S(2)}, u32[]{:S(2)}) collective-permute-start(f32[6,24,192]{2,1,0:T(8,128)S(1)} %stack_rows.1.b0_ref), channel_id=1, source_target_pairs={{0,8},{4,12},{8,0},{12,4},{16,24},{20,28},{24,16},{28,20},{1,9},{5... | collective-permute-start | bytes 331784 | tf_op jit(solution)/shard_map/ppermute | solution.py:610
  19.0 1.5 %collective-permute-start.4 = (f32[6,24,192]{2,1,0:T(8,128)S(1)}, f32[6,24,192]{2,1,0:T(8,128)S(1)}, u32[]{:S(2)}, u32[]{:S(2)}) collective-permute-start(f32[6,24,192]{2,1,0:T(8,128)S(1)} %stack_rows.1.b0_ref), channel_id=1, source_target_pairs={{0,16},{4,20},{8,24},{12,28},{16,0},{20,4},{24,8},{28,12},{1,17},{... | collective-permute-start | bytes 331784 | tf_op jit(solution)/shard_map/ppermute | solution.py:610
  21.0 3.5 %collective-permute-start.12 = (f32[2,48,256]{2,1,0:T(8,128)S(1)}, f32[2,48,256]{2,1,0:T(8,128)S(1)}, u32[]{:S(2)}, u32[]{:S(2)}) collective-permute-start(f32[2,48,256]{2,1,0:T(8,128)S(1)} %copy-done.9), channel_id=1, source_target_pairs={{0,2},{1,3},{2,0},{3,1},{4,6},{5,7},{6,4},{7,5},{8,10},{9,11},{10,... | collective-permute-start | bytes 294920 | tf_op jit(solution)/shard_map/ppermute | solution.py:610
  25.2 4.4 %collective-permute-done.12.y2_ref = f32[2,48,256]{2,1,0:T(8,128)S(1)} collective-permute-done((f32[2,48,256]{2,1,0:T(8,128)S(1)}, f32[2,48,256]{2,1,0:T(8,128)S(1)}, u32[]{:S(2)}, u32[]{:S(2)}) %collective-permute-start.12) | collective-permute-done | bytes 98336 | tf_op jit(solution)/shard_map/ppermute | solution.py:610
  30.6 0.8 copy.25.g_ref
  31.4 3.7 %msa_project.1 = (f32[96,256]{1,0:T(8,128)}, f32[96,256]{1,0:T(8,128)}, f32[96,256]{1,0:T(8,128)}, f32[96,256]{1,0:T(8,128)}, f32[384,256]{1,0:T(8,128)}, /*index=5*/f32[384,256]{1,0:T(8,128)}) custom-call(f32[2,48,256]{2,1,0:T(8,128)} %y_ref.1, f32[2,48,256]{2,1,0:T(8,128)} %copy-done.32, f32[2,48,256]{2,1,0:T(8,128)} %copy-done.33, ...), custom_call_target="tpu_custom_call" | custom-call | flops 1000000000 | bytes 10000000 | tf_op jit(solution)/shard_map/msa_project/pallas_call | solution.py:686
  35.2 1.1 %copy-done.29 = bf16[6,192,256]{2,1,0:T(8,128)(2,1)S(1)} copy-done((bf16[6,192,256]{2,1,0:T(8,128)(2,1)S(1)}, bf16[6,192,256]{2,1,0:T(8,128)(2,1)}, u32[]{:S(2)}) %copy-start.29) | copy-done | bytes 589848
  36.2 1.1 %copy-done.30 = bf16[6,192,256]{2,1,0:T(8,128)(2,1)S(1)} copy-done((bf16[6,192,256]{2,1,0:T(8,128)(2,1)S(1)}, bf16[6,192,256]{2,1,0:T(8,128)(2,1)}, u32[]{:S(2)}) %copy-start.30) | copy-done | bytes 589848
  37.3 14.6 %pair_attention.1 = (f32[6,32,768]{2,1,0:T(8,128)S(1)}, f32[6,32,768]{2,1,0:T(8,128)S(1)}, f32[6,192,128]{2,1,0:T(8,128)S(1)}, f32[6,192,128]{2,1,0:T(8,128)S(1)...) custom-call(bf16[6,192,384]{2,1,0:T(8,128)(2,1)} %get-tuple-element.46.q_ref, ...), custom_call_target="tpu_custom_call" | custom-call | flops 10000000000 | bytes 10000000 | tf_op jit(solution)/shard_map/pair_attention/pallas_call | solution.py:702
  52.2 5.2 %msa_attention.1 = (f32[96,256]{1,0:T(8,128)S(1)}, f32[96,256]{1,0:T(8,128)S(1)}, f32[2,48,256]{2,1,0:T(8,128)S(1)}, f32[2,48,256]{2,1,0:T(8,128)S(1)}, f32[2,48...) custom-call(f32[96,256]{1,0:T(8,128)S(1)} %copy-done.27, ...), custom_call_target="tpu_custom_call" | custom-call | flops 4000000000 | bytes 10000000 | tf_op jit(solution)/shard_map/msa_attention/pallas_call | solution.py:741
  58.0 1.3 %pair_back.1.after_ref.dn_ref = f32[6,192,128]{2,1,0:T(8,128)S(1)} custom-call(f32[6,32,768]{2,1,0:T(8,128)S(1)} %get-tuple-element.54.ot_ref, f32[6,32,768]{2,1,0:T(8,128)S(1)} %get-tuple-element.55.dqt_ref, f32[6,192,128]{2,1,0:T(8,128)S(1)} %get-tuple-element.56.dk_ref, f32[6,192,128]{2,1,0:T(8,128)S(1)} %get-tuple-element.57.dv_ref, ...), custom_call_target="tpu_custom_call" | custom-call | flops 1000000000 | bytes 10000000 | tf_op jit(solution)/shard_map/pair_back/pallas_call | solution.py:730
  59.4 1.6 %collective-permute-start.15 = (f32[6,24,192]{2,1,0:T(8,128)S(1)}, f32[6,24,192]{2,1,0:T(8,128)S(1)}, u32[]{:S(2)}, u32[]{:S(2)}) collective-permute-start(f32[6,24,192]{2,1,0:T(8,128)S(1)} %get-tuple-element.69), channel_id=1, source_target_pairs={{0,8},{4,12},{8,0},{12,4},{16,24},{20,28},{24,16},{28,20},{1,9},{5... | collective-permute-start | bytes 331784 | tf_op jit(solution)/shard_map/ppermute | solution.py:610
  60.9 1.5 %collective-permute-start.16 = (f32[6,24,192]{2,1,0:T(8,128)S(1)}, f32[6,24,192]{2,1,0:T(8,128)S(1)}, u32[]{:S(2)}, u32[]{:S(2)}) collective-permute-start(f32[6,24,192]{2,1,0:T(8,128)S(1)} %get-tuple-element.70), channel_id=1, source_target_pairs={{0,16},{4,20},{8,24},{12,28},{16,0},{20,4},{24,8},{28,12},{1,17},{... | collective-permute-start | bytes 331784 | tf_op jit(solution)/shard_map/ppermute | solution.py:610
  62.9 0.9 %collective-permute-start.21 = (f32[2,48,256]{2,1,0:T(8,128)S(1)}, f32[2,48,256]{2,1,0:T(8,128)S(1)}, u32[]{:S(2)}, u32[]{:S(2)}) collective-permute-start(f32[2,48,256]{2,1,0:T(8,128)S(1)} %get-tuple-element.83), channel_id=1, source_target_pairs={{0,1},{1,0},{2,3},{3,2},{4,5},{5,4},{6,7},{7,6},{8,9},{9,8},{10,11... | collective-permute-start | bytes 294920 | tf_op jit(solution)/shard_map/ppermute | solution.py:610
  63.9 3.1 %collective-permute-start.22 = (f32[2,48,256]{2,1,0:T(8,128)S(1)}, f32[2,48,256]{2,1,0:T(8,128)S(1)}, u32[]{:S(2)}, u32[]{:S(2)}) collective-permute-start(f32[2,48,256]{2,1,0:T(8,128)S(1)} %get-tuple-element.84), channel_id=1, source_target_pairs={{0,2},{1,3},{2,0},{3,1},{4,6},{5,7},{6,4},{7,5},{8,10},{9,11},{10,... | collective-permute-start | bytes 294920 | tf_op jit(solution)/shard_map/ppermute | solution.py:610
  66.9 2.5 %collective-permute-start.23 = (f32[2,48,256]{2,1,0:T(8,128)S(1)}, f32[2,48,256]{2,1,0:T(8,128)S(1)}, u32[]{:S(2)}, u32[]{:S(2)}) collective-permute-start(f32[2,48,256]{2,1,0:T(8,128)S(1)} %get-tuple-element.85), channel_id=1, source_target_pairs={{0,3},{1,2},{2,1},{3,0},{4,7},{5,6},{6,5},{7,4},{8,11},{9,10},{10,... | collective-permute-start | bytes 294920 | tf_op jit(solution)/shard_map/ppermute | solution.py:610
  70.0 0.7 collective-permute-start.18
  70.7 3.1 %collective-permute-start.19 = (f32[24,192]{1,0:T(8,128)S(1)}, f32[24,192]{1,0:T(8,128)S(1)}, u32[]{:S(2)}, u32[]{:S(2)}) collective-permute-start(f32[24,192]{1,0:T(8,128)S(1)} %get-tuple-element.79), channel_id=1, source_target_pairs={{0,2},{1,3},{2,0},{3,1},{4,6},{5,7},{6,4},{7,5},{8,10},{9,11},{10,... | collective-permute-start | bytes 55304 | tf_op jit(solution)/shard_map/ppermute | solution.py:610
  73.8 0.7 collective-permute-start.20
  74.5 0.9 %aligned_end.1 = f32[2,48,256]{2,1,0:T(8,128)} custom-call(f32[2,48,256]{2,1,0:T(8,128)S(1)} %copy-done.10, f32[2,48,256]{2,1,0:T(8,128)S(1)} %aligned_back.1.after_ref.dy_ref, f32[2,48,256]{2,1,0:T(8,128)S(1)} %collective-permute-done.21.r1_ref, f32[2,48,256]{2,1,0:T(8,128)S(1)} %collective-permute-done.22.r2_ref, ...), custom_call_target="tpu_custom_call" | custom-call | tf_op jit(solution)/shard_map/aligned_end/pallas_call | solution.py:782
  75.4 1.1 %collective-permute-done.19.p2_ref = f32[24,192]{1,0:T(8,128)S(1)} collective-permute-done((f32[24,192]{1,0:T(8,128)S(1)}, f32[24,192]{1,0:T(8,128)S(1)}, u32[]{:S(2)}, u32[]{:S(2)}) %collective-permute-start.19) | collective-permute-done | bytes 18464 | tf_op jit(solution)/shard_map/ppermute | solution.py:610
  76.5 2.9 %collective-permute-done.20.p3_ref = f32[24,192]{1,0:T(8,128)S(1)} collective-permute-done((f32[24,192]{1,0:T(8,128)S(1)}, f32[24,192]{1,0:T(8,128)S(1)}, u32[]{:S(2)}, u32[]{:S(2)}) %collective-permute-start.20) | collective-permute-done | bytes 18464 | tf_op jit(solution)/shard_map/ppermute | solution.py:610
  79.4 1.4 %pair_end.1 = f32[6,192,128]{2,1,0:T(8,128)} custom-call(f32[6,192,128]{2,1,0:T(8,128)S(1)} %copy-done.1, f32[6,192,128]{2,1,0:T(8,128)S(1)} %copy-done.5, f32[6,192,128]{2,1,0:T(8,128)S(1)} %pair_back.1.after_ref.dn_ref, f32[24,192]{1,0:T(8,128)S(1)} %get-tuple-element.77.p0_ref, f32[24,192]{1,0:T(8,128)S(1)} %collective-permute-done.18.p1_ref, ...), custom_call_target="tpu_custom_call" | custom-call | tf_op jit(solution)/shard_map/pair_end/pallas_call | solution.py:788
  (98 shorter events, 4.0 us)
Async XLA Ops:
  3.2 13.2 %collective-permute-start = (f32[24,192]{1,0:T(8,128)S(1)}, f32[24,192]{1,0:T(8,128)S(1)}, u32[]{:S(2)}, u32[]{:S(2)}) collective-permute-start(f32[24,192]{1,0:T(8,128)S(1)} %get-tuple-element.52.p0_ref), channel_id=1, source_target_pairs={{0,1},{1,0},{2,3},{3,2},{4,5},{5,4},{6,7},{7,6},{8,9},{9,8},{10,11... | collective-permute-start | bytes 55304 | tf_op jit(solution)/shard_map/ppermute | solution.py:610
  6.3 10.1 %collective-permute-start.1 = (f32[24,192]{1,0:T(8,128)S(1)}, f32[24,192]{1,0:T(8,128)S(1)}, u32[]{:S(2)}, u32[]{:S(2)}) collective-permute-start(f32[24,192]{1,0:T(8,128)S(1)} %get-tuple-element.52.p0_ref), channel_id=1, source_target_pairs={{0,2},{1,3},{2,0},{3,1},{4,6},{5,7},{6,4},{7,5},{8,10},{9,11},{10,... | collective-permute-start | bytes 55304 | tf_op jit(solution)/shard_map/ppermute | solution.py:610
  8.9 7.5 %collective-permute-start.2 = (f32[24,192]{1,0:T(8,128)S(1)}, f32[24,192]{1,0:T(8,128)S(1)}, u32[]{:S(2)}, u32[]{:S(2)}) collective-permute-start(f32[24,192]{1,0:T(8,128)S(1)} %get-tuple-element.52.p0_ref), channel_id=1, source_target_pairs={{0,3},{1,2},{2,1},{3,0},{4,7},{5,6},{6,5},{7,4},{8,11},{9,10},{10,... | collective-permute-start | bytes 55304 | tf_op jit(solution)/shard_map/ppermute | solution.py:610
  8.9 15.7 %collective-permute-start.11 = (f32[2,48,256]{2,1,0:T(8,128)S(1)}, f32[2,48,256]{2,1,0:T(8,128)S(1)}, u32[]{:S(2)}, u32[]{:S(2)}) collective-permute-start(f32[2,48,256]{2,1,0:T(8,128)S(1)} %copy-done.9), channel_id=1, source_target_pairs={{0,1},{1,0},{2,3},{3,2},{4,5},{5,4},{6,7},{7,6},{8,9},{9,8},{10,11... | collective-permute-start | bytes 294920 | tf_op jit(solution)/shard_map/ppermute | solution.py:610
  17.5 13.1 %copy-start.31 = (f32[256]{0:T(256)S(1)}, f32[256]{0:T(256)}, u32[]{:S(2)}) copy-start(f32[256]{0:T(256)} %param.30) | copy-start | bytes 3076
  17.5 12.1 %collective-permute-start.3 = (f32[6,24,192]{2,1,0:T(8,128)S(1)}, f32[6,24,192]{2,1,0:T(8,128)S(1)}, u32[]{:S(2)}, u32[]{:S(2)}) collective-permute-start(f32[6,24,192]{2,1,0:T(8,128)S(1)} %stack_rows.1.b0_ref), channel_id=1, source_target_pairs={{0,8},{4,12},{8,0},{12,4},{16,24},{20,28},{24,16},{28,20},{1,9},{5... | collective-permute-start | bytes 331784 | tf_op jit(solution)/shard_map/ppermute | solution.py:610
  19.0 11.1 %collective-permute-start.4 = (f32[6,24,192]{2,1,0:T(8,128)S(1)}, f32[6,24,192]{2,1,0:T(8,128)S(1)}, u32[]{:S(2)}, u32[]{:S(2)}) collective-permute-start(f32[6,24,192]{2,1,0:T(8,128)S(1)} %stack_rows.1.b0_ref), channel_id=1, source_target_pairs={{0,16},{4,20},{8,24},{12,28},{16,0},{20,4},{24,8},{28,12},{1,17},{... | collective-permute-start | bytes 331784 | tf_op jit(solution)/shard_map/ppermute | solution.py:610
  20.6 9.6 %collective-permute-start.5 = (f32[6,24,192]{2,1,0:T(8,128)S(1)}, f32[6,24,192]{2,1,0:T(8,128)S(1)}, u32[]{:S(2)}, u32[]{:S(2)}) collective-permute-start(f32[6,24,192]{2,1,0:T(8,128)S(1)} %stack_rows.1.b0_ref), channel_id=1, source_target_pairs={{0,24},{4,28},{8,16},{12,20},{16,8},{20,12},{24,0},{28,4},{1,25},{... | collective-permute-start | bytes 331784 | tf_op jit(solution)/shard_map/ppermute | solution.py:610
  21.0 8.5 %collective-permute-start.12 = (f32[2,48,256]{2,1,0:T(8,128)S(1)}, f32[2,48,256]{2,1,0:T(8,128)S(1)}, u32[]{:S(2)}, u32[]{:S(2)}) collective-permute-start(f32[2,48,256]{2,1,0:T(8,128)S(1)} %copy-done.9), channel_id=1, source_target_pairs={{0,2},{1,3},{2,0},{3,1},{4,6},{5,7},{6,4},{7,5},{8,10},{9,11},{10,... | collective-permute-start | bytes 294920 | tf_op jit(solution)/shard_map/ppermute | solution.py:610
  24.5 6.9 %collective-permute-start.13 = (f32[2,48,256]{2,1,0:T(8,128)S(1)}, f32[2,48,256]{2,1,0:T(8,128)}, u32[]{:S(2)}, u32[]{:S(2)}) collective-permute-start(f32[2,48,256]{2,1,0:T(8,128)S(1)} %copy-done.9), channel_id=1, source_target_pairs={{0,3},{1,2},{2,1},{3,0},{4,7},{5,6},{6,5},{7,4},{8,11},{9,10},{10,... | collective-permute-start | bytes 294920 | tf_op jit(solution)/shard_map/ppermute | solution.py:610
  29.6 5.6 %collective-permute-start.6 = (f32[6,24,192]{2,1,0:T(8,128)S(1)}, f32[6,24,192]{2,1,0:T(8,128)S(1)}, u32[]{:S(2)}, u32[]{:S(2)}) collective-permute-start(f32[6,24,192]{2,1,0:T(8,128)S(1)} %stack_rows.1.b0_ref), channel_id=1, source_target_pairs={{0,4},{4,0},{8,12},{12,8},{16,20},{20,16},{24,28},{28,24},{1,5},{5... | collective-permute-start | bytes 331784 | tf_op jit(solution)/shard_map/ppermute | solution.py:610
  29.6 5.6 %collective-permute-start.7 = (f32[6,24,192]{2,1,0:T(8,128)S(1)}, f32[6,24,192]{2,1,0:T(8,128)S(1)}, u32[]{:S(2)}, u32[]{:S(2)}) collective-permute-start(f32[6,24,192]{2,1,0:T(8,128)S(1)} %collective-permute-done.3.b1_ref), channel_id=1, source_target_pairs={{0,4},{4,0},{8,12},{12,8},{16,20},{20,16},{24,28},{28,24},{1,5},{5... | collective-permute-start | bytes 331784 | tf_op jit(solution)/shard_map/ppermute | solution.py:610
  30.1 5.1 %collective-permute-start.8 = (f32[6,24,192]{2,1,0:T(8,128)S(1)}, f32[6,24,192]{2,1,0:T(8,128)}, u32[]{:S(2)}, u32[]{:S(2)}) collective-permute-start(f32[6,24,192]{2,1,0:T(8,128)S(1)} %collective-permute-done.4.b2_ref), channel_id=1, source_target_pairs={{0,4},{4,0},{8,12},{12,8},{16,20},{20,16},{24,28},{28,24},{1,5},{5... | collective-permute-start | bytes 331784 | tf_op jit(solution)/shard_map/ppermute | solution.py:610
  30.2 5.0 %collective-permute-start.9 = (f32[6,24,192]{2,1,0:T(8,128)S(1)}, f32[6,24,192]{2,1,0:T(8,128)}, u32[]{:S(2)}, u32[]{:S(2)}) collective-permute-start(f32[6,24,192]{2,1,0:T(8,128)S(1)} %collective-permute-done.5.b3_ref), channel_id=1, source_target_pairs={{0,4},{4,0},{8,12},{12,8},{16,20},{20,16},{24,28},{28,24},{1,5},{5... | collective-permute-start | bytes 331784 | tf_op jit(solution)/shard_map/ppermute | solution.py:610
  37.3 14.8 %copy-start.8 = (f32[256,1]{1,0:T(8,128)S(1)}, f32[256,1]{1,0:T(8,128)}, u32[]{:S(2)}) copy-start(f32[256,1]{1,0:T(8,128)} %copy.25.g_ref) | copy-start | bytes 3076
  37.3 14.8 %copy-start.19 = (f32[256,256]{1,0:T(8,128)S(1)}, f32[256,256]{1,0:T(8,128)}, u32[]{:S(2)}) copy-start(f32[256,256]{1,0:T(8,128)} %wk_ref.7) | copy-start | bytes 786436
  37.3 14.8 %copy-start.20 = (f32[256,256]{1,0:T(8,128)S(1)}, f32[256,256]{1,0:T(8,128)}, u32[]{:S(2)}) copy-start(f32[256,256]{1,0:T(8,128)} %wv_ref.7) | copy-start | bytes 786436
  37.3 14.8 %copy-start.23 = (f32[384,256]{1,0:T(8,128)S(1)}, f32[384,256]{1,0:T(8,128)}, u32[]{:S(2)}) copy-start(f32[384,256]{1,0:T(8,128)} %get-tuple-element.64.k_ref) | copy-start | bytes 1179652
  37.3 14.8 %copy-start.24 = (f32[384,256]{1,0:T(8,128)S(1)}, f32[384,256]{1,0:T(8,128)}, u32[]{:S(2)}) copy-start(f32[384,256]{1,0:T(8,128)} %get-tuple-element.65.v_ref) | copy-start | bytes 1179652
  37.3 14.8 %copy-start.27 = (f32[96,256]{1,0:T(8,128)S(1)}, f32[96,256]{1,0:T(8,128)}, u32[]{:S(2)}) copy-start(f32[96,256]{1,0:T(8,128)} %get-tuple-element.62.q_ref) | copy-start | bytes 294916
  37.3 14.8 %copy-start.28 = (f32[96,256]{1,0:T(8,128)S(1)}, f32[96,256]{1,0:T(8,128)}, u32[]{:S(2)}) copy-start(f32[96,256]{1,0:T(8,128)} %get-tuple-element.63.m_ref) | copy-start | bytes 294916
  51.9 7.3 %collective-permute-start.10 = (f32[4,4,24,192]{3,2,1,0:T(8,128)S(1)}, f32[4,4,24,192]{3,2,1,0:T(8,128)S(1)}, u32[]{:S(2)}, u32[]{:S(2)}) collective-permute-start(f32[4,4,24,192]{3,2,1,0:T(8,128)S(1)} %get-tuple-element.61), channel_id=1, source_target_pairs={{0,4},{4,0},{8,12},{12,8},{16,20},{20,16},{24,28},{28,24},{1,5},{5... | collective-permute-start | bytes 884744 | tf_op jit(solution)/shard_map/ppermute | solution.py:610
  57.4 1.8 %collective-permute-start.14 = (f32[4,48,192]{2,1,0:T(8,128)S(1)}, f32[4,48,192]{2,1,0:T(8,128)S(1)}, u32[]{:S(2)}, u32[]{:S(2)}) collective-permute-start(f32[4,48,192]{2,1,0:T(8,128)S(1)} %get-tuple-element.67), channel_id=1, source_target_pairs={{0,4},{4,0},{8,12},{12,8},{16,20},{20,16},{24,28},{28,24},{1,5},{5... | collective-permute-start | bytes 442376 | tf_op jit(solution)/shard_map/ppermute | solution.py:610
  59.4 7.5 %collective-permute-start.15 = (f32[6,24,192]{2,1,0:T(8,128)S(1)}, f32[6,24,192]{2,1,0:T(8,128)S(1)}, u32[]{:S(2)}, u32[]{:S(2)}) collective-permute-start(f32[6,24,192]{2,1,0:T(8,128)S(1)} %get-tuple-element.69), channel_id=1, source_target_pairs={{0,8},{4,12},{8,0},{12,4},{16,24},{20,28},{24,16},{28,20},{1,9},{5... | collective-permute-start | bytes 331784 | tf_op jit(solution)/shard_map/ppermute | solution.py:610
  60.9 9.0 %collective-permute-start.16 = (f32[6,24,192]{2,1,0:T(8,128)S(1)}, f32[6,24,192]{2,1,0:T(8,128)S(1)}, u32[]{:S(2)}, u32[]{:S(2)}) collective-permute-start(f32[6,24,192]{2,1,0:T(8,128)S(1)} %get-tuple-element.70), channel_id=1, source_target_pairs={{0,16},{4,20},{8,24},{12,28},{16,0},{20,4},{24,8},{28,12},{1,17},{... | collective-permute-start | bytes 331784 | tf_op jit(solution)/shard_map/ppermute | solution.py:610
  62.5 7.5 %collective-permute-start.17 = (f32[6,24,192]{2,1,0:T(8,128)S(1)}, f32[6,24,192]{2,1,0:T(8,128)S(1)}, u32[]{:S(2)}, u32[]{:S(2)}) collective-permute-start(f32[6,24,192]{2,1,0:T(8,128)S(1)} %get-tuple-element.71), channel_id=1, source_target_pairs={{0,24},{4,28},{8,16},{12,20},{16,8},{20,12},{24,0},{28,4},{1,25},{... | collective-permute-start | bytes 331784 | tf_op jit(solution)/shard_map/ppermute | solution.py:610
  62.9 10.8 %collective-permute-start.21 = (f32[2,48,256]{2,1,0:T(8,128)S(1)}, f32[2,48,256]{2,1,0:T(8,128)S(1)}, u32[]{:S(2)}, u32[]{:S(2)}) collective-permute-start(f32[2,48,256]{2,1,0:T(8,128)S(1)} %get-tuple-element.83), channel_id=1, source_target_pairs={{0,1},{1,0},{2,3},{3,2},{4,5},{5,4},{6,7},{7,6},{8,9},{9,8},{10,11... | collective-permute-start | bytes 294920 | tf_op jit(solution)/shard_map/ppermute | solution.py:610
  63.9 10.6 %collective-permute-start.22 = (f32[2,48,256]{2,1,0:T(8,128)S(1)}, f32[2,48,256]{2,1,0:T(8,128)S(1)}, u32[]{:S(2)}, u32[]{:S(2)}) collective-permute-start(f32[2,48,256]{2,1,0:T(8,128)S(1)} %get-tuple-element.84), channel_id=1, source_target_pairs={{0,2},{1,3},{2,0},{3,1},{4,6},{5,7},{6,4},{7,5},{8,10},{9,11},{10,... | collective-permute-start | bytes 294920 | tf_op jit(solution)/shard_map/ppermute | solution.py:610
  66.9 7.5 %collective-permute-start.23 = (f32[2,48,256]{2,1,0:T(8,128)S(1)}, f32[2,48,256]{2,1,0:T(8,128)S(1)}, u32[]{:S(2)}, u32[]{:S(2)}) collective-permute-start(f32[2,48,256]{2,1,0:T(8,128)S(1)} %get-tuple-element.85), channel_id=1, source_target_pairs={{0,3},{1,2},{2,1},{3,0},{4,7},{5,6},{6,5},{7,4},{8,11},{9,10},{10,... | collective-permute-start | bytes 294920 | tf_op jit(solution)/shard_map/ppermute | solution.py:610
  70.0 5.4 %collective-permute-start.18 = (f32[24,192]{1,0:T(8,128)S(1)}, f32[24,192]{1,0:T(8,128)S(1)}, u32[]{:S(2)}, u32[]{:S(2)}) collective-permute-start(f32[24,192]{1,0:T(8,128)S(1)} %get-tuple-element.78), channel_id=1, source_target_pairs={{0,1},{1,0},{2,3},{3,2},{4,5},{5,4},{6,7},{7,6},{8,9},{9,8},{10,11... | collective-permute-start | bytes 55304 | tf_op jit(solution)/shard_map/ppermute | solution.py:610
  70.7 5.8 %collective-permute-start.19 = (f32[24,192]{1,0:T(8,128)S(1)}, f32[24,192]{1,0:T(8,128)S(1)}, u32[]{:S(2)}, u32[]{:S(2)}) collective-permute-start(f32[24,192]{1,0:T(8,128)S(1)} %get-tuple-element.79), channel_id=1, source_target_pairs={{0,2},{1,3},{2,0},{3,1},{4,6},{5,7},{6,4},{7,5},{8,10},{9,11},{10,... | collective-permute-start | bytes 55304 | tf_op jit(solution)/shard_map/ppermute | solution.py:610
  73.8 5.6 %collective-permute-start.20 = (f32[24,192]{1,0:T(8,128)S(1)}, f32[24,192]{1,0:T(8,128)S(1)}, u32[]{:S(2)}, u32[]{:S(2)}) collective-permute-start(f32[24,192]{1,0:T(8,128)S(1)} %get-tuple-element.80), channel_id=1, source_target_pairs={{0,3},{1,2},{2,1},{3,0},{4,7},{5,6},{6,5},{7,4},{8,11},{9,10},{10,... | collective-permute-start | bytes 55304 | tf_op jit(solution)/shard_map/ppermute | solution.py:610
  (26 other events, 131.0 us)

commit v3 on v2

--- a/solution.py
+++ b/solution.py
@@ -245,7 +245,19 @@
     return jnp.where((lane // HEAD) == h, 1.0, 0.0).astype(dtype)
 
 
-def bias_kernel(rows, x_ref, g_ref, wp_ref, g2_ref, wm_ref, bp_ref, bm_ref):
+def fetch(pairs, sem):
+    copies = [pltpu.make_async_copy(a, b, sem.at[t]) for t, (a, b) in enumerate(pairs)]
+    for copy in copies:
+        copy.start()
+    return copies
+
+
+def bias_kernel(rows, x_ref, y_ref, g_ref, wp_ref, g2_ref, wm_ref, joint_ref, bm_ref):
+    length = x_ref.shape[1]
+    base, wide = y_ref.shape
+    joint_ref[:base] = y_ref[...]
+    if length < wide:
+        joint_ref[base:, length:] = jnp.zeros((wp_ref.shape[0] * rows, wide - length), F32)
     hp, hm = wp_ref.shape[0], wm_ref.shape[0]
     w = cat([wp_ref[...] * g_ref[...], wm_ref[...] * g2_ref[...]], 0)
     wcat = cat(left6(split3(w)), 1)
@@ -253,36 +265,46 @@
         n, _ = normed(x_ref[j])
         res = nt(wcat, cat(right6(split3(n)), 1))
         for h in range(hp):
-            bp_ref[h * rows + j : h * rows + j + 1, :] = res[h : h + 1]
+            at = base + h * rows + j
+            joint_ref[at : at + 1, :length] = res[h : h + 1]
         for h in range(hm):
             bm_ref[h * rows + j : h * rows + j + 1, :] = res[hp + h : hp + h + 1]
 
 
 def pair_project_kernel(
-    x_ref, adj_ref, g_ref, wq_ref, wk_ref, wv_ref, wg_ref, wo_ref, gl_ref, wp_ref, gl2_ref, wm_ref,
-    q_ref, k_ref, v_ref, m_ref, kt_ref, vt_ref, dout_ref, sig_ref, n_ref, scale_ref, wj_ref,
+    x_hbm, adj_hbm, g_ref, wq_hbm, wk_hbm, wv_hbm, wg_hbm, wo_hbm, wp_ref, g2_ref, wm_ref,
+    q_ref, k_ref, v_ref, m_ref, kt_ref, vt_ref, dout_ref, sig_ref, n_ref, scale_ref, wj_ref, wb_ref,
+    x_ref, adj_ref, wq_ref, wk_ref, wv_ref, wg_ref, wo_ref, sem,
 ):
     rows, length, feats = x_ref.shape
     g = g_ref[...]
-    wq = wq_ref[...] * g * (1.0 / math.sqrt(HEAD))
-    wk = wk_ref[...] * g
-    wv = wv_ref[...] * g
-    wg = wg_ref[...] * g
-    w6 = cat(right6(split3(cat([wq, wk], 1))), 0)
-    w3 = cat(right3(split2(cat([wv, wg], 1))), 0)
+    copies = fetch(
+        [
+            (wq_hbm, wq_ref), (wk_hbm, wk_ref), (wv_hbm, wv_ref), (wg_hbm, wg_ref),
+            (wo_hbm, wo_ref), (x_hbm, x_ref), (adj_hbm, adj_ref),
+        ],
+        sem,
+    )
+    for copy in copies:
+        copy.wait()
+    top, low = split2(cat([wq_ref[...], wk_ref[...], wv_ref[...], wg_ref[...]], 1))
+    wb_ref[0] = top
+    wb_ref[1] = low
+    w6 = cat(right6(split3(cat([wq_ref[...], wk_ref[...]], 1))), 0)
+    w3 = cat(right3(split2(cat([wv_ref[...], wg_ref[...]], 1))), 0)
     wo3 = cat(right3(split2(wo_ref[...])), 1)
     for i in range(rows):
         n, scale = normed(x_ref[i])
         n_ref[i] = n
         scale_ref[i] = jnp.broadcast_to(scale, n.shape)
-        parts = split3(n)
+        parts = split3(n * g)
         qk = nn(cat(left6(parts), 1), w6)
         vg = nn(cat(left3(parts), 1), w3)
         d_out = nt(cat(left3(split2(adj_ref[i])), 1), wo3)
         sig = jax.nn.sigmoid(vg[:, feats:])
         dout_ref[i] = d_out
         sig_ref[i] = sig
-        q, k, v = qk[:, :feats], qk[:, feats:], vg[:, :feats]
+        q, k, v = qk[:, :feats] * (1.0 / math.sqrt(HEAD)), qk[:, feats:], vg[:, :feats]
         q_ref[i] = cat(split3(q), 1)
         k_ref[i] = cat(split3(k), 1)
         v_ref[i] = cat(split2(v), 1)
@@ -290,7 +312,7 @@
         kt_ref[i] = cat(split2(k.T), 0)
         vt_ref[i] = cat(split2(v.T), 0)
     hp, hm = wp_ref.shape[0], wm_ref.shape[0]
-    w = cat([wp_ref[...] * gl_ref[...], wm_ref[...] * gl2_ref[...]], 0)
+    w = cat([wp_ref[...] * g, wm_ref[...] * g2_ref[...]], 0)
     lines = [jnp.broadcast_to(w[h : h + 1], (rows, feats)) for h in range(hp + hm)]
     lines += [jnp.zeros((LANES - rows * (hp + hm), feats), F32)]
     spread = cat(lines, 0)
@@ -300,18 +322,41 @@
         wj_ref[:, j * feats : (j + 1) * feats] = cat(right3(split2(mine)), 0)
 
 
+def pack(block_of, count, lines, out_ref):
+    half = count // 2
+    for t in range(half):
+        first, second = block_of(t), block_of(t + half)
+        out_ref[t * lines : (t + 1) * lines] = first[:, :LANES]
+        out_ref[(t + half) * lines : (t + half + 1) * lines] = second[:, :LANES]
+        rest = cat([first[:, LANES:], second[:, LANES:]], 1)
+        out_ref[(t + count) * lines : (t + count + 1) * lines] = rest
+
+
+def unpack(dense, count, lines):
+    half = count // 2
+    blocks = []
+    for t in range(count):
+        rest = dense[(count + t % half) * lines : (count + t % half + 1) * lines]
+        rest = rest[:, : LANES // 2] if t < half else rest[:, LANES // 2 :]
+        blocks.append(cat([dense[t * lines : (t + 1) * lines], rest], 1))
+    return blocks
+
+
 def gather_chips(natural, refs, core, chip):
-    half = len(refs) // 2
-    for t in range(half):
-        at = lax.bitwise_xor(chip, t) * 2
-        natural[at + core] = refs[t][...]
-        natural[at + 1 - core] = refs[half + t][...]
+    _, count, lines, _ = natural.shape
+    for (own_ref, others_ref), side in zip((refs[:2], refs[2:]), (core, 1 - core)):
+        for t in range(others_ref.shape[0] + 1):
+            at = lax.bitwise_xor(chip, t) * 2 + side
+            dense = others_ref[t - 1] if t > 0 else own_ref[...]
+            for i, block in enumerate(unpack(dense, count, lines)):
+                natural[at, i] = block
 
 
 def pair_kernel(
     dims,
     q_ref, k_ref, v_ref, m_ref, kt_ref, vt_ref,
-    b0_ref, b1_ref, b2_ref, b3_ref, b4_ref, b5_ref, b6_ref, b7_ref,
+    b0_ref, b1_ref, b2_ref, b3_ref,
+    after_ref,
     ot_ref, dqt_ref, dk_ref, dv_ref, near_ref, far_ref,
     bt, dbt, stack, natural,
 ):
@@ -323,7 +368,7 @@
 
     @pl.when(step == 0)
     def _():
-        blocks = (b0_ref, b1_ref, b2_ref, b3_ref, b4_ref, b5_ref, b6_ref, b7_ref)
+        blocks = (b0_ref, b1_ref, b2_ref, b3_ref)
         gather_chips(natural, blocks, core, chip)
         for z in range(res_n):
             zi = lax.bitwise_xor(res, z)
@@ -405,12 +450,11 @@
 
 def pair_back_kernel(
     ot_ref, dqt_ref, dk_ref, dv_ref, dout_ref, sig_ref,
-    g_ref, wq_ref, wk_ref, wv_ref, wg_ref, dn_ref,
+    g_ref, wb_ref, dn_ref,
 ):
     rows, length, feats = dk_ref.shape
     g = g_ref[...]
-    wq = wq_ref[...] * g * (1.0 / math.sqrt(HEAD))
-    w1, w2 = split2(cat([wq, wk_ref[...] * g, wv_ref[...] * g, wg_ref[...] * g], 1))
+    w1, w2 = wb_ref[0], wb_ref[1]
 
     def lines(flat):
         heads = flat.shape[1] // length
@@ -419,36 +463,49 @@
     for i in range(rows):
         o, sig = lines(ot_ref[i]), sig_ref[i]
         d_gate = dout_ref[i] * o * sig * (1.0 - sig)
-        t1, t2 = split2(cat([lines(dqt_ref[i]), dk_ref[i], dv_ref[i], d_gate], 1))
-        dn_ref[i] = nt(t1, w1) + nt(t1, w2) + nt(t2, w1)
+        dq = lines(dqt_ref[i]) * (1.0 / math.sqrt(HEAD))
+        t1, t2 = split2(cat([dq, dk_ref[i], dv_ref[i], d_gate], 1))
+        dn_ref[i] = g * (nt(t1, w1) + nt(t1, w2) + nt(t2, w1))
 
 
 def msa_project_kernel(
-    y0_ref, y1_ref, y2_ref, y3_ref, adj_ref,
-    g_ref, wq_ref, wk_ref, wv_ref, wg_ref, wo_ref,
-    q_ref, m_ref, dout_ref, sig_ref, k_ref, v_ref,
-    yall,
+    y0_ref, y1_ref, y2_ref, y3_ref, adj_hbm,
+    g_ref, wq_hbm, wk_hbm, wv_hbm, wg_hbm, wo_hbm,
+    q_ref, m_ref, dout_ref, sig_ref, k_ref, v_ref, wkv_ref, wqg_ref,
+    yall, adj_ref, wq_ref, wk_ref, wv_ref, wg_ref, wo_ref, sem,
 ):
     res = lax.axis_index("res")
-    n_seqs, own, feats = y0_ref.shape
+    n_seqs, own, feats = adj_ref.shape
     n_keys = yall.shape[1]
     g = g_ref[...]
+    copies = fetch(
+        [
+            (wk_hbm, wk_ref), (wv_hbm, wv_ref), (wq_hbm, wq_ref), (wg_hbm, wg_ref),
+            (wo_hbm, wo_ref), (adj_hbm, adj_ref),
+        ],
+        sem,
+    )
     for t, ref in enumerate((y0_ref, y1_ref, y2_ref, y3_ref)):
         at = pl.multiple_of(lax.bitwise_xor(res, t) * own, own)
         for b in range(n_seqs):
-            yall[b, pl.ds(at, own), :] = ref[b]
-    n_own, _ = normed(y0_ref[...].reshape(n_seqs * own, feats))
+            yall[b, pl.ds(at, own), :] = ref[b * own : (b + 1) * own, :]
+    n_own, _ = normed(y0_ref[: n_seqs * own])
     n_all, _ = normed(yall[...].reshape(n_seqs * n_keys, feats))
-    own_parts, all_parts = split3(n_own), split3(n_all)
-    wq = wq_ref[...] * g * (1.0 / math.sqrt(HEAD))
-    q = nn(cat(left6(own_parts), 1), cat(right6(split3(wq)), 0))
-    gate = nn(cat(left3(own_parts), 1), cat(right3(split2(wg_ref[...] * g)), 0))
-    k = nn(cat(left6(all_parts), 1), cat(right6(split3(wk_ref[...] * g)), 0))
-    v = nn(cat(left3(all_parts), 1), cat(right3(split2(wv_ref[...] * g)), 0))
+    own_parts, all_parts = split3(n_own * g), split3(n_all * g)
+    for copy in copies:
+        copy.wait()
+    for ref, pair in ((wkv_ref, (wk_ref, wv_ref)), (wqg_ref, (wq_ref, wg_ref))):
+        top, low = split2(cat([pair[0][...], pair[1][...]], 1))
+        ref[0] = top
+        ref[1] = low
+    q = nn(cat(left6(own_parts), 1), cat(right6(split3(wq_ref[...])), 0))
+    gate = nn(cat(left3(own_parts), 1), cat(right3(split2(wg_ref[...])), 0))
+    k = nn(cat(left6(all_parts), 1), cat(right6(split3(wk_ref[...])), 0))
+    v = nn(cat(left3(all_parts), 1), cat(right3(split2(wv_ref[...])), 0))
     adj = adj_ref[...].reshape(n_seqs * own, feats)
     d_out = nt(cat(left3(split2(adj)), 1), cat(right3(split2(wo_ref[...])), 1))
     sig = jax.nn.sigmoid(gate)
-    q_ref[...] = q
+    q_ref[...] = q * (1.0 / math.sqrt(HEAD))
     m_ref[...] = d_out * sig
     dout_ref[...] = d_out
     sig_ref[...] = sig
@@ -459,18 +516,18 @@
 def msa_kernel(
     dims,
     q_ref, m_ref, k_ref, v_ref,
-    b0_ref, b1_ref, b2_ref, b3_ref, b4_ref, b5_ref, b6_ref, b7_ref,
-    g_ref, wk_ref, wv_ref, after_ref,
-    o_ref, dq_ref, r0_ref, r1_ref, r2_ref, r3_ref, near_ref, far_ref,
+    b0_ref, b1_ref, b2_ref, b3_ref,
+    wkv_ref,
+    o_ref, dq_ref, r0_ref, r1_ref, r23_ref, near_ref, far_ref,
     bias, dbias, dyall, natural,
 ):
     rows, heads, seq_n, res_n = dims
     seq, res = lax.axis_index("seq"), lax.axis_index("res")
     core, chip = lax.rem(seq, 2), lax.div(seq, 2)
-    n_seqs, own, feats = r0_ref.shape
-    n_keys = own * res_n
+    n_seqs, n_keys, feats = dyall.shape
+    own = n_keys // res_n
     tiles, group = feats // LANES, LANES // HEAD
-    blocks = (b0_ref, b1_ref, b2_ref, b3_ref, b4_ref, b5_ref, b6_ref, b7_ref)
+    blocks = (b0_ref, b1_ref, b2_ref, b3_ref)
     gather_chips(natural, blocks, core, chip)
     for s in range(seq_n):
         block = cat([natural[s, res_n], natural[s, res_n + 1]], 0)
@@ -489,7 +546,7 @@
             total = total + fmasks[u] * full[u * own : (u + 1) * own]
         return total
 
-    b1, b2 = split2(cat([wk_ref[...] * g_ref[...], wv_ref[...] * g_ref[...]], 1))
+    b1, b2 = wkv_ref[0], wkv_ref[1]
     for b in range(n_seqs):
         near = slice(b * own, (b + 1) * own)
         wide = slice(b * n_keys, (b + 1) * n_keys)
@@ -522,10 +579,11 @@
             dvt.append(both[:LANES] + both[LANES:] + nn(mt1, p2))
         t1, t2 = split2(cat([a.T for a in dkt + dvt], 1))
         dyall[b] = nt(t1, b1) + nt(t1, b2) + nt(t2, b1)
-    for t, ref in enumerate((r0_ref, r1_ref, r2_ref, r3_ref)):
+    for t, (ref, base) in enumerate(((r0_ref, 0), (r1_ref, 0), (r23_ref, 0), (r23_ref, n_seqs))):
         at = pl.multiple_of(lax.bitwise_xor(res, t) * own, own)
         for b in range(n_seqs):
-            ref[b] = dyall[b, pl.ds(at, own), :]
+            to = (base + b) * own
+            ref[to : to + own, :] = dyall[b, pl.ds(at, own), :]
     for s in range(seq_n):
         ci = lax.bitwise_xor(chip, s // 2)
         at = [h * own + s * rows for h in range(heads)]
@@ -540,56 +598,71 @@
             far_ref[ci] = block
 
 
-def aligned_back_kernel(
-    o_ref, dq_ref, dout_ref, sig_ref, g_ref, wq_ref, wg_ref, r0_ref, dy_ref
-):
-    n_seqs, own, feats = r0_ref.shape
+def aligned_back_kernel(o_ref, dq_ref, dout_ref, sig_ref, wqg_ref, r0_ref, dy_ref):
     sig = sig_ref[...]
     d_gate = dout_ref[...] * o_ref[...] * sig * (1.0 - sig)
-    t1, t2 = split2(cat([dq_ref[...], d_gate], 1))
-    wq = wq_ref[...] * g_ref[...] * (1.0 / math.sqrt(HEAD))
-    b1, b2 = split2(cat([wq, wg_ref[...] * g_ref[...]], 1))
-    dy = nt(t1, b1) + nt(t1, b2) + nt(t2, b1)
-    dy_ref[...] = dy.reshape(n_seqs, own, feats) + r0_ref[...]
-
-
-def aligned_end_kernel(y_ref, dy_ref, r1_ref, r2_ref, r3_ref, out_ref):
-    n, scale = normed(y_ref[...])
-    out_ref[...] = normed_back(n, scale, dy_ref[...] + r1_ref[...] + r2_ref[...] + r3_ref[...])
-
-
-def stack_kernel(p0_ref, p1_ref, p2_ref, p3_ref, m_ref, after_ref, out_ref):
-    lines = p0_ref.shape[0]
-    for t, ref in enumerate((p0_ref, p1_ref, p2_ref, p3_ref)):
+    t1, t2 = split2(cat([dq_ref[...] * (1.0 / math.sqrt(HEAD)), d_gate], 1))
+    b1, b2 = wqg_ref[0], wqg_ref[1]
+    dy_ref[...] = nt(t1, b1) + nt(t1, b2) + nt(t2, b1) + r0_ref[...]
+
+
+def aligned_end_kernel(y_ref, g_ref, dy_ref, r23_ref, r1_ref, out_ref):
+    n_seqs, own, _ = out_ref.shape
+    g = g_ref[...]
+    for b in range(n_seqs):
+        at = slice(b * own, (b + 1) * own)
+        n, scale = normed(y_ref[at])
+        out_ref[b] = normed_back(n, scale, g * (dy_ref[at] + r23_ref[at] + r1_ref[at]))
+
+
+def stack_kernel(length, p0_ref, p1_ref, p2_ref, p3_ref, m_ref, after_ref, out_ref):
+    lines = m_ref.shape[0] // 2
+    blocks = [ref[ref.shape[0] - lines :, :length] for ref in (p0_ref, p1_ref, p2_ref, p3_ref)]
+    blocks += [m_ref[:lines], m_ref[lines:]]
+    pack(lambda t: blocks[t], len(blocks), lines, out_ref)
+
+
+def chip_stack_kernel(b1_ref, b2_ref, b3_ref, after_ref, out_ref):
+    for t, ref in enumerate((b1_ref, b2_ref, b3_ref)):
         out_ref[t] = ref[...]
-    out_ref[4] = m_ref[:lines]
-    out_ref[5] = m_ref[lines:]
 
 
 def core_sum_kernel(p0_ref, p1_ref, m0_ref, m1_ref, after_ref, s0_ref, s1_ref, s2_ref, s3_ref):
     res_n, lines = p0_ref.shape[1:3]
     for t, ref in enumerate((s0_ref, s1_ref, s2_ref, s3_ref)):
-        ref[:res_n] = p0_ref[t] + p1_ref[t]
-        ref[res_n] = m0_ref[t, :lines] + m1_ref[t, :lines]
-        ref[res_n + 1] = m0_ref[t, lines:] + m1_ref[t, lines:]
+        pair = p0_ref[t] + p1_ref[t]
+        msa = m0_ref[t] + m1_ref[t]
+        blocks = [pair[z] for z in range(res_n)] + [msa[:lines], msa[lines:]]
+        pack(lambda i: blocks[i], len(blocks), lines, ref)
 
 
 def chip_sum_kernel(
-    s0_ref, s1_ref, s2_ref, s3_ref, after_ref, c0_ref, c1_ref, c2_ref, c3_ref, m_ref
+    s0_ref, s1_ref, s2_ref, s3_ref, r1_ref, r23_ref, after_ref,
+    c0_ref, joint_ref, c2_ref, c3_ref, m_ref,
 ):
-    lines = c0_ref.shape[0]
-    for t, ref in enumerate((c0_ref, c1_ref, c2_ref, c3_ref)):
-        ref[...] = s0_ref[t] + s1_ref[t] + s2_ref[t] + s3_ref[t]
-    for t in range(2):
-        total = s0_ref[4 + t] + s1_ref[4 + t] + s2_ref[4 + t] + s3_ref[4 + t]
-        m_ref[t * lines : (t + 1) * lines] = total
+    lines, length = c0_ref.shape
+    base = r1_ref.shape[0]
+    joint_ref[:base] = r1_ref[...] + r23_ref[base:]
+    if length < joint_ref.shape[1]:
+        joint_ref[base:, length:] = jnp.zeros((lines, joint_ref.shape[1] - length), F32)
+    total = s0_ref[...] + s1_ref[...] + s2_ref[...] + s3_ref[...]
+    blocks = unpack(total, 2 * total.shape[0] // (3 * lines), lines)
+    for t, ref in enumerate((c0_ref, joint_ref, c2_ref, c3_ref)):
+        if t == 1:
+            ref[base:, :length] = blocks[t]
+        else:
+            ref[...] = blocks[t]
+    m_ref[:lines] = blocks[-2]
+    m_ref[lines:] = blocks[-1]
 
 
 def pair_end_kernel(
     n_ref, scale_ref, dn_ref, p0_ref, p1_ref, p2_ref, p3_ref, m_ref, wj_ref, out_ref
 ):
     rows, length, feats = n_ref.shape
-    pair = p0_ref[...] + p1_ref[...] + p2_ref[...] + p3_ref[...]
+    lines = p0_ref.shape[0]
+    pair = p0_ref[...] + p2_ref[...] + p3_ref[...]
+    pair = pair + p1_ref[p1_ref.shape[0] - lines :, :length]
     msa = m_ref[...]
     pad = jnp.zeros((LANES - pair.shape[0] - msa.shape[0], length), F32)
     b = cat([pair, msa, pad], 0).T
@@ -604,6 +677,14 @@
 
 def params(mib, **more):
     return pltpu.CompilerParams(vmem_limit_bytes=mib * MIB, **more)
+
+
+def hbm(count):
+    return [pl.BlockSpec(memory_space=pltpu.HBM)] * count
+
+
+def vmem(count):
+    return [pl.BlockSpec(memory_space=pltpu.VMEM)] * count
 
 
 def swap(values, axis, size, offset):
@@ -642,59 +723,93 @@
     gain = coupled_scaler.reshape(1, feats)
     gain2 = coupled_scaler_for_offset.reshape(1, feats)
 
-    others = [swap(aligned_embedding, "res", res_n, t) for t in range(1, res_n)]
-    pair_rows, msa_rows = pl.pallas_call(
+    lines, base = hp * rows, n_seqs * own
+    mixed_rows, msa_rows = pl.pallas_call(
         functools.partial(bias_kernel, rows),
-        out_shape=(shape(hp * rows, length), shape(hm * rows, length)),
-        compiler_params=params(16),
+        out_shape=(shape(base + lines, wide), shape(hm * rows, length)),
+        compiler_params=params(63),
         name="bias_rows",
-    )(coupled_embedding, gain, wp_t, gain2, wm_t)
+    )(
+        coupled_embedding, aligned_embedding.reshape(base, wide), gain, wp_t, gain2, wm_t
+    )
+    columns = [mixed_rows] + [swap(mixed_rows, "res", res_n, t) for t in range(1, res_n)]
+
     bf = lambda *s: jax.ShapeDtypeStruct(s, BF16)
-    gain_in = coupled_scaler.reshape(feats, 1)
-    q, k, v, m, kt, vt, d_out, sig, n, scale, wj = pl.pallas_call(
+    q, k, v, m, kt, vt, d_out, sig, n, scale, wj, wb = pl.pallas_call(
         pair_project_kernel,
+        in_specs=hbm(2) + vmem(1) + hbm(5) + vmem(3),
+        scratch_shapes=[pltpu.VMEM((rows, length, feats), F32)] * 2
+        + [pltpu.VMEM((feats, feats), F32)] * 5 + [pltpu.SemaphoreType.DMA((7,))],
         out_shape=(
             bf(rows, length, 3 * feats), bf(rows, length, 3 * feats),
             bf(rows, length, 2 * feats), bf(rows, length, 2 * feats),
             bf(rows, 2 * feats, length), bf(rows, 2 * feats, length),
-        ) + (shape(rows, length, feats),) * 4 + (bf(3 * LANES, rows * feats),),
-        compiler_params=params(63),
+        ) + (shape(rows, length, feats),) * 4
+        + (bf(3 * LANES, rows * feats), bf(2, feats, 4 * feats)),
+        compiler_params=params(32),
         name="pair_project",
         cost_estimate=pl.CostEstimate(flops=2 * 10**9, bytes_accessed=10**7, transcendentals=0),
     )(
-        coupled_embedding, coupled_change_adjoint, gain_in, coupled_asking_matrix,
+        coupled_embedding, coupled_change_adjoint, gain, coupled_asking_matrix,
         coupled_lookup_matrix, coupled_content_matrix, coupled_sigmoid_matrix,
-        coupled_result_matrix, gain, wp_t, gain2, wm_t,
-    )
-
-    lines = hp * rows
-    joint = (res_n + 2, lines, length)
-    vmem = lambda count: [pl.BlockSpec(memory_space=pltpu.VMEM)] * count
+        coupled_result_matrix, wp_t, gain2, wm_t,
+    )
+
+    joint = (3 * (res_n + 2) * lines // 2, LANES)
+    spread = pltpu.VMEM((seq_n, res_n + 2, lines, length), F32)
     after = [pl.BlockSpec(memory_space=pl.ANY)]
     first = pl.pallas_call(
-        stack_kernel,
+        functools.partial(stack_kernel, length),
         in_specs=vmem(5) + after,
         out_shape=shape(*joint),
         compiler_params=params(16),
         name="stack_rows",
-    )(pair_rows, *[swap(pair_rows, "res", res_n, t) for t in range(1, res_n)], msa_rows, n)
-    blocks = [first] + [swap(first, "seq", seq_n, 2 * t) for t in range(1, chips)]
-    blocks = blocks + [swap(a, "seq", seq_n, 1) for a in blocks]
-
-    wide_gain = aligned_scaler.reshape(wide, 1)
+    )(*columns, msa_rows, n)
+
+    wide_gain = aligned_scaler.reshape(1, wide)
     flat = lambda count: shape(n_seqs * count, wide)
-    mq, mm, m_out, m_sig, mk, mv = pl.pallas_call(
+    mq, mm, m_out, m_sig, mk, mv, wkv, wqg = pl.pallas_call(
         msa_project_kernel,
-        out_shape=(flat(own),) * 4 + (flat(length),) * 2,
-        scratch_shapes=[pltpu.VMEM((n_seqs, length, wide), F32)],
-        compiler_params=params(63),
+        in_specs=vmem(4) + hbm(1) + vmem(1) + hbm(5),
+        out_shape=(flat(own),) * 4 + (flat(length),) * 2 + (bf(2, wide, 2 * wide),) * 2,
+        scratch_shapes=[
+            pltpu.VMEM((n_seqs, length, wide), F32), pltpu.VMEM((n_seqs, own, wide), F32),
+        ] + [pltpu.VMEM((wide, wide), F32)] * 5 + [pltpu.SemaphoreType.DMA((6,))],
+        compiler_params=params(32),
         name="msa_project",
         cost_estimate=pl.CostEstimate(flops=10**9, bytes_accessed=10**7, transcendentals=0),
     )(
-        aligned_embedding, *others, aligned_change_adjoint, wide_gain, aligned_asking_matrix,
+        *columns, aligned_change_adjoint, wide_gain, aligned_asking_matrix,
         aligned_lookup_matrix, aligned_content_matrix, aligned_sigmoid_matrix,
         aligned_result_matrix,
     )
+
+    rest = pl.pallas_call(
+        chip_stack_kernel,
+        in_specs=vmem(3) + after,
+        out_shape=shape(chips - 1, *joint),
+        compiler_params=params(16),
+        name="stack_chips",
+    )(*[swap(first, "seq", seq_n, 2 * t) for t in range(1, chips)], mq)
+    blocks = [first, rest, swap(first, "seq", seq_n, 1), swap(rest, "seq", seq_n, 1)]
+
+    stretch = pltpu.VMEM((hm * own, length), F32)
+    o, dq, kept, r1, r23, msa_near, msa_far = pl.pallas_call(
+        functools.partial(msa_kernel, (rows, hm, seq_n, res_n)),
+        out_shape=(flat(own),) * 4 + (shape(2 * base, wide),)
+        + (shape(chips, hm * rows, length),) * 2,
+        scratch_shapes=[
+            stretch, stretch, pltpu.VMEM((n_seqs, length, wide), F32),
+            spread,
+        ],
+        compiler_params=params(32),
+        name="msa_attention",
+        cost_estimate=pl.CostEstimate(flops=4 * 10**9, bytes_accessed=10**7, transcendentals=0),
+    )(
+        mq, mm, mk, mv, *blocks, wkv,
+    )
+    far_msa = swap(msa_far, "seq", seq_n, 1)
+    r23 = swap(r23, "res", res_n, 2)
 
     piece = lambda *s: pl.BlockSpec((1,) + s, lambda i: (i, 0, 0))
     whole = lambda *s: pl.BlockSpec(s, lambda i: (0,) * len(s))
@@ -706,7 +821,7 @@
             piece(length, 3 * feats), piece(length, 3 * feats),
             piece(length, 2 * feats), piece(length, 2 * feats),
             piece(2 * feats, length), piece(2 * feats, length),
-        ] + [whole(*joint)] * seq_n,
+        ] + [whole(*joint), whole(chips - 1, *joint)] * 2 + after,
         out_specs=(
             piece(HEAD, hp * length), piece(HEAD, hp * length),
             piece(length, feats), piece(length, feats), whole(*quarter), whole(*quarter),
@@ -720,12 +835,12 @@
             pltpu.VMEM((length, hp * length), F32),
             pltpu.VMEM((length, hp * length), F32),
             pltpu.VMEM((hp * length, length), F32),
-            pltpu.VMEM((seq_n,) + joint, F32),
+            spread,
         ],
-        compiler_params=params(48),
+        compiler_params=params(32),
         name="pair_attention",
         cost_estimate=pl.CostEstimate(flops=10**10, bytes_accessed=10**7, transcendentals=0),
-    )(q, k, v, m, kt, vt, *blocks)
+    )(q, k, v, m, kt, vt, *blocks, kept)
     far_pair = swap(far, "seq", seq_n, 1)
     dn = pl.pallas_call(
         pair_back_kernel,
@@ -734,28 +849,8 @@
         name="pair_back",
         cost_estimate=pl.CostEstimate(flops=10**9, bytes_accessed=10**7, transcendentals=0),
     )(
-        ot, dqt, dk, dv, d_out, sig, gain_in, coupled_asking_matrix,
-        coupled_lookup_matrix, coupled_content_matrix, coupled_sigmoid_matrix,
-    )
-    stretch = pltpu.VMEM((hm * own, length), F32)
-    o, dq, kept, r1, r2, r3, msa_near, msa_far = pl.pallas_call(
-        functools.partial(msa_kernel, (rows, hm, seq_n, res_n)),
-        out_shape=(flat(own),) * 2 + (shape(n_seqs, own, wide),) * 4
-        + (shape(chips, hm * rows, length),) * 2,
-        in_specs=vmem(15) + after,
-        scratch_shapes=[
-            stretch, stretch, pltpu.VMEM((n_seqs, length, wide), F32),
-            pltpu.VMEM((seq_n,) + joint, F32),
-        ],
-        compiler_params=params(48),
-        name="msa_attention",
-        cost_estimate=pl.CostEstimate(flops=4 * 10**9, bytes_accessed=10**7, transcendentals=0),
-    )(
-        mq, mm, mk, mv, *blocks, wide_gain,
-        aligned_lookup_matrix, aligned_content_matrix, near,
-    )
-    far_msa = swap(msa_far, "seq", seq_n, 1)
-    arrived = [swap(a, "res", res_n, t + 1) for t, a in enumerate((r1, r2, r3))]
+        ot, dqt, dk, dv, d_out, sig, gain, wb,
+    )
     sums = pl.pallas_call(
         core_sum_kernel,
         in_specs=vmem(4) + after,
@@ -765,41 +860,44 @@
     )(near, far_pair, msa_near, far_msa, dn)
     dy = pl.pallas_call(
         aligned_back_kernel,
-        out_shape=shape(n_seqs, own, wide),
+        out_shape=flat(own),
         compiler_params=params(16),
         name="aligned_back",
         cost_estimate=pl.CostEstimate(flops=10**9, bytes_accessed=10**6, transcendentals=0),
-    )(o, dq, m_out, m_sig, wide_gain, aligned_asking_matrix, aligned_sigmoid_matrix, kept)
-    *column, msa_sum = pl.pallas_call(
+    )(o, dq, m_out, m_sig, wqg, kept)
+    c0, mixed_sum, c2, c3, msa_sum = pl.pallas_call(
         chip_sum_kernel,
-        in_specs=vmem(4) + after,
-        out_shape=(shape(lines, length),) * res_n + (shape(hm * rows, length),),
+        in_specs=vmem(6) + after,
+        out_shape=(
+            shape(lines, length), shape(base + lines, wide), shape(lines, length),
+            shape(lines, length), shape(hm * rows, length),
+        ),
         compiler_params=params(16),
         name="chip_sum",
-    )(sums[0], *[swap(sums[t], "seq", seq_n, 2 * t) for t in range(1, chips)], dy)
-    parts = [column[0]] + [swap(column[t], "res", res_n, t) for t in range(1, res_n)]
+    )(sums[0], *[swap(sums[t], "seq", seq_n, 2 * t) for t in range(1, chips)], r1, r23, dy)
+    mixed_sum, c2, c3 = [swap(a, "res", res_n, t) for a, t in ((mixed_sum, 1), (c2, 2), (c3, 3))]
 
     aligned_out = pl.pallas_call(
         aligned_end_kernel,
         out_shape=shape(n_seqs, own, wide),
         compiler_params=params(16),
         name="aligned_end",
-    )(aligned_embedding, dy, *arrived)
+    )(mixed_rows, wide_gain, dy, r23, mixed_sum)
     coupled_out = pl.pallas_call(
         pair_end_kernel,
         out_shape=shape(rows, length, feats),
         compiler_params=params(16),
         name="pair_end",
-    )(n, scale, dn, *parts, msa_sum, wj)
+    )(n, scale, dn, c0, mixed_sum, c2, c3, msa_sum, wj)
     return coupled_out, aligned_out
 
 
 def on_device(seq_n, res_n, *arrays):
     length = arrays[0].shape[1]
     rows = arrays[0].shape[0]
-    narrow = length <= 2 * LANES and HP * length % TILE == 0
+    narrow = length <= arrays[1].shape[2] and HP * length % TILE == 0
     narrow = narrow and rows * (HP + ALIGNED_SPLITS) <= LANES
-    narrow = narrow and ALIGNED_SPLITS == 2 * HP
+    narrow = narrow and ALIGNED_SPLITS == 2 * HP and 2 * (length - LANES) == LANES
     if narrow and seq_n == 8 and res_n == 4:
         return fused_on_device(seq_n, res_n, *arrays)
     return scanned_on_device(*arrays)

time: 81.3 us -> 70.3 us (0.86)
  starting transfers between devices: 29.8 us -> 21.2 us
  waiting for transfers between devices: 8.47 us -> 14.8 us
  Pallas kernels: 34.3 us -> 28.6 us
  local copies, waits for them, and re-layouts: 7.21 us -> 4.49 us
    ppermute x24 -> x17, starting transfers between devices: 29.8 us -> 21.2 us  [swap(): return lax.ppermute(values, axis, [(i, i ^ offset) for i in range(size)])]
    ppermute x24 -> x17, waiting for transfers between devices: 8.47 us -> 14.8 us  [swap(): return lax.ppermute(values, axis, [(i, i ^ offset) for i in range(size)])]
    pallas_call x6 -> x7, Pallas kernels: 10.9 us -> 7.47 us  [the longest x1 2.65 us: fused_on_device(): pl.pallas_call(functools.partial(bias_kernel, rows), out_shape=(shape(bas...]
    reshape x2 -> x0, local copies, waits for them, and re-layouts: 1.53 us -> none  [the longest x1 0.81 us: fused_on_device(): wide_gain = aligned_scaler.reshape(wide, 1)]
    pallas_call x1, Pallas kernels: 14.6 us -> 13.2 us  [fused_on_device(): pl.pallas_call(functools.partial(pair_kernel, (rows, hp, seq_n, res_n)),...]
    unnamed x68 -> x40, local copies, waits for them, and re-layouts: 5.67 us -> 4.49 us
    pallas_call x1, Pallas kernels: 5.24 us -> 4.22 us  [fused_on_device(): pl.pallas_call(functools.partial(msa_kernel, (rows, hm, seq_n, res_n)), o...]
  transfers between devices with their start and end apart: 24 -> 17, of which waited for: 3 -> 7; matrix products, arithmetic and copies ran while one was open for 2% -> 0% of each run, Pallas kernels for 22% -> 10%
where the time goes in v3:
time: 70.3 us; the launch traced here: 69.9 us
  Pallas kernels  28.6 us (41%)
  starting transfers between devices  21.2 us (30%)
  waiting for transfers between devices  14.8 us (21%)
  local copies, waits for them, and re-layouts  4.49 us (6%)
  between operations  0.92 us (1%)
    ppermute x17, starting transfers between devices, swap(): return lax.ppermute(values, axis, [(i, i ^ offset) for i in range(size)])  21.2 us
    ppermute x17, waiting for transfers between devices, swap(): return lax.ppermute(values, axis, [(i, i ^ offset) for i in range(size)])  14.8 us
    pallas_call x1, Pallas kernels, fused_on_device(): pl.pallas_call(functools.partial(pair_kernel, (rows, hp, seq_n, res_n)),...  13.2 us
    unnamed x40, local copies, waits for them, and re-layouts  4.49 us
    pallas_call x1, Pallas kernels, fused_on_device(): pl.pallas_call(functools.partial(msa_kernel, (rows, hm, seq_n, res_n)), o...  4.22 us
    pallas_call x1, Pallas kernels, fused_on_device(): pl.pallas_call(functools.partial(bias_kernel, rows), out_shape=(shape(bas...  2.65 us
    pallas_call x1, Pallas kernels, fused_on_device(): pl.pallas_call(pair_project_kernel, in_specs=hbm(2) + vmem(1) + hbm(5) +...  2.46 us
    pallas_call x1, Pallas kernels, fused_on_device(): pl.pallas_call(msa_project_kernel, in_specs=vmem(4) + hbm(1) + vmem(1) +...  1.77 us
  transfers between devices with their start and end apart: 17, of which 7 were waited for; matrix products, arithmetic and copies ran while one was open for 0% of the time, Pallas kernels for 10%

profile of v3, /device:TPU:0, one launch (start us, length us, event | category | flops | bytes accessed | tf_op | source)
XLA Modules:
  0.0 69.9 jit_solution(10159478979054255672)
XLA Ops:
  0.7 2.6 %bias_rows.1 = (f32[120,256]{1,0:T(8,128)}, f32[48,192]{1,0:T(8,128)}) custom-call(f32[6,192,128]{2,1,0:T(8,128)} %x_ref.1, f32[96,256]{1,0:T(8,128)} %bitcast.17, f32[1,128]{1,0:T(1,128)} %bitcast.10, f32[4,128]{1,0:T(4,128)} %bitcast.8, f32[1,128]{1,0:T(1,128)} %bitcast.15, f32[8,128]{1,0:T(8,128)} %bitcast.6), custom_call_target="tpu_custom_call" | custom-call | tf_op jit(solution)/shard_map/bias_rows/pallas_call | solution.py:727
  3.3 3.1 %collective-permute-start = (f32[120,256]{1,0:T(8,128)}, f32[120,256]{1,0:T(8,128)S(1)}, u32[]{:S(2)}, u32[]{:S(2)}) collective-permute-start(f32[120,256]{1,0:T(8,128)} %get-tuple-element.54.p0_ref.y0_ref.y_ref), channel_id=1, source_target_pairs={{0,1},{1,0},{2,3},{3,2},{4,5},{5,4},{6,7},{7,6},{8,9},{9,8},{10,11... | collective-permute-start | bytes 368648 | tf_op jit(solution)/shard_map/ppermute | solution.py:691
  6.4 2.6 %collective-permute-start.1 = (f32[120,256]{1,0:T(8,128)}, f32[120,256]{1,0:T(8,128)S(1)}, u32[]{:S(2)}, u32[]{:S(2)}) collective-permute-start(f32[120,256]{1,0:T(8,128)} %get-tuple-element.54.p0_ref.y0_ref.y_ref), channel_id=1, source_target_pairs={{0,2},{1,3},{2,0},{3,1},{4,6},{5,7},{6,4},{7,5},{8,10},{9,11},{10,... | collective-permute-start | bytes 368648 | tf_op jit(solution)/shard_map/ppermute | solution.py:691
  9.1 1.1 %copy-done.8 = f32[6,192,128]{2,1,0:T(8,128)S(1)} copy-done((f32[6,192,128]{2,1,0:T(8,128)S(1)}, f32[6,192,128]{2,1,0:T(8,128)}, u32[]{:S(2)}) %copy-start.8) | copy-done | bytes 589848
  10.1 0.8 %copy-done.16 = f32[128,128]{1,0:T(8,128)S(1)} copy-done((f32[128,128]{1,0:T(8,128)S(1)}, f32[128,128]{1,0:T(8,128)}, u32[]{:S(2)}) %copy-start.16) | copy-done | bytes 65560
  11.0 0.8 %copy-done.17 = f32[128,128]{1,0:T(8,128)S(1)} copy-done((f32[128,128]{1,0:T(8,128)S(1)}, f32[128,128]{1,0:T(8,128)}, u32[]{:S(2)}) %copy-start.17) | copy-done | bytes 65560
  11.8 0.8 %copy-done.18 = f32[128,128]{1,0:T(8,128)S(1)} copy-done((f32[128,128]{1,0:T(8,128)S(1)}, f32[128,128]{1,0:T(8,128)}, u32[]{:S(2)}) %copy-start.18) | copy-done | bytes 65560
  12.7 0.8 %copy-done.19 = f32[128,128]{1,0:T(8,128)S(1)} copy-done((f32[128,128]{1,0:T(8,128)S(1)}, f32[128,128]{1,0:T(8,128)}, u32[]{:S(2)}) %copy-start.19) | copy-done | bytes 65560
  13.5 2.5 %pair_project.1 = (bf16[6,192,384]{2,1,0:T(8,128)(2,1)S(1)}, bf16[6,192,384]{2,1,0:T(8,128)(2,1)S(1)}, bf16[6,192,256]{2,1,0:T(8,128)(2,1)S(1)}, bf16[6,192,256]...) custom-call(f32[6,192,128]{2,1,0:T(8,128)S(1)} %copy-done, ...), custom_call_target="tpu_custom_call" | custom-call | flops 2000000000 | bytes 10000000 | tf_op jit(solution)/shard_map/pair_project/pallas_call | solution.py:738
  16.0 3.0 %collective-permute-done.1.p2_ref.y2_ref = f32[120,256]{1,0:T(8,128)S(1)} collective-permute-done((f32[120,256]{1,0:T(8,128)}, f32[120,256]{1,0:T(8,128)S(1)}, u32[]{:S(2)}, u32[]{:S(2)}) %collective-permute-start.1) | collective-permute-done | bytes 122912 | tf_op jit(solution)/shard_map/ppermute | solution.py:691
  19.1 1.6 %collective-permute-start.3 = (f32[216,128]{1,0:T(8,128)S(1)}, f32[216,128]{1,0:T(8,128)S(1)}, u32[]{:S(2)}, u32[]{:S(2)}) collective-permute-start(f32[216,128]{1,0:T(8,128)S(1)} %stack_rows.1.b0_ref), channel_id=1, source_target_pairs={{0,8},{4,12},{8,0},{12,4},{16,24},{20,28},{24,16},{28,20},{1,9},{5... | collective-permute-start | bytes 331784 | tf_op jit(solution)/shard_map/ppermute | solution.py:691
  20.7 1.5 %collective-permute-start.4 = (f32[216,128]{1,0:T(8,128)S(1)}, f32[216,128]{1,0:T(8,128)S(1)}, u32[]{:S(2)}, u32[]{:S(2)}) collective-permute-start(f32[216,128]{1,0:T(8,128)S(1)} %stack_rows.1.b0_ref), channel_id=1, source_target_pairs={{0,16},{4,20},{8,24},{12,28},{16,0},{20,4},{24,8},{28,12},{1,17},{... | collective-permute-start | bytes 331784 | tf_op jit(solution)/shard_map/ppermute | solution.py:691
  22.2 0.5 collective-permute-start.5
  22.7 1.8 %msa_project.1 = (f32[96,256]{1,0:T(8,128)S(1)}, f32[96,256]{1,0:T(8,128)S(1)}, f32[96,256]{1,0:T(8,128)S(1)}, f32[96,256]{1,0:T(8,128)S(1)}, f32[384,256]{1,0:T...) custom-call(f32[120,256]{1,0:T(8,128)S(1)} %copy-done.1, ...), custom_call_target="tpu_custom_call" | custom-call | flops 1000000000 | bytes 10000000 | tf_op jit(solution)/shard_map/msa_project/pallas_call | solution.py:771
  24.5 0.9 %collective-permute-done.4.b2_ref = f32[216,128]{1,0:T(8,128)S(1)} collective-permute-done((f32[216,128]{1,0:T(8,128)S(1)}, f32[216,128]{1,0:T(8,128)S(1)}, u32[]{:S(2)}, u32[]{:S(2)}) %collective-permute-start.4) | collective-permute-done | bytes 110624 | tf_op jit(solution)/shard_map/ppermute | solution.py:691
  25.4 2.4 %collective-permute-done.5.b3_ref = f32[216,128]{1,0:T(8,128)S(1)} collective-permute-done((f32[216,128]{1,0:T(8,128)S(1)}, f32[216,128]{1,0:T(8,128)S(1)}, u32[]{:S(2)}, u32[]{:S(2)}) %collective-permute-start.5) | collective-permute-done | bytes 110624 | tf_op jit(solution)/shard_map/ppermute | solution.py:691
  28.0 0.5 collective-permute-start.6
  28.5 1.3 %collective-permute-done.6.b2_ref = f32[216,128]{1,0:T(8,128)S(1)} collective-permute-done((f32[216,128]{1,0:T(8,128)S(1)}, f32[216,128]{1,0:T(8,128)S(1)}, u32[]{:S(2)}, u32[]{:S(2)}) %collective-permute-start.6) | collective-permute-done | bytes 110624 | tf_op jit(solution)/shard_map/ppermute | solution.py:691
  29.8 4.2 %msa_attention.1 = (f32[96,256]{1,0:T(8,128)S(1)}, f32[96,256]{1,0:T(8,128)S(1)}, f32[96,256]{1,0:T(8,128)S(1)}, f32[96,256]{1,0:T(8,128)S(1)}, f32[192,256]{1,0...) custom-call(f32[96,256]{1,0:T(8,128)S(1)} %get-tuple-element.56.after_ref.q_ref, ...), custom_call_target="tpu_custom_call" | custom-call | flops 4000000000 | bytes 10000000 | tf_op jit(solution)/shard_map/msa_attention/pallas_call | solution.py:797
  34.0 13.2 %pair_attention.1 = (f32[6,32,768]{2,1,0:T(8,128)S(1)}, f32[6,32,768]{2,1,0:T(8,128)S(1)}, f32[6,192,128]{2,1,0:T(8,128)S(1)}, f32[6,192,128]{2,1,0:T(8,128)S(1)...) custom-call(bf16[6,192,384]{2,1,0:T(8,128)(2,1)S(1)} %get-tuple-element.48.q_ref, ...), custom_call_target="tpu_custom_call" | custom-call | flops 10000000000 | bytes 10000000 | tf_op jit(solution)/shard_map/pair_attention/pallas_call | solution.py:817
  47.7 2.9 %collective-permute-start.13 = (f32[192,256]{1,0:T(8,128)S(1)}, f32[192,256]{1,0:T(8,128)S(1)}, u32[]{:S(2)}, u32[]{:S(2)}) collective-permute-start(f32[192,256]{1,0:T(8,128)S(1)} %get-tuple-element.78), channel_id=1, source_target_pairs={{0,2},{1,3},{2,0},{3,1},{4,6},{5,7},{6,4},{7,5},{8,10},{9,11},{10,... | collective-permute-start | bytes 589832 | tf_op jit(solution)/shard_map/ppermute | solution.py:691
  50.6 1.2 %pair_back.1.after_ref.dn_ref = f32[6,192,128]{2,1,0:T(8,128)S(1)} custom-call(f32[6,32,768]{2,1,0:T(8,128)S(1)} %get-tuple-element.62.ot_ref, f32[6,32,768]{2,1,0:T(8,128)S(1)} %get-tuple-element.63.dqt_ref, f32[6,192,128]{2,1,0:T(8,128)S(1)} %get-tuple-element.64.dk_ref, f32[6,192,128]{2,1,0:T(8,128)S(1)} %get-tuple-element.65.dv_ref, ...), custom_call_target="tpu_custom_call" | custom-call | flops 1000000000 | bytes 10000000 | tf_op jit(solution)/shard_map/pair_back/pallas_call | solution.py:845
  52.0 0.6 collective-permute-start.10
  52.6 0.6 collective-permute-start.11
  53.1 2.4 %collective-permute-start.12 = (f32[216,128]{1,0:T(8,128)S(1)}, f32[216,128]{1,0:T(8,128)S(1)}, u32[]{:S(2)}, u32[]{:S(2)}) collective-permute-start(f32[216,128]{1,0:T(8,128)S(1)} %get-tuple-element.76), channel_id=1, source_target_pairs={{0,24},{4,28},{8,16},{12,20},{16,8},{20,12},{24,0},{28,4},{1,25},{... | collective-permute-start | bytes 331784 | tf_op jit(solution)/shard_map/ppermute | solution.py:691
  55.9 4.1 %collective-permute-done.13.r23_ref = f32[192,256]{1,0:T(8,128)S(1)} collective-permute-done((f32[192,256]{1,0:T(8,128)S(1)}, f32[192,256]{1,0:T(8,128)S(1)}, u32[]{:S(2)}, u32[]{:S(2)}) %collective-permute-start.13) | collective-permute-done | bytes 196640 | tf_op jit(solution)/shard_map/ppermute | solution.py:691
  60.2 2.7 %collective-permute-start.15 = (f32[24,192]{1,0:T(8,128)S(1)}, f32[24,192]{1,0:T(8,128)S(1)}, u32[]{:S(2)}, u32[]{:S(2)}) collective-permute-start(f32[24,192]{1,0:T(8,128)S(1)} %get-tuple-element.86), channel_id=1, source_target_pairs={{0,2},{1,3},{2,0},{3,1},{4,6},{5,7},{6,4},{7,5},{8,10},{9,11},{10,... | collective-permute-start | bytes 55304 | tf_op jit(solution)/shard_map/ppermute | solution.py:691
  62.9 1.7 %collective-permute-start.16 = (f32[24,192]{1,0:T(8,128)S(1)}, f32[24,192]{1,0:T(8,128)S(1)}, u32[]{:S(2)}, u32[]{:S(2)}) collective-permute-start(f32[24,192]{1,0:T(8,128)S(1)} %get-tuple-element.87), channel_id=1, source_target_pairs={{0,3},{1,2},{2,1},{3,0},{4,7},{5,6},{6,5},{7,4},{8,11},{9,10},{10,... | collective-permute-start | bytes 55304 | tf_op jit(solution)/shard_map/ppermute | solution.py:691
  64.5 0.9 %collective-permute-done.14.p1_ref.r1_ref = f32[120,256]{1,0:T(8,128)S(1)} collective-permute-done((f32[120,256]{1,0:T(8,128)S(1)}, f32[120,256]{1,0:T(8,128)S(1)}, u32[]{:S(2)}, u32[]{:S(2)}) %collective-permute-start.14) | collective-permute-done | bytes 122912 | tf_op jit(solution)/shard_map/ppermute | solution.py:691
  65.5 0.9 %aligned_end.1 = f32[2,48,256]{2,1,0:T(8,128)} custom-call(f32[120,256]{1,0:T(8,128)S(1)} %copy-done.1, f32[1,256]{1,0:T(1,128)S(1)} %bitcast.14, f32[96,256]{1,0:T(8,128)S(1)} %aligned_back.1.after_ref.dy_ref, f32[192,256]{1,0:T(8,128)S(1)} %collective-permute-done.13.r23_ref, f32[120,256]{1,0:T(8,128)S(1)} %collective-permute-done.14.p1_ref.r1_ref), custom_call_target="tpu_custom_call" | custom-call | tf_op jit(solution)/shard_map/aligned_end/pallas_call | solution.py:880
  66.4 2.1 %collective-permute-done.16.p3_ref = f32[24,192]{1,0:T(8,128)S(1)} collective-permute-done((f32[24,192]{1,0:T(8,128)S(1)}, f32[24,192]{1,0:T(8,128)S(1)}, u32[]{:S(2)}, u32[]{:S(2)}) %collective-permute-start.16) | collective-permute-done | bytes 18464 | tf_op jit(solution)/shard_map/ppermute | solution.py:691
  68.5 1.4 %pair_end.1 = f32[6,192,128]{2,1,0:T(8,128)} custom-call(f32[6,192,128]{2,1,0:T(8,128)S(1)} %get-tuple-element.46.after_ref.n_ref, f32[6,192,128]{2,1,0:T(8,128)S(1)} %get-tuple-element.47.scale_ref, f32[6,192,128]{2,1,0:T(8,128)S(1)} %pair_back.1.after_ref.dn_ref, f32[24,192]{1,0:T(8,128)S(1)} %get-tuple-element.84.p0_ref, ...), custom_call_target="tpu_custom_call" | custom-call | tf_op jit(solution)/shard_map/pair_end/pallas_call | solution.py:886
  (55 shorter events, 1.5 us)
Async XLA Ops:
  0.6 8.4 %copy-start = (f32[6,192,128]{2,1,0:T(8,128)S(1)}, f32[6,192,128]{2,1,0:T(8,128)}, u32[]{:S(2)}) copy-start(f32[6,192,128]{2,1,0:T(8,128)} %x_ref.1) | copy-start | bytes 1769476
  0.6 8.4 %copy-start.3 = (f32[128,8]{0,1:T(8,128)S(1)}, f32[128,8]{0,1:T(8,128)}, u32[]{:S(2)}) copy-start(f32[128,8]{0,1:T(8,128)} %param.36) | copy-start | bytes 12292
  0.7 8.4 %copy-start.4 = (f32[128,4]{0,1:T(4,128)S(1)}, f32[128,4]{0,1:T(4,128)}, u32[]{:S(2)}) copy-start(f32[128,4]{0,1:T(4,128)} %param.28) | copy-start | bytes 6148
  0.7 8.4 %copy-start.15 = (f32[128,128]{1,0:T(8,128)S(1)}, f32[128,128]{1,0:T(8,128)}, u32[]{:S(2)}) copy-start(f32[128,128]{1,0:T(8,128)} %wq_hbm.2) | copy-start | bytes 196612
  3.3 5.7 %copy-start.5 = (f32[128]{0:T(128)S(1)}, f32[128]{0:T(128)}, u32[]{:S(2)}) copy-start(f32[128]{0:T(128)} %param.23) | copy-start | bytes 1540
  3.3 5.7 %copy-start.7 = (f32[128]{0:T(128)S(1)}, f32[128]{0:T(128)}, u32[]{:S(2)}) copy-start(f32[128]{0:T(128)} %param.31) | copy-start | bytes 1540
  3.3 15.7 %copy-start.1 = (f32[120,256]{1,0:T(8,128)S(1)}, f32[120,256]{1,0:T(8,128)}, u32[]{:S(2)}) copy-start(f32[120,256]{1,0:T(8,128)} %get-tuple-element.54.p0_ref.y0_ref.y_ref) | copy-start | bytes 368644
  3.3 15.6 %copy-start.2 = (f32[48,192]{1,0:T(8,128)S(1)}, f32[48,192]{1,0:T(8,128)}, u32[]{:S(2)}) copy-start(f32[48,192]{1,0:T(8,128)} %get-tuple-element.55.m_ref) | copy-start | bytes 110596
  3.3 12.6 %collective-permute-start = (f32[120,256]{1,0:T(8,128)}, f32[120,256]{1,0:T(8,128)S(1)}, u32[]{:S(2)}, u32[]{:S(2)}) collective-permute-start(f32[120,256]{1,0:T(8,128)} %get-tuple-element.54.p0_ref.y0_ref.y_ref), channel_id=1, source_target_pairs={{0,1},{1,0},{2,3},{3,2},{4,5},{5,4},{6,7},{7,6},{8,9},{9,8},{10,11... | collective-permute-start | bytes 368648 | tf_op jit(solution)/shard_map/ppermute | solution.py:691
  6.4 12.5 %collective-permute-start.1 = (f32[120,256]{1,0:T(8,128)}, f32[120,256]{1,0:T(8,128)S(1)}, u32[]{:S(2)}, u32[]{:S(2)}) collective-permute-start(f32[120,256]{1,0:T(8,128)} %get-tuple-element.54.p0_ref.y0_ref.y_ref), channel_id=1, source_target_pairs={{0,2},{1,3},{2,0},{3,1},{4,6},{5,7},{6,4},{7,5},{8,10},{9,11},{10,... | collective-permute-start | bytes 368648 | tf_op jit(solution)/shard_map/ppermute | solution.py:691
  9.0 10.0 %collective-permute-start.2 = (f32[120,256]{1,0:T(8,128)}, f32[120,256]{1,0:T(8,128)S(1)}, u32[]{:S(2)}, u32[]{:S(2)}) collective-permute-start(f32[120,256]{1,0:T(8,128)} %get-tuple-element.54.p0_ref.y0_ref.y_ref), channel_id=1, source_target_pairs={{0,3},{1,2},{2,1},{3,0},{4,7},{5,6},{6,5},{7,4},{8,11},{9,10},{10,... | collective-permute-start | bytes 368648 | tf_op jit(solution)/shard_map/ppermute | solution.py:691
  13.5 9.2 %copy-start.13 = (f32[256,256]{1,0:T(8,128)S(1)}, f32[256,256]{1,0:T(8,128)}, u32[]{:S(2)}) copy-start(f32[256,256]{1,0:T(8,128)} %wo_hbm.3) | copy-start | bytes 786436
  19.0 3.7 %copy-start.9 = (f32[256,256]{1,0:T(8,128)S(1)}, f32[256,256]{1,0:T(8,128)}, u32[]{:S(2)}) copy-start(f32[256,256]{1,0:T(8,128)} %wq_hbm.3) | copy-start | bytes 786436
  19.0 3.7 %copy-start.10 = (f32[256,256]{1,0:T(8,128)S(1)}, f32[256,256]{1,0:T(8,128)}, u32[]{:S(2)}) copy-start(f32[256,256]{1,0:T(8,128)} %wk_hbm.3) | copy-start | bytes 786436
  19.0 3.7 %copy-start.11 = (f32[256,256]{1,0:T(8,128)S(1)}, f32[256,256]{1,0:T(8,128)}, u32[]{:S(2)}) copy-start(f32[256,256]{1,0:T(8,128)} %wv_hbm.3) | copy-start | bytes 786436
  19.0 3.7 %copy-start.12 = (f32[256,256]{1,0:T(8,128)S(1)}, f32[256,256]{1,0:T(8,128)}, u32[]{:S(2)}) copy-start(f32[256,256]{1,0:T(8,128)} %wg_hbm.3) | copy-start | bytes 786436
  19.0 3.7 %copy-start.14 = (f32[2,48,256]{2,1,0:T(8,128)S(1)}, f32[2,48,256]{2,1,0:T(8,128)}, u32[]{:S(2)}) copy-start(f32[2,48,256]{2,1,0:T(8,128)} %adj_hbm.3) | copy-start | bytes 294916
  19.1 3.6 %copy-start.6 = (f32[256]{0:T(256)S(1)}, f32[256]{0:T(256)}, u32[]{:S(2)}) copy-start(f32[256]{0:T(256)} %param.30) | copy-start | bytes 3076
  19.1 5.4 %collective-permute-start.3 = (f32[216,128]{1,0:T(8,128)S(1)}, f32[216,128]{1,0:T(8,128)S(1)}, u32[]{:S(2)}, u32[]{:S(2)}) collective-permute-start(f32[216,128]{1,0:T(8,128)S(1)} %stack_rows.1.b0_ref), channel_id=1, source_target_pairs={{0,8},{4,12},{8,0},{12,4},{16,24},{20,28},{24,16},{28,20},{1,9},{5... | collective-permute-start | bytes 331784 | tf_op jit(solution)/shard_map/ppermute | solution.py:691
  20.7 4.7 %collective-permute-start.4 = (f32[216,128]{1,0:T(8,128)S(1)}, f32[216,128]{1,0:T(8,128)S(1)}, u32[]{:S(2)}, u32[]{:S(2)}) collective-permute-start(f32[216,128]{1,0:T(8,128)S(1)} %stack_rows.1.b0_ref), channel_id=1, source_target_pairs={{0,16},{4,20},{8,24},{12,28},{16,0},{20,4},{24,8},{28,12},{1,17},{... | collective-permute-start | bytes 331784 | tf_op jit(solution)/shard_map/ppermute | solution.py:691
  22.2 5.6 %collective-permute-start.5 = (f32[216,128]{1,0:T(8,128)S(1)}, f32[216,128]{1,0:T(8,128)S(1)}, u32[]{:S(2)}, u32[]{:S(2)}) collective-permute-start(f32[216,128]{1,0:T(8,128)S(1)} %stack_rows.1.b0_ref), channel_id=1, source_target_pairs={{0,24},{4,28},{8,16},{12,20},{16,8},{20,12},{24,0},{28,4},{1,25},{... | collective-permute-start | bytes 331784 | tf_op jit(solution)/shard_map/ppermute | solution.py:691
  27.9 1.9 %collective-permute-start.7 = (f32[3,216,128]{2,1,0:T(8,128)S(1)}, f32[3,216,128]{2,1,0:T(8,128)S(1)}, u32[]{:S(2)}, u32[]{:S(2)}) collective-permute-start(f32[3,216,128]{2,1,0:T(8,128)S(1)} %stack_chips.1.b1_ref), channel_id=1, source_target_pairs={{0,4},{4,0},{8,12},{12,8},{16,20},{20,16},{24,28},{28,24},{1,5},{5... | collective-permute-start | bytes 995336 | tf_op jit(solution)/shard_map/ppermute | solution.py:691
  28.0 1.8 %collective-permute-start.6 = (f32[216,128]{1,0:T(8,128)S(1)}, f32[216,128]{1,0:T(8,128)S(1)}, u32[]{:S(2)}, u32[]{:S(2)}) collective-permute-start(f32[216,128]{1,0:T(8,128)S(1)} %stack_rows.1.b0_ref), channel_id=1, source_target_pairs={{0,4},{4,0},{8,12},{12,8},{16,20},{20,16},{24,28},{28,24},{1,5},{5... | collective-permute-start | bytes 331784 | tf_op jit(solution)/shard_map/ppermute | solution.py:691
  47.2 4.7 %collective-permute-start.8 = (f32[4,4,24,192]{3,2,1,0:T(8,128)S(1)}, f32[4,4,24,192]{3,2,1,0:T(8,128)S(1)}, u32[]{:S(2)}, u32[]{:S(2)}) collective-permute-start(f32[4,4,24,192]{3,2,1,0:T(8,128)S(1)} %get-tuple-element.70), channel_id=1, source_target_pairs={{0,4},{4,0},{8,12},{12,8},{16,20},{20,16},{24,28},{28,24},{1,5},{5... | collective-permute-start | bytes 884744 | tf_op jit(solution)/shard_map/ppermute | solution.py:691
  47.4 4.5 %collective-permute-start.9 = (f32[4,48,192]{2,1,0:T(8,128)S(1)}, f32[4,48,192]{2,1,0:T(8,128)S(1)}, u32[]{:S(2)}, u32[]{:S(2)}) collective-permute-start(f32[4,48,192]{2,1,0:T(8,128)S(1)} %get-tuple-element.72), channel_id=1, source_target_pairs={{0,4},{4,0},{8,12},{12,8},{16,20},{20,16},{24,28},{28,24},{1,5},{5... | collective-permute-start | bytes 442376 | tf_op jit(solution)/shard_map/ppermute | solution.py:691
  47.7 12.3 %collective-permute-start.13 = (f32[192,256]{1,0:T(8,128)S(1)}, f32[192,256]{1,0:T(8,128)S(1)}, u32[]{:S(2)}, u32[]{:S(2)}) collective-permute-start(f32[192,256]{1,0:T(8,128)S(1)} %get-tuple-element.78), channel_id=1, source_target_pairs={{0,2},{1,3},{2,0},{3,1},{4,6},{5,7},{6,4},{7,5},{8,10},{9,11},{10,... | collective-permute-start | bytes 589832 | tf_op jit(solution)/shard_map/ppermute | solution.py:691
  52.0 8.0 %collective-permute-start.10 = (f32[216,128]{1,0:T(8,128)S(1)}, f32[216,128]{1,0:T(8,128)S(1)}, u32[]{:S(2)}, u32[]{:S(2)}) collective-permute-start(f32[216,128]{1,0:T(8,128)S(1)} %get-tuple-element.74), channel_id=1, source_target_pairs={{0,8},{4,12},{8,0},{12,4},{16,24},{20,28},{24,16},{28,20},{1,9},{5... | collective-permute-start | bytes 331784 | tf_op jit(solution)/shard_map/ppermute | solution.py:691
  52.6 7.4 %collective-permute-start.11 = (f32[216,128]{1,0:T(8,128)S(1)}, f32[216,128]{1,0:T(8,128)S(1)}, u32[]{:S(2)}, u32[]{:S(2)}) collective-permute-start(f32[216,128]{1,0:T(8,128)S(1)} %get-tuple-element.75), channel_id=1, source_target_pairs={{0,16},{4,20},{8,24},{12,28},{16,0},{20,4},{24,8},{28,12},{1,17},{... | collective-permute-start | bytes 331784 | tf_op jit(solution)/shard_map/ppermute | solution.py:691
  53.1 6.9 %collective-permute-start.12 = (f32[216,128]{1,0:T(8,128)S(1)}, f32[216,128]{1,0:T(8,128)S(1)}, u32[]{:S(2)}, u32[]{:S(2)}) collective-permute-start(f32[216,128]{1,0:T(8,128)S(1)} %get-tuple-element.76), channel_id=1, source_target_pairs={{0,24},{4,28},{8,16},{12,20},{16,8},{20,12},{24,0},{28,4},{1,25},{... | collective-permute-start | bytes 331784 | tf_op jit(solution)/shard_map/ppermute | solution.py:691
  60.1 5.3 %collective-permute-start.14 = (f32[120,256]{1,0:T(8,128)S(1)}, f32[120,256]{1,0:T(8,128)S(1)}, u32[]{:S(2)}, u32[]{:S(2)}) collective-permute-start(f32[120,256]{1,0:T(8,128)S(1)} %get-tuple-element.85), channel_id=1, source_target_pairs={{0,1},{1,0},{2,3},{3,2},{4,5},{5,4},{6,7},{7,6},{8,9},{9,8},{10,11... | collective-permute-start | bytes 368648 | tf_op jit(solution)/shard_map/ppermute | solution.py:691
  60.2 6.2 %collective-permute-start.15 = (f32[24,192]{1,0:T(8,128)S(1)}, f32[24,192]{1,0:T(8,128)S(1)}, u32[]{:S(2)}, u32[]{:S(2)}) collective-permute-start(f32[24,192]{1,0:T(8,128)S(1)} %get-tuple-element.86), channel_id=1, source_target_pairs={{0,2},{1,3},{2,0},{3,1},{4,6},{5,7},{6,4},{7,5},{8,10},{9,11},{10,... | collective-permute-start | bytes 55304 | tf_op jit(solution)/shard_map/ppermute | solution.py:691
  62.9 5.6 %collective-permute-start.16 = (f32[24,192]{1,0:T(8,128)S(1)}, f32[24,192]{1,0:T(8,128)S(1)}, u32[]{:S(2)}, u32[]{:S(2)}) collective-permute-start(f32[24,192]{1,0:T(8,128)S(1)} %get-tuple-element.87), channel_id=1, source_target_pairs={{0,3},{1,2},{2,1},{3,0},{4,7},{5,6},{6,5},{7,4},{8,11},{9,10},{10,... | collective-permute-start | bytes 55304 | tf_op jit(solution)/shard_map/ppermute | solution.py:691
  (5 other events, 4.4 us)

commit v4 on v3

--- a/solution.py
+++ b/solution.py
@@ -245,14 +245,27 @@
     return jnp.where((lane // HEAD) == h, 1.0, 0.0).astype(dtype)
 
 
-def fetch(pairs, sem):
-    copies = [pltpu.make_async_copy(a, b, sem.at[t]) for t, (a, b) in enumerate(pairs)]
-    for copy in copies:
-        copy.start()
-    return copies
-
-
-def bias_kernel(rows, x_ref, y_ref, g_ref, wp_ref, g2_ref, wm_ref, joint_ref, bm_ref):
+def pack(block_of, count, lines, out_ref):
+    half = count // 2
+    for t in range(half):
+        first, second = block_of(t), block_of(t + half)
+        out_ref[t * lines : (t + 1) * lines] = first[:, :LANES]
+        out_ref[(t + half) * lines : (t + half + 1) * lines] = second[:, :LANES]
+        rest = cat([first[:, LANES:], second[:, LANES:]], 1)
+        out_ref[(t + count) * lines : (t + count + 1) * lines] = rest
+
+
+def unpack(dense, count, lines):
+    half = count // 2
+    blocks = []
+    for t in range(count):
+        rest = dense[(count + t % half) * lines : (count + t % half + 1) * lines]
+        rest = rest[:, : LANES // 2] if t < half else rest[:, LANES // 2 :]
+        blocks.append(cat([dense[t * lines : (t + 1) * lines], rest], 1))
+    return blocks
+
+
+def bias_kernel(rows, x_ref, y_ref, g_ref, wp_ref, g2_ref, wm_ref, joint_ref, packed_ref, bm_ref):
     length = x_ref.shape[1]
     base, wide = y_ref.shape
     joint_ref[:base] = y_ref[...]
@@ -269,24 +282,16 @@
             joint_ref[at : at + 1, :length] = res[h : h + 1]
         for h in range(hm):
             bm_ref[h * rows + j : h * rows + j + 1, :] = res[hp + h : hp + h + 1]
+    lines = hp * rows
+    pack(lambda t: bm_ref[t * lines : (t + 1) * lines], hm // hp, lines, packed_ref)
 
 
 def pair_project_kernel(
-    x_hbm, adj_hbm, g_ref, wq_hbm, wk_hbm, wv_hbm, wg_hbm, wo_hbm, wp_ref, g2_ref, wm_ref,
+    x_ref, adj_ref, g_ref, wq_ref, wk_ref, wv_ref, wg_ref, wo_ref, wp_ref, g2_ref, wm_ref,
     q_ref, k_ref, v_ref, m_ref, kt_ref, vt_ref, dout_ref, sig_ref, n_ref, scale_ref, wj_ref, wb_ref,
-    x_ref, adj_ref, wq_ref, wk_ref, wv_ref, wg_ref, wo_ref, sem,
 ):
     rows, length, feats = x_ref.shape
     g = g_ref[...]
-    copies = fetch(
-        [
-            (wq_hbm, wq_ref), (wk_hbm, wk_ref), (wv_hbm, wv_ref), (wg_hbm, wg_ref),
-            (wo_hbm, wo_ref), (x_hbm, x_ref), (adj_hbm, adj_ref),
-        ],
-        sem,
-    )
-    for copy in copies:
-        copy.wait()
     top, low = split2(cat([wq_ref[...], wk_ref[...], wv_ref[...], wg_ref[...]], 1))
     wb_ref[0] = top
     wb_ref[1] = low
@@ -322,26 +327,6 @@
         wj_ref[:, j * feats : (j + 1) * feats] = cat(right3(split2(mine)), 0)
 
 
-def pack(block_of, count, lines, out_ref):
-    half = count // 2
-    for t in range(half):
-        first, second = block_of(t), block_of(t + half)
-        out_ref[t * lines : (t + 1) * lines] = first[:, :LANES]
-        out_ref[(t + half) * lines : (t + half + 1) * lines] = second[:, :LANES]
-        rest = cat([first[:, LANES:], second[:, LANES:]], 1)
-        out_ref[(t + count) * lines : (t + count + 1) * lines] = rest
-
-
-def unpack(dense, count, lines):
-    half = count // 2
-    blocks = []
-    for t in range(count):
-        rest = dense[(count + t % half) * lines : (count + t % half + 1) * lines]
-        rest = rest[:, : LANES // 2] if t < half else rest[:, LANES // 2 :]
-        blocks.append(cat([dense[t * lines : (t + 1) * lines], rest], 1))
-    return blocks
-
-
 def gather_chips(natural, refs, core, chip):
     _, count, lines, _ = natural.shape
     for (own_ref, others_ref), side in zip((refs[:2], refs[2:]), (core, 1 - core)):
@@ -450,7 +435,7 @@
 
 def pair_back_kernel(
     ot_ref, dqt_ref, dk_ref, dv_ref, dout_ref, sig_ref,
-    g_ref, wb_ref, dn_ref,
+    g_ref, wb_ref, after1_ref, after2_ref, dn_ref,
 ):
     rows, length, feats = dk_ref.shape
     g = g_ref[...]
@@ -469,22 +454,15 @@
 
 
 def msa_project_kernel(
-    y0_ref, y1_ref, y2_ref, y3_ref, adj_hbm,
-    g_ref, wq_hbm, wk_hbm, wv_hbm, wg_hbm, wo_hbm,
+    y0_ref, y1_ref, y2_ref, y3_ref, adj_ref,
+    g_ref, wq_ref, wk_ref, wv_ref, wg_ref, wo_ref,
     q_ref, m_ref, dout_ref, sig_ref, k_ref, v_ref, wkv_ref, wqg_ref,
-    yall, adj_ref, wq_ref, wk_ref, wv_ref, wg_ref, wo_ref, sem,
+    yall,
 ):
     res = lax.axis_index("res")
     n_seqs, own, feats = adj_ref.shape
     n_keys = yall.shape[1]
     g = g_ref[...]
-    copies = fetch(
-        [
-            (wk_hbm, wk_ref), (wv_hbm, wv_ref), (wq_hbm, wq_ref), (wg_hbm, wg_ref),
-            (wo_hbm, wo_ref), (adj_hbm, adj_ref),
-        ],
-        sem,
-    )
     for t, ref in enumerate((y0_ref, y1_ref, y2_ref, y3_ref)):
         at = pl.multiple_of(lax.bitwise_xor(res, t) * own, own)
         for b in range(n_seqs):
@@ -492,8 +470,6 @@
     n_own, _ = normed(y0_ref[: n_seqs * own])
     n_all, _ = normed(yall[...].reshape(n_seqs * n_keys, feats))
     own_parts, all_parts = split3(n_own * g), split3(n_all * g)
-    for copy in copies:
-        copy.wait()
     for ref, pair in ((wkv_ref, (wk_ref, wv_ref)), (wqg_ref, (wq_ref, wg_ref))):
         top, low = split2(cat([pair[0][...], pair[1][...]], 1))
         ref[0] = top
@@ -530,7 +506,7 @@
     blocks = (b0_ref, b1_ref, b2_ref, b3_ref)
     gather_chips(natural, blocks, core, chip)
     for s in range(seq_n):
-        block = cat([natural[s, res_n], natural[s, res_n + 1]], 0)
+        block = cat([natural[s, 0], natural[s, 1]], 0)
         for h in range(heads):
             at = h * own + s * rows
             bias[at : at + rows, :] = block[h * rows : (h + 1) * rows]
@@ -615,10 +591,8 @@
         out_ref[b] = normed_back(n, scale, g * (dy_ref[at] + r23_ref[at] + r1_ref[at]))
 
 
-def stack_kernel(length, p0_ref, p1_ref, p2_ref, p3_ref, m_ref, after_ref, out_ref):
-    lines = m_ref.shape[0] // 2
+def stack_kernel(length, lines, p0_ref, p1_ref, p2_ref, p3_ref, after_ref, out_ref):
     blocks = [ref[ref.shape[0] - lines :, :length] for ref in (p0_ref, p1_ref, p2_ref, p3_ref)]
-    blocks += [m_ref[:lines], m_ref[lines:]]
     pack(lambda t: blocks[t], len(blocks), lines, out_ref)
 
 
@@ -677,10 +651,6 @@
 
 def params(mib, **more):
     return pltpu.CompilerParams(vmem_limit_bytes=mib * MIB, **more)
-
-
-def hbm(count):
-    return [pl.BlockSpec(memory_space=pltpu.HBM)] * count
 
 
 def vmem(count):
@@ -724,22 +694,36 @@
     gain2 = coupled_scaler_for_offset.reshape(1, feats)
 
     lines, base = hp * rows, n_seqs * own
+    after = [pl.BlockSpec(memory_space=pl.ANY)]
+    packed = lambda count: (3 * count * lines // 2, LANES)
+    spread = lambda count: pltpu.VMEM((seq_n, count, lines, length), F32)
     mixed_rows, msa_rows = pl.pallas_call(
         functools.partial(bias_kernel, rows),
-        out_shape=(shape(base + lines, wide), shape(hm * rows, length)),
+        out_shape=(shape(base + lines, wide), shape(*packed(2))),
+        scratch_shapes=[pltpu.VMEM((hm * rows, length), F32)],
         compiler_params=params(63),
         name="bias_rows",
     )(
         coupled_embedding, aligned_embedding.reshape(base, wide), gain, wp_t, gain2, wm_t
     )
+
+    def over_chips(first, *behind):
+        return pl.pallas_call(
+            chip_stack_kernel,
+            in_specs=vmem(3) + after * len(behind),
+            out_shape=shape(chips - 1, *first.shape),
+            compiler_params=params(16),
+            name="stack_chips",
+        )(*[swap(first, "seq", seq_n, 2 * t) for t in range(1, chips)], *behind)
+
+    def over_cores(first, rest):
+        return [first, rest, swap(first, "seq", seq_n, 1), swap(rest, "seq", seq_n, 1)]
+
     columns = [mixed_rows] + [swap(mixed_rows, "res", res_n, t) for t in range(1, res_n)]
 
     bf = lambda *s: jax.ShapeDtypeStruct(s, BF16)
     q, k, v, m, kt, vt, d_out, sig, n, scale, wj, wb = pl.pallas_call(
         pair_project_kernel,
-        in_specs=hbm(2) + vmem(1) + hbm(5) + vmem(3),
-        scratch_shapes=[pltpu.VMEM((rows, length, feats), F32)] * 2
-        + [pltpu.VMEM((feats, feats), F32)] * 5 + [pltpu.SemaphoreType.DMA((7,))],
         out_shape=(
             bf(rows, length, 3 * feats), bf(rows, length, 3 * feats),
             bf(rows, length, 2 * feats), bf(rows, length, 2 * feats),
@@ -755,26 +739,23 @@
         coupled_result_matrix, wp_t, gain2, wm_t,
     )
 
-    joint = (3 * (res_n + 2) * lines // 2, LANES)
-    spread = pltpu.VMEM((seq_n, res_n + 2, lines, length), F32)
-    after = [pl.BlockSpec(memory_space=pl.ANY)]
+    msa_rest = over_chips(msa_rows, n)
+    msa_blocks = over_cores(msa_rows, msa_rest)
+    joint = packed(res_n + 2)
     first = pl.pallas_call(
-        functools.partial(stack_kernel, length),
-        in_specs=vmem(5) + after,
-        out_shape=shape(*joint),
+        functools.partial(stack_kernel, length, lines),
+        in_specs=vmem(4) + after,
+        out_shape=shape(*packed(res_n)),
         compiler_params=params(16),
         name="stack_rows",
-    )(*columns, msa_rows, n)
+    )(*columns, msa_rest)
 
     wide_gain = aligned_scaler.reshape(1, wide)
     flat = lambda count: shape(n_seqs * count, wide)
     mq, mm, m_out, m_sig, mk, mv, wkv, wqg = pl.pallas_call(
         msa_project_kernel,
-        in_specs=vmem(4) + hbm(1) + vmem(1) + hbm(5),
         out_shape=(flat(own),) * 4 + (flat(length),) * 2 + (bf(2, wide, 2 * wide),) * 2,
-        scratch_shapes=[
-            pltpu.VMEM((n_seqs, length, wide), F32), pltpu.VMEM((n_seqs, own, wide), F32),
-        ] + [pltpu.VMEM((wide, wide), F32)] * 5 + [pltpu.SemaphoreType.DMA((6,))],
+        scratch_shapes=[pltpu.VMEM((n_seqs, length, wide), F32)],
         compiler_params=params(32),
         name="msa_project",
         cost_estimate=pl.CostEstimate(flops=10**9, bytes_accessed=10**7, transcendentals=0),
@@ -784,15 +765,6 @@
         aligned_result_matrix,
     )
 
-    rest = pl.pallas_call(
-        chip_stack_kernel,
-        in_specs=vmem(3) + after,
-        out_shape=shape(chips - 1, *joint),
-        compiler_params=params(16),
-        name="stack_chips",
-    )(*[swap(first, "seq", seq_n, 2 * t) for t in range(1, chips)], mq)
-    blocks = [first, rest, swap(first, "seq", seq_n, 1), swap(rest, "seq", seq_n, 1)]
-
     stretch = pltpu.VMEM((hm * own, length), F32)
     o, dq, kept, r1, r23, msa_near, msa_far = pl.pallas_call(
         functools.partial(msa_kernel, (rows, hm, seq_n, res_n)),
@@ -800,16 +772,18 @@
         + (shape(chips, hm * rows, length),) * 2,
         scratch_shapes=[
             stretch, stretch, pltpu.VMEM((n_seqs, length, wide), F32),
-            spread,
+            spread(hm // hp),
         ],
         compiler_params=params(32),
         name="msa_attention",
         cost_estimate=pl.CostEstimate(flops=4 * 10**9, bytes_accessed=10**7, transcendentals=0),
     )(
-        mq, mm, mk, mv, *blocks, wkv,
+        mq, mm, mk, mv, *msa_blocks, wkv,
     )
     far_msa = swap(msa_far, "seq", seq_n, 1)
     r23 = swap(r23, "res", res_n, 2)
+
+    blocks = over_cores(first, over_chips(first, kept))
 
     piece = lambda *s: pl.BlockSpec((1,) + s, lambda i: (i, 0, 0))
     whole = lambda *s: pl.BlockSpec(s, lambda i: (0,) * len(s))
@@ -821,7 +795,7 @@
             piece(length, 3 * feats), piece(length, 3 * feats),
             piece(length, 2 * feats), piece(length, 2 * feats),
             piece(2 * feats, length), piece(2 * feats, length),
-        ] + [whole(*joint), whole(chips - 1, *joint)] * 2 + after,
+        ] + [whole(*packed(res_n)), whole(chips - 1, *packed(res_n))] * 2 + after,
         out_specs=(
             piece(HEAD, hp * length), piece(HEAD, hp * length),
             piece(length, feats), piece(length, feats), whole(*quarter), whole(*quarter),
@@ -835,7 +809,7 @@
             pltpu.VMEM((length, hp * length), F32),
             pltpu.VMEM((length, hp * length), F32),
             pltpu.VMEM((hp * length, length), F32),
-            spread,
+            spread(res_n),
         ],
         compiler_params=params(32),
         name="pair_attention",
@@ -844,12 +818,13 @@
     far_pair = swap(far, "seq", seq_n, 1)
     dn = pl.pallas_call(
         pair_back_kernel,
+        in_specs=vmem(8) + after * 2,
         out_shape=shape(rows, length, feats),
         compiler_params=params(32),
         name="pair_back",
-        cost_estimate=pl.CostEstimate(flops=10**9, bytes_accessed=10**7, transcendentals=0),
+        cost_estimate=pl.CostEstimate(flops=10**11, bytes_accessed=10**8, transcendentals=0),
     )(
-        ot, dqt, dk, dv, d_out, sig, gain, wb,
+        ot, dqt, dk, dv, d_out, sig, gain, wb, r23, far_msa,
     )
     sums = pl.pallas_call(
         core_sum_kernel,

time: 70.3 us -> 67.2 us (0.956)
  waiting for transfers between devices: 14.8 us -> 11.3 us
  starting transfers between devices: 21.2 us -> 22.7 us
  Pallas kernels: 28.6 us -> 27.4 us
    ppermute x17 -> x22, waiting for transfers between devices: 14.8 us -> 11.3 us  [swap(): return lax.ppermute(values, axis, [(i, i ^ offset) for i in range(size)])]
    ppermute x17 -> x22, starting transfers between devices: 21.2 us -> 22.7 us  [swap(): return lax.ppermute(values, axis, [(i, i ^ offset) for i in range(size)])]
    pallas_call x5 -> x6, Pallas kernels: 5.59 us -> 4.36 us  [the longest x1 1.65 us: fused_on_device(): pl.pallas_call(pair_project_kernel, out_shape=(bf(rows, length, 3 * feats...]
  transfers between devices with their start and end apart: 17 -> 22, of which waited for: 7 -> 8; matrix products, arithmetic and copies ran while one was open for 0% -> 0% of each run, Pallas kernels for 10% -> 35%
where the time goes in v4:
time: 67.2 us; the launch traced here: 66.8 us
  Pallas kernels  27.4 us (41%)
  starting transfers between devices  22.7 us (34%)
  waiting for transfers between devices  11.3 us (17%)
  local copies, waits for them, and re-layouts  4.49 us (7%)
  between operations  0.93 us (1%)
    ppermute x22, starting transfers between devices, swap(): return lax.ppermute(values, axis, [(i, i ^ offset) for i in range(size)])  22.7 us
    pallas_call x1, Pallas kernels, fused_on_device(): pl.pallas_call(functools.partial(pair_kernel, (rows, hp, seq_n, res_n)),...  13.3 us
    ppermute x22, waiting for transfers between devices, swap(): return lax.ppermute(values, axis, [(i, i ^ offset) for i in range(size)])  11.3 us
    unnamed x40, local copies, waits for them, and re-layouts  4.49 us
    pallas_call x1, Pallas kernels, fused_on_device(): pl.pallas_call(functools.partial(msa_kernel, (rows, hm, seq_n, res_n)), o...  4.17 us
    pallas_call x1, Pallas kernels, fused_on_device(): pl.pallas_call(functools.partial(bias_kernel, rows), out_shape=(shape(bas...  2.68 us
    pallas_call x1, Pallas kernels, fused_on_device(): pl.pallas_call(pair_project_kernel, out_shape=(bf(rows, length, 3 * feats...  1.65 us
    pallas_call x1, Pallas kernels, fused_on_device(): pl.pallas_call(pair_end_kernel, out_shape=shape(rows, length, feats), com...  1.44 us
  transfers between devices with their start and end apart: 22, of which 8 were waited for; matrix products, arithmetic and copies ran while one was open for 0% of the time, Pallas kernels for 35%

profile of v4, /device:TPU:0, one launch (start us, length us, event | category | flops | bytes accessed | tf_op | source)
XLA Modules:
  0.0 66.8 jit_solution(17171722757631827902)
XLA Ops:
  0.7 2.7 %bias_rows.1 = (f32[120,256]{1,0:T(8,128)}, f32[72,128]{1,0:T(8,128)}) custom-call(f32[6,192,128]{2,1,0:T(8,128)} %x_ref.3, f32[96,256]{1,0:T(8,128)} %bitcast.17, f32[1,128]{1,0:T(1,128)} %bitcast.14, f32[4,128]{1,0:T(4,128)} %bitcast.8, f32[1,128]{1,0:T(1,128)} %bitcast.12, f32[8,128]{1,0:T(8,128)} %bitcast.6), custom_call_target="tpu_custom_call" | custom-call | tf_op jit(solution)/shard_map/bias_rows/pallas_call | solution.py:700
  3.4 4.0 %collective-permute-start.5 = (f32[72,128]{1,0:T(8,128)}, f32[72,128]{1,0:T(8,128)S(1)}, u32[]{:S(2)}, u32[]{:S(2)}) collective-permute-start(f32[72,128]{1,0:T(8,128)} %get-tuple-element.55.b0_ref), channel_id=1, source_target_pairs={{0,24},{4,28},{8,16},{12,20},{16,8},{20,12},{24,0},{28,4},{1,25},{... | collective-permute-start | bytes 110600 | tf_op jit(solution)/shard_map/ppermute | solution.py:661
  7.3 0.5 collective-permute-start.4
  8.0 4.0 %collective-permute-start.2 = (f32[120,256]{1,0:T(8,128)}, f32[120,256]{1,0:T(8,128)S(1)}, u32[]{:S(2)}, u32[]{:S(2)}) collective-permute-start(f32[120,256]{1,0:T(8,128)} %get-tuple-element.54.p0_ref.y0_ref.y_ref), channel_id=1, source_target_pairs={{0,3},{1,2},{2,1},{3,0},{4,7},{5,6},{6,5},{7,4},{8,11},{9,10},{10,... | collective-permute-start | bytes 368648 | tf_op jit(solution)/shard_map/ppermute | solution.py:661
  12.0 0.6 collective-permute-start
  12.6 1.1 %copy-done.7 = f32[6,192,128]{2,1,0:T(8,128)S(1)} copy-done((f32[6,192,128]{2,1,0:T(8,128)S(1)}, f32[6,192,128]{2,1,0:T(8,128)}, u32[]{:S(2)}) %copy-start.7) | copy-done | bytes 589848
  13.6 0.8 %copy-done.15 = f32[128,128]{1,0:T(8,128)S(1)} copy-done((f32[128,128]{1,0:T(8,128)S(1)}, f32[128,128]{1,0:T(8,128)}, u32[]{:S(2)}) %copy-start.15) | copy-done | bytes 65560
  14.5 0.8 %copy-done.16 = f32[128,128]{1,0:T(8,128)S(1)} copy-done((f32[128,128]{1,0:T(8,128)S(1)}, f32[128,128]{1,0:T(8,128)}, u32[]{:S(2)}) %copy-start.16) | copy-done | bytes 65560
  15.3 0.8 %copy-done.17 = f32[128,128]{1,0:T(8,128)S(1)} copy-done((f32[128,128]{1,0:T(8,128)S(1)}, f32[128,128]{1,0:T(8,128)}, u32[]{:S(2)}) %copy-start.17) | copy-done | bytes 65560
  16.2 0.8 %copy-done.18 = f32[128,128]{1,0:T(8,128)S(1)} copy-done((f32[128,128]{1,0:T(8,128)S(1)}, f32[128,128]{1,0:T(8,128)}, u32[]{:S(2)}) %copy-start.18) | copy-done | bytes 65560
  17.0 1.6 %pair_project.1 = (bf16[6,192,384]{2,1,0:T(8,128)(2,1)S(1)}, bf16[6,192,384]{2,1,0:T(8,128)(2,1)S(1)}, bf16[6,192,256]{2,1,0:T(8,128)(2,1)S(1)}, bf16[6,192,256]...) custom-call(f32[6,192,128]{2,1,0:T(8,128)S(1)} %copy-done, ...), custom_call_target="tpu_custom_call" | custom-call | flops 2000000000 | bytes 10000000 | tf_op jit(solution)/shard_map/pair_project/pallas_call | solution.py:725
  19.3 2.4 %collective-permute-done.1.p2_ref.y2_ref = f32[120,256]{1,0:T(8,128)S(1)} collective-permute-done((f32[120,256]{1,0:T(8,128)}, f32[120,256]{1,0:T(8,128)S(1)}, u32[]{:S(2)}, u32[]{:S(2)}) %collective-permute-start.1) | collective-permute-done | bytes 122912 | tf_op jit(solution)/shard_map/ppermute | solution.py:661
  21.8 2.5 %collective-permute-start.8 = (f32[144,128]{1,0:T(8,128)S(1)}, f32[144,128]{1,0:T(8,128)S(1)}, u32[]{:S(2)}, u32[]{:S(2)}) collective-permute-start(f32[144,128]{1,0:T(8,128)S(1)} %stack_rows.1.b0_ref), channel_id=1, source_target_pairs={{0,24},{4,28},{8,16},{12,20},{16,8},{20,12},{24,0},{28,4},{1,25},{... | collective-permute-start | bytes 221192 | tf_op jit(solution)/shard_map/ppermute | solution.py:661
  24.3 0.5 collective-permute-start.7
  24.8 0.5 collective-permute-start.6
  25.4 1.3 %msa_project.1 = (f32[96,256]{1,0:T(8,128)S(1)}, f32[96,256]{1,0:T(8,128)S(1)}, f32[96,256]{1,0:T(8,128)S(1)}, f32[96,256]{1,0:T(8,128)S(1)}, f32[384,256]{1,0:T...) custom-call(f32[120,256]{1,0:T(8,128)S(1)} %copy-done.1, ...), custom_call_target="tpu_custom_call" | custom-call | flops 1000000000 | bytes 10000000 | tf_op jit(solution)/shard_map/msa_project/pallas_call | solution.py:755
  26.7 4.2 %msa_attention.1 = (f32[96,256]{1,0:T(8,128)S(1)}, f32[96,256]{1,0:T(8,128)S(1)}, f32[96,256]{1,0:T(8,128)S(1)}, f32[96,256]{1,0:T(8,128)S(1)}, f32[192,256]{1,0...) custom-call(f32[96,256]{1,0:T(8,128)S(1)} %get-tuple-element.56.q_ref, ...), custom_call_target="tpu_custom_call" | custom-call | flops 4000000000 | bytes 10000000 | tf_op jit(solution)/shard_map/msa_attention/pallas_call | solution.py:769
  31.8 0.8 %collective-permute-done.11.b2_ref = f32[144,128]{1,0:T(8,128)S(1)} collective-permute-done((f32[144,128]{1,0:T(8,128)S(1)}, f32[144,128]{1,0:T(8,128)S(1)}, u32[]{:S(2)}, u32[]{:S(2)}) %collective-permute-start.11) | collective-permute-done | bytes 73760 | tf_op jit(solution)/shard_map/ppermute | solution.py:661
  32.6 13.3 %pair_attention.1 = (f32[6,32,768]{2,1,0:T(8,128)S(1)}, f32[6,32,768]{2,1,0:T(8,128)S(1)}, f32[6,192,128]{2,1,0:T(8,128)S(1)}, f32[6,192,128]{2,1,0:T(8,128)S(1)...) custom-call(bf16[6,192,384]{2,1,0:T(8,128)(2,1)S(1)} %get-tuple-element.48.q_ref, ...), custom_call_target="tpu_custom_call" | custom-call | flops 10000000000 | bytes 10000000 | tf_op jit(solution)/shard_map/pair_attention/pallas_call | solution.py:791
  46.1 1.3 %pair_back.1.after_ref.dn_ref = f32[6,192,128]{2,1,0:T(8,128)S(1)} custom-call(f32[6,32,768]{2,1,0:T(8,128)S(1)} %get-tuple-element.62.ot_ref, f32[6,32,768]{2,1,0:T(8,128)S(1)} %get-tuple-element.63.dqt_ref, f32[6,192,128]{2,1,0:T(8,128)S(1)} %get-tuple-element.64.dk_ref, f32[6,192,128]{2,1,0:T(8,128)S(1)} %get-tuple-element.65.dv_ref, ...), custom_call_target="tpu_custom_call" | custom-call | flops 99999997952 | bytes 100000000 | tf_op jit(solution)/shard_map/pair_back/pallas_call | solution.py:819
  47.7 1.6 %collective-permute-start.16 = (f32[216,128]{1,0:T(8,128)S(1)}, f32[216,128]{1,0:T(8,128)S(1)}, u32[]{:S(2)}, u32[]{:S(2)}) collective-permute-start(f32[216,128]{1,0:T(8,128)S(1)} %get-tuple-element.75), channel_id=1, source_target_pairs={{0,8},{4,12},{8,0},{12,4},{16,24},{20,28},{24,16},{28,20},{1,9},{5... | collective-permute-start | bytes 331784 | tf_op jit(solution)/shard_map/ppermute | solution.py:661
  49.3 1.5 %collective-permute-start.17 = (f32[216,128]{1,0:T(8,128)S(1)}, f32[216,128]{1,0:T(8,128)S(1)}, u32[]{:S(2)}, u32[]{:S(2)}) collective-permute-start(f32[216,128]{1,0:T(8,128)S(1)} %get-tuple-element.76), channel_id=1, source_target_pairs={{0,16},{4,20},{8,24},{12,28},{16,0},{20,4},{24,8},{28,12},{1,17},{... | collective-permute-start | bytes 331784 | tf_op jit(solution)/shard_map/ppermute | solution.py:661
  51.7 1.3 %collective-permute-done.16.s1_ref = f32[216,128]{1,0:T(8,128)S(1)} collective-permute-done((f32[216,128]{1,0:T(8,128)S(1)}, f32[216,128]{1,0:T(8,128)S(1)}, u32[]{:S(2)}, u32[]{:S(2)}) %collective-permute-start.16) | collective-permute-done | bytes 110624 | tf_op jit(solution)/shard_map/ppermute | solution.py:661
  53.0 3.6 %collective-permute-done.17.s2_ref = f32[216,128]{1,0:T(8,128)S(1)} collective-permute-done((f32[216,128]{1,0:T(8,128)S(1)}, f32[216,128]{1,0:T(8,128)S(1)}, u32[]{:S(2)}, u32[]{:S(2)}) %collective-permute-start.17) | collective-permute-done | bytes 110624 | tf_op jit(solution)/shard_map/ppermute | solution.py:661
  56.7 2.3 %collective-permute-start.19 = (f32[120,256]{1,0:T(8,128)S(1)}, f32[120,256]{1,0:T(8,128)S(1)}, u32[]{:S(2)}, u32[]{:S(2)}) collective-permute-start(f32[120,256]{1,0:T(8,128)S(1)} %get-tuple-element.85), channel_id=1, source_target_pairs={{0,1},{1,0},{2,3},{3,2},{4,5},{5,4},{6,7},{7,6},{8,9},{9,8},{10,11... | collective-permute-start | bytes 368648 | tf_op jit(solution)/shard_map/ppermute | solution.py:661
  59.0 0.8 %collective-permute-start.20 = (f32[24,192]{1,0:T(8,128)S(1)}, f32[24,192]{1,0:T(8,128)S(1)}, u32[]{:S(2)}, u32[]{:S(2)}) collective-permute-start(f32[24,192]{1,0:T(8,128)S(1)} %get-tuple-element.86), channel_id=1, source_target_pairs={{0,2},{1,3},{2,0},{3,1},{4,6},{5,7},{6,4},{7,5},{8,10},{9,11},{10,... | collective-permute-start | bytes 55304 | tf_op jit(solution)/shard_map/ppermute | solution.py:661
  59.8 1.7 %collective-permute-start.21 = (f32[24,192]{1,0:T(8,128)S(1)}, f32[24,192]{1,0:T(8,128)S(1)}, u32[]{:S(2)}, u32[]{:S(2)}) collective-permute-start(f32[24,192]{1,0:T(8,128)S(1)} %get-tuple-element.87), channel_id=1, source_target_pairs={{0,3},{1,2},{2,1},{3,0},{4,7},{5,6},{6,5},{7,4},{8,11},{9,10},{10,... | collective-permute-start | bytes 55304 | tf_op jit(solution)/shard_map/ppermute | solution.py:661
  61.4 0.7 %collective-permute-done.19.p1_ref.r1_ref = f32[120,256]{1,0:T(8,128)S(1)} collective-permute-done((f32[120,256]{1,0:T(8,128)S(1)}, f32[120,256]{1,0:T(8,128)S(1)}, u32[]{:S(2)}, u32[]{:S(2)}) %collective-permute-start.19) | collective-permute-done | bytes 122912 | tf_op jit(solution)/shard_map/ppermute | solution.py:661
  62.1 0.9 %aligned_end.1 = f32[2,48,256]{2,1,0:T(8,128)} custom-call(f32[120,256]{1,0:T(8,128)S(1)} %copy-done.1, f32[1,256]{1,0:T(1,128)S(1)} %bitcast.11, f32[96,256]{1,0:T(8,128)S(1)} %aligned_back.1.after_ref.dy_ref, f32[192,256]{1,0:T(8,128)S(1)} %collective-permute-done.13.after1_ref.r23_ref, f32[120,256]{1,0:T(8,128)S(1)} %collective-permute-done.19.p1_ref.r1_ref), custom_call_target="tpu_custom_call" | custom-call | tf_op jit(solution)/shard_map/aligned_end/pallas_call | solution.py:855
  63.0 0.9 %collective-permute-done.20.p2_ref = f32[24,192]{1,0:T(8,128)S(1)} collective-permute-done((f32[24,192]{1,0:T(8,128)S(1)}, f32[24,192]{1,0:T(8,128)S(1)}, u32[]{:S(2)}, u32[]{:S(2)}) %collective-permute-start.20) | collective-permute-done | bytes 18464 | tf_op jit(solution)/shard_map/ppermute | solution.py:661
  64.0 1.4 %collective-permute-done.21.p3_ref = f32[24,192]{1,0:T(8,128)S(1)} collective-permute-done((f32[24,192]{1,0:T(8,128)S(1)}, f32[24,192]{1,0:T(8,128)S(1)}, u32[]{:S(2)}, u32[]{:S(2)}) %collective-permute-start.21) | collective-permute-done | bytes 18464 | tf_op jit(solution)/shard_map/ppermute | solution.py:661
  65.4 1.4 %pair_end.1 = f32[6,192,128]{2,1,0:T(8,128)} custom-call(f32[6,192,128]{2,1,0:T(8,128)S(1)} %get-tuple-element.46.after_ref.n_ref, f32[6,192,128]{2,1,0:T(8,128)S(1)} %get-tuple-element.47.scale_ref, f32[6,192,128]{2,1,0:T(8,128)S(1)} %pair_back.1.after_ref.dn_ref, f32[24,192]{1,0:T(8,128)S(1)} %get-tuple-element.84.p0_ref, ...), custom_call_target="tpu_custom_call" | custom-call | tf_op jit(solution)/shard_map/pair_end/pallas_call | solution.py:861
  (66 shorter events, 3.3 us)
Async XLA Ops:
  0.6 11.9 %copy-start = (f32[6,192,128]{2,1,0:T(8,128)S(1)}, f32[6,192,128]{2,1,0:T(8,128)}, u32[]{:S(2)}) copy-start(f32[6,192,128]{2,1,0:T(8,128)} %x_ref.3) | copy-start | bytes 1769476
  0.6 11.9 %copy-start.2 = (f32[128,8]{0,1:T(8,128)S(1)}, f32[128,8]{0,1:T(8,128)}, u32[]{:S(2)}) copy-start(f32[128,8]{0,1:T(8,128)} %param.36) | copy-start | bytes 12292
  0.7 11.9 %copy-start.14 = (f32[128,128]{1,0:T(8,128)S(1)}, f32[128,128]{1,0:T(8,128)}, u32[]{:S(2)}) copy-start(f32[128,128]{1,0:T(8,128)} %wq_ref.2) | copy-start | bytes 196612
  3.3 9.2 %copy-start.3 = (f32[128,4]{0,1:T(4,128)S(1)}, f32[128,4]{0,1:T(4,128)}, u32[]{:S(2)}) copy-start(f32[128,4]{0,1:T(4,128)} %param.28) | copy-start | bytes 6148
  3.3 9.2 %copy-start.5 = (f32[128]{0:T(128)S(1)}, f32[128]{0:T(128)}, u32[]{:S(2)}) copy-start(f32[128]{0:T(128)} %param.31) | copy-start | bytes 1540
  3.3 9.2 %copy-start.6 = (f32[128]{0:T(128)S(1)}, f32[128]{0:T(128)}, u32[]{:S(2)}) copy-start(f32[128]{0:T(128)} %param.23) | copy-start | bytes 1540
  3.4 8.6 %collective-permute-start.5 = (f32[72,128]{1,0:T(8,128)}, f32[72,128]{1,0:T(8,128)S(1)}, u32[]{:S(2)}, u32[]{:S(2)}) collective-permute-start(f32[72,128]{1,0:T(8,128)} %get-tuple-element.55.b0_ref), channel_id=1, source_target_pairs={{0,24},{4,28},{8,16},{12,20},{16,8},{20,12},{24,0},{28,4},{1,25},{... | collective-permute-start | bytes 110600 | tf_op jit(solution)/shard_map/ppermute | solution.py:661
  7.3 11.3 %collective-permute-start.4 = (f32[72,128]{1,0:T(8,128)}, f32[72,128]{1,0:T(8,128)S(1)}, u32[]{:S(2)}, u32[]{:S(2)}) collective-permute-start(f32[72,128]{1,0:T(8,128)} %get-tuple-element.55.b0_ref), channel_id=1, source_target_pairs={{0,16},{4,20},{8,24},{12,28},{16,0},{20,4},{24,8},{28,12},{1,17},{... | collective-permute-start | bytes 110600 | tf_op jit(solution)/shard_map/ppermute | solution.py:661
  7.8 10.8 %collective-permute-start.3 = (f32[72,128]{1,0:T(8,128)}, f32[72,128]{1,0:T(8,128)S(1)}, u32[]{:S(2)}, u32[]{:S(2)}) collective-permute-start(f32[72,128]{1,0:T(8,128)} %get-tuple-element.55.b0_ref), channel_id=1, source_target_pairs={{0,8},{4,12},{8,0},{12,4},{16,24},{20,28},{24,16},{28,20},{1,9},{5... | collective-permute-start | bytes 110600 | tf_op jit(solution)/shard_map/ppermute | solution.py:661
  8.0 11.4 %collective-permute-start.2 = (f32[120,256]{1,0:T(8,128)}, f32[120,256]{1,0:T(8,128)S(1)}, u32[]{:S(2)}, u32[]{:S(2)}) collective-permute-start(f32[120,256]{1,0:T(8,128)} %get-tuple-element.54.p0_ref.y0_ref.y_ref), channel_id=1, source_target_pairs={{0,3},{1,2},{2,1},{3,0},{4,7},{5,6},{6,5},{7,4},{8,11},{9,10},{10,... | collective-permute-start | bytes 368648 | tf_op jit(solution)/shard_map/ppermute | solution.py:661
  12.0 9.7 %collective-permute-start.1 = (f32[120,256]{1,0:T(8,128)}, f32[120,256]{1,0:T(8,128)S(1)}, u32[]{:S(2)}, u32[]{:S(2)}) collective-permute-start(f32[120,256]{1,0:T(8,128)} %get-tuple-element.54.p0_ref.y0_ref.y_ref), channel_id=1, source_target_pairs={{0,2},{1,3},{2,0},{3,1},{4,6},{5,7},{6,4},{7,5},{8,10},{9,11},{10,... | collective-permute-start | bytes 368648 | tf_op jit(solution)/shard_map/ppermute | solution.py:661
  12.0 9.7 %collective-permute-start = (f32[120,256]{1,0:T(8,128)}, f32[120,256]{1,0:T(8,128)S(1)}, u32[]{:S(2)}, u32[]{:S(2)}) collective-permute-start(f32[120,256]{1,0:T(8,128)} %get-tuple-element.54.p0_ref.y0_ref.y_ref), channel_id=1, source_target_pairs={{0,1},{1,0},{2,3},{3,2},{4,5},{5,4},{6,7},{7,6},{8,9},{9,8},{10,11... | collective-permute-start | bytes 368648 | tf_op jit(solution)/shard_map/ppermute | solution.py:661
  17.0 8.3 %copy-start.13 = (f32[2,48,256]{2,1,0:T(8,128)S(1)}, f32[2,48,256]{2,1,0:T(8,128)}, u32[]{:S(2)}) copy-start(f32[2,48,256]{2,1,0:T(8,128)} %adj_ref.3) | copy-start | bytes 294916
  18.7 6.6 %copy-start.10 = (f32[256,256]{1,0:T(8,128)S(1)}, f32[256,256]{1,0:T(8,128)}, u32[]{:S(2)}) copy-start(f32[256,256]{1,0:T(8,128)} %wv_ref.3) | copy-start | bytes 786436
  18.7 6.6 %copy-start.11 = (f32[256,256]{1,0:T(8,128)S(1)}, f32[256,256]{1,0:T(8,128)}, u32[]{:S(2)}) copy-start(f32[256,256]{1,0:T(8,128)} %wg_ref.3) | copy-start | bytes 786436
  18.7 6.6 %copy-start.12 = (f32[256,256]{1,0:T(8,128)S(1)}, f32[256,256]{1,0:T(8,128)}, u32[]{:S(2)}) copy-start(f32[256,256]{1,0:T(8,128)} %wo_ref.3) | copy-start | bytes 786436
  18.8 7.9 %collective-permute-start.10 = (f32[3,72,128]{2,1,0:T(8,128)S(1)}, f32[3,72,128]{2,1,0:T(8,128)S(1)}, u32[]{:S(2)}, u32[]{:S(2)}) collective-permute-start(f32[3,72,128]{2,1,0:T(8,128)S(1)} %stack_chips.2.after_ref.b1_ref), channel_id=1, source_target_pairs={{0,4},{4,0},{8,12},{12,8},{16,20},{20,16},{24,28},{28,24},{1,5},{5... | collective-permute-start | bytes 331784 | tf_op jit(solution)/shard_map/ppermute | solution.py:661
  18.9 7.8 %collective-permute-start.9 = (f32[72,128]{1,0:T(8,128)S(1)}, f32[72,128]{1,0:T(8,128)S(1)}, u32[]{:S(2)}, u32[]{:S(2)}) collective-permute-start(f32[72,128]{1,0:T(8,128)S(1)} %copy-done.19), channel_id=1, source_target_pairs={{0,4},{4,0},{8,12},{12,8},{16,20},{20,16},{24,28},{28,24},{1,5},{5... | collective-permute-start | bytes 110600 | tf_op jit(solution)/shard_map/ppermute | solution.py:661
  21.8 9.1 %collective-permute-start.8 = (f32[144,128]{1,0:T(8,128)S(1)}, f32[144,128]{1,0:T(8,128)S(1)}, u32[]{:S(2)}, u32[]{:S(2)}) collective-permute-start(f32[144,128]{1,0:T(8,128)S(1)} %stack_rows.1.b0_ref), channel_id=1, source_target_pairs={{0,24},{4,28},{8,16},{12,20},{16,8},{20,12},{24,0},{28,4},{1,25},{... | collective-permute-start | bytes 221192 | tf_op jit(solution)/shard_map/ppermute | solution.py:661
  24.3 6.6 %collective-permute-start.7 = (f32[144,128]{1,0:T(8,128)S(1)}, f32[144,128]{1,0:T(8,128)S(1)}, u32[]{:S(2)}, u32[]{:S(2)}) collective-permute-start(f32[144,128]{1,0:T(8,128)S(1)} %stack_rows.1.b0_ref), channel_id=1, source_target_pairs={{0,16},{4,20},{8,24},{12,28},{16,0},{20,4},{24,8},{28,12},{1,17},{... | collective-permute-start | bytes 221192 | tf_op jit(solution)/shard_map/ppermute | solution.py:661
  24.8 6.1 %collective-permute-start.6 = (f32[144,128]{1,0:T(8,128)S(1)}, f32[144,128]{1,0:T(8,128)S(1)}, u32[]{:S(2)}, u32[]{:S(2)}) collective-permute-start(f32[144,128]{1,0:T(8,128)S(1)} %stack_rows.1.b0_ref), channel_id=1, source_target_pairs={{0,8},{4,12},{8,0},{12,4},{16,24},{20,28},{24,16},{28,20},{1,9},{5... | collective-permute-start | bytes 221192 | tf_op jit(solution)/shard_map/ppermute | solution.py:661
  30.9 1.7 %collective-permute-start.12 = (f32[3,144,128]{2,1,0:T(8,128)S(1)}, f32[3,144,128]{2,1,0:T(8,128)S(1)}, u32[]{:S(2)}, u32[]{:S(2)}) collective-permute-start(f32[3,144,128]{2,1,0:T(8,128)S(1)} %stack_chips.3.b1_ref), channel_id=1, source_target_pairs={{0,4},{4,0},{8,12},{12,8},{16,20},{20,16},{24,28},{28,24},{1,5},{5... | collective-permute-start | bytes 663560 | tf_op jit(solution)/shard_map/ppermute | solution.py:661
  31.0 1.6 %collective-permute-start.11 = (f32[144,128]{1,0:T(8,128)S(1)}, f32[144,128]{1,0:T(8,128)S(1)}, u32[]{:S(2)}, u32[]{:S(2)}) collective-permute-start(f32[144,128]{1,0:T(8,128)S(1)} %stack_rows.1.b0_ref), channel_id=1, source_target_pairs={{0,4},{4,0},{8,12},{12,8},{16,20},{20,16},{24,28},{28,24},{1,5},{5... | collective-permute-start | bytes 221192 | tf_op jit(solution)/shard_map/ppermute | solution.py:661
  31.5 14.7 %collective-permute-start.13 = (f32[192,256]{1,0:T(8,128)S(1)}, f32[192,256]{1,0:T(8,128)S(1)}, u32[]{:S(2)}, u32[]{:S(2)}) collective-permute-start(f32[192,256]{1,0:T(8,128)S(1)} %get-tuple-element.69), channel_id=1, source_target_pairs={{0,2},{1,3},{2,0},{3,1},{4,6},{5,7},{6,4},{7,5},{8,10},{9,11},{10,... | collective-permute-start | bytes 589832 | tf_op jit(solution)/shard_map/ppermute | solution.py:661
  31.8 14.4 %collective-permute-start.14 = (f32[4,48,192]{2,1,0:T(8,128)S(1)}, f32[4,48,192]{2,1,0:T(8,128)S(1)}, u32[]{:S(2)}, u32[]{:S(2)}) collective-permute-start(f32[4,48,192]{2,1,0:T(8,128)S(1)} %get-tuple-element.70), channel_id=1, source_target_pairs={{0,4},{4,0},{8,12},{12,8},{16,20},{20,16},{24,28},{28,24},{1,5},{5... | collective-permute-start | bytes 442376 | tf_op jit(solution)/shard_map/ppermute | solution.py:661
  45.8 1.8 %collective-permute-start.15 = (f32[4,4,24,192]{3,2,1,0:T(8,128)S(1)}, f32[4,4,24,192]{3,2,1,0:T(8,128)S(1)}, u32[]{:S(2)}, u32[]{:S(2)}) collective-permute-start(f32[4,4,24,192]{3,2,1,0:T(8,128)S(1)} %get-tuple-element.72), channel_id=1, source_target_pairs={{0,4},{4,0},{8,12},{12,8},{16,20},{20,16},{24,28},{28,24},{1,5},{5... | collective-permute-start | bytes 884744 | tf_op jit(solution)/shard_map/ppermute | solution.py:661
  47.7 5.3 %collective-permute-start.16 = (f32[216,128]{1,0:T(8,128)S(1)}, f32[216,128]{1,0:T(8,128)S(1)}, u32[]{:S(2)}, u32[]{:S(2)}) collective-permute-start(f32[216,128]{1,0:T(8,128)S(1)} %get-tuple-element.75), channel_id=1, source_target_pairs={{0,8},{4,12},{8,0},{12,4},{16,24},{20,28},{24,16},{28,20},{1,9},{5... | collective-permute-start | bytes 331784 | tf_op jit(solution)/shard_map/ppermute | solution.py:661
  49.3 7.3 %collective-permute-start.17 = (f32[216,128]{1,0:T(8,128)S(1)}, f32[216,128]{1,0:T(8,128)S(1)}, u32[]{:S(2)}, u32[]{:S(2)}) collective-permute-start(f32[216,128]{1,0:T(8,128)S(1)} %get-tuple-element.76), channel_id=1, source_target_pairs={{0,16},{4,20},{8,24},{12,28},{16,0},{20,4},{24,8},{28,12},{1,17},{... | collective-permute-start | bytes 331784 | tf_op jit(solution)/shard_map/ppermute | solution.py:661
  50.8 5.8 %collective-permute-start.18 = (f32[216,128]{1,0:T(8,128)S(1)}, f32[216,128]{1,0:T(8,128)S(1)}, u32[]{:S(2)}, u32[]{:S(2)}) collective-permute-start(f32[216,128]{1,0:T(8,128)S(1)} %get-tuple-element.77), channel_id=1, source_target_pairs={{0,24},{4,28},{8,16},{12,20},{16,8},{20,12},{24,0},{28,4},{1,25},{... | collective-permute-start | bytes 331784 | tf_op jit(solution)/shard_map/ppermute | solution.py:661
  56.7 5.4 %collective-permute-start.19 = (f32[120,256]{1,0:T(8,128)S(1)}, f32[120,256]{1,0:T(8,128)S(1)}, u32[]{:S(2)}, u32[]{:S(2)}) collective-permute-start(f32[120,256]{1,0:T(8,128)S(1)} %get-tuple-element.85), channel_id=1, source_target_pairs={{0,1},{1,0},{2,3},{3,2},{4,5},{5,4},{6,7},{7,6},{8,9},{9,8},{10,11... | collective-permute-start | bytes 368648 | tf_op jit(solution)/shard_map/ppermute | solution.py:661
  59.0 5.0 %collective-permute-start.20 = (f32[24,192]{1,0:T(8,128)S(1)}, f32[24,192]{1,0:T(8,128)S(1)}, u32[]{:S(2)}, u32[]{:S(2)}) collective-permute-start(f32[24,192]{1,0:T(8,128)S(1)} %get-tuple-element.86), channel_id=1, source_target_pairs={{0,2},{1,3},{2,0},{3,1},{4,6},{5,7},{6,4},{7,5},{8,10},{9,11},{10,... | collective-permute-start | bytes 55304 | tf_op jit(solution)/shard_map/ppermute | solution.py:661
  59.8 5.6 %collective-permute-start.21 = (f32[24,192]{1,0:T(8,128)S(1)}, f32[24,192]{1,0:T(8,128)S(1)}, u32[]{:S(2)}, u32[]{:S(2)}) collective-permute-start(f32[24,192]{1,0:T(8,128)S(1)} %get-tuple-element.87), channel_id=1, source_target_pairs={{0,3},{1,2},{2,1},{3,0},{4,7},{5,6},{6,5},{7,4},{8,11},{9,10},{10,... | collective-permute-start | bytes 55304 | tf_op jit(solution)/shard_map/ppermute | solution.py:661
  (10 other events, 26.1 us)

commit v5 on v4

--- a/solution.py
+++ b/solution.py
@@ -366,54 +366,86 @@
         bt[...] = stack[...].T
         dbt[...] = jnp.zeros_like(dbt)
 
-    def pieces(ref, count):
-        return [ref[0, :, t * LANES : (t + 1) * LANES] for t in range(count)]
+    def pieces(ref, u, count):
+        return [ref[u, :, t * LANES : (t + 1) * LANES] for t in range(count)]
 
     masks = [head_mask(h, BF16) for h in range(heads)]
-    qs = [cat([a * mask for mask in masks], 0) for a in pieces(q_ref, 3)]
-    ms = [cat([a * mask for mask in masks], 0) for a in pieces(m_ref, 2)]
-    kcat = cat(left6(pieces(k_ref, 3)), 1)
-    vcat = cat(left3(pieces(v_ref, 2)), 1)
-    kt1, kt2 = kt_ref[0, :LANES], kt_ref[0, LANES:]
-    vt1, vt2 = vt_ref[0, :LANES], vt_ref[0, LANES:]
-    dk = jnp.zeros((n_keys, LANES), F32)
-    dv = jnp.zeros((n_keys, LANES), F32)
-    for c in range(heads * n_keys // TILE):
+    tiles = heads * n_keys // TILE
+    batch = q_ref.shape[0]
+
+    def operands(u):
+        qs = [cat([a * mask for mask in masks], 0) for a in pieces(q_ref, u, 3)]
+        ms = [cat([a * mask for mask in masks], 0) for a in pieces(m_ref, u, 2)]
+        kcat = cat(left6(pieces(k_ref, u, 3)), 1)
+        vcat = cat(left3(pieces(v_ref, u, 2)), 1)
+        return qs, ms, kcat, vcat
+
+    rows_in = {}
+
+    def logits(item):
+        u, c = divmod(item, tiles)
+        if u not in rows_in:
+            rows_in[u] = operands(u)
+        qs, ms, kcat, vcat = rows_in[u]
+        cols = slice(c * TILE, (c + 1) * TILE)
+        qc, mc = [a[cols] for a in qs], [a[cols] for a in ms]
+        s = nt(kcat, cat(right6(qc), 1)) + bt[:, cols]
+        return s, nt(vcat, cat(right3(mc), 1)), qc, mc
+
+    def weights(item, s, dp):
+        c = item % tiles
+        cols = slice(c * TILE, (c + 1) * TILE)
+        e = jnp.exp(s - jnp.max(s, axis=0, keepdims=True))
+        p = e * (1.0 / jnp.sum(e, axis=0, keepdims=True))
+        ds = p * (dp - jnp.sum(p * dp, axis=0, keepdims=True))
+        dbt[:, cols] = dbt[:, cols] + ds
+        return split2(p) + split2(ds)
+
+    sums = {}
+
+    def products(item, p1, p2, s1, s2, qc, mc):
+        u, c = divmod(item, tiles)
         cols = slice(c * TILE, (c + 1) * TILE)
         first, last = c * TILE // n_keys, ((c + 1) * TILE - 1) // n_keys
-        band = slice(first * HEAD, (last + 1) * HEAD)
         lane = lax.broadcasted_iota(jnp.int32, (1, TILE), 1) + c * TILE
 
-        def of_heads(top, low, a1, a2):
-            both = nn(cat([top[band], low[band]], 0), a1)
+        def of_heads(ref, a1, a2):
+            top = ref[u, first * HEAD : (last + 1) * HEAD]
+            low = ref[u, LANES + first * HEAD : LANES + (last + 1) * HEAD]
+            both = nn(cat([top, low], 0), a1)
             half = both.shape[0] // 2
-            total = both[:half] + both[half:] + nn(top[band], a2)
+            total = both[:half] + both[half:] + nn(top, a2)
             picked = total[:HEAD]
             for h in range(first + 1, last + 1):
                 rest = total[(h - first) * HEAD : (h - first + 1) * HEAD]
                 picked = jnp.where(lane >= h * n_keys, rest, picked)
             return picked
 
-        qc = [a[cols] for a in qs]
-        mc = [a[cols] for a in ms]
-        s = nt(kcat, cat(right6(qc), 1)) + bt[:, cols]
-        dp = nt(vcat, cat(right3(mc), 1))
-        e = jnp.exp(s - jnp.max(s, axis=0, keepdims=True))
-        p = e * (1.0 / jnp.sum(e, axis=0, keepdims=True))
-        p1, p2 = split2(p)
-        ot_ref[0, :, cols] = of_heads(vt1, vt2, p1, p2)
-        ds = p * (dp - jnp.sum(p * dp, axis=0, keepdims=True))
-        dbt[:, cols] = dbt[:, cols] + ds
-        s1, s2 = split2(ds)
-        dqt_ref[0, :, cols] = of_heads(kt1, kt2, s1, s2)
+        ot_ref[u, :, cols] = of_heads(vt_ref, p1, p2)
+        dqt_ref[u, :, cols] = of_heads(kt_ref, s1, s2)
         both = nn(s1, cat(qc[:2], 1))
-        dk = dk + both[:, :LANES] + both[:, LANES:] + nn(s2, qc[0])
+        dk = both[:, :LANES] + both[:, LANES:] + nn(s2, qc[0])
         both = nn(p1, cat(mc, 1))
-        dv = dv + both[:, :LANES] + both[:, LANES:] + nn(p2, mc[0])
-    dk_ref[0] = dk
-    dv_ref[0] = dv
-
-    @pl.when(step == rows - 1)
+        dv = both[:, :LANES] + both[:, LANES:] + nn(p2, mc[0])
+        if c > 0:
+            dk, dv = sums[u][0] + dk, sums[u][1] + dv
+        sums[u] = (dk, dv)
+        if c == tiles - 1:
+            dk_ref[u] = dk
+            dv_ref[u] = dv
+
+    count = batch * tiles
+    ready, waiting = {}, {}
+    for item in range(-1, count + 1):
+        if 0 <= item + 1 < count:
+            ready[item + 1] = logits(item + 1)
+        if 0 <= item < count:
+            s, dp, qc, mc = ready.pop(item)
+            waiting[item] = weights(item, s, dp) + (qc, mc)
+        if 0 <= item - 1 < count:
+            products(item - 1, *waiting.pop(item - 1))
+
+    @pl.when(step == pl.num_programs(0) - 1)
     def _():
         stack[...] = dbt[...].T
         for z in range(res_n):
@@ -435,7 +467,7 @@
 
 def pair_back_kernel(
     ot_ref, dqt_ref, dk_ref, dv_ref, dout_ref, sig_ref,
-    g_ref, wb_ref, after1_ref, after2_ref, dn_ref,
+    g_ref, wb_ref, dn_ref,
 ):
     rows, length, feats = dk_ref.shape
     g = g_ref[...]
@@ -523,38 +555,61 @@
         return total
 
     b1, b2 = wkv_ref[0], wkv_ref[1]
-    for b in range(n_seqs):
+
+    def spans(item):
+        b, t = divmod(item, tiles)
         near = slice(b * own, (b + 1) * own)
         wide = slice(b * n_keys, (b + 1) * n_keys)
-        dkt, dvt = [], []
-        for t in range(tiles):
-            cols = slice(t * LANES, (t + 1) * LANES)
-            lines = slice(t * group * own, (t + 1) * group * own)
-            q_t, m_t = q_ref[near, cols], m_ref[near, cols]
-            qs = [stacked(a, masks) for a in split3(q_t)]
-            ms = [stacked(a, masks) for a in split2(m_t)]
-            qt1, qt2 = split2(stacked(q_t, fmasks).T)
-            mt1, mt2 = split2(stacked(m_t, fmasks).T)
-            kp = split3(k_ref[wide, cols])
-            vp = split2(v_ref[wide, cols])
-            s = nt(cat(left6(qs), 1), cat(right6(kp), 1)) + bias[lines]
-            dp = nt(cat(left3(ms), 1), cat(right3(vp), 1))
-            e = jnp.exp(s - jnp.max(s, axis=1, keepdims=True))
-            p = e * (1.0 / jnp.sum(e, axis=1, keepdims=True))
-            p1, p2 = split2(p)
-            both = nn(p1, cat(vp, 1))
-            o_ref[near, cols] = own_rows(both[:, :LANES] + both[:, LANES:] + nn(p2, vp[0]))
-            ds = p * (dp - jnp.sum(p * dp, axis=1, keepdims=True))
-            dbias[lines] = ds if b == 0 else dbias[lines] + ds
-            s1, s2 = split2(ds)
-            both = nn(s1, cat(kp[:2], 1))
-            dq_ref[near, cols] = own_rows(both[:, :LANES] + both[:, LANES:] + nn(s2, kp[0]))
-            both = nn(cat([qt1, qt2], 0), s1)
-            dkt.append(both[:LANES] + both[LANES:] + nn(qt1, s2))
-            both = nn(cat([mt1, mt2], 0), p1)
-            dvt.append(both[:LANES] + both[LANES:] + nn(mt1, p2))
-        t1, t2 = split2(cat([a.T for a in dkt + dvt], 1))
-        dyall[b] = nt(t1, b1) + nt(t1, b2) + nt(t2, b1)
+        cols = slice(t * LANES, (t + 1) * LANES)
+        return b, near, wide, cols, slice(t * group * own, (t + 1) * group * own)
+
+    def logits(item):
+        b, near, wide, cols, lines = spans(item)
+        qs = [stacked(a, masks) for a in split3(q_ref[near, cols])]
+        ms = [stacked(a, masks) for a in split2(m_ref[near, cols])]
+        kp = split3(k_ref[wide, cols])
+        vp = split2(v_ref[wide, cols])
+        s = nt(cat(left6(qs), 1), cat(right6(kp), 1)) + bias[lines]
+        return s, nt(cat(left3(ms), 1), cat(right3(vp), 1)), kp, vp
+
+    def weights(item, s, dp):
+        b, near, wide, cols, lines = spans(item)
+        e = jnp.exp(s - jnp.max(s, axis=1, keepdims=True))
+        p = e * (1.0 / jnp.sum(e, axis=1, keepdims=True))
+        ds = p * (dp - jnp.sum(p * dp, axis=1, keepdims=True))
+        dbias[lines] = ds if b == 0 else dbias[lines] + ds
+        return split2(p) + split2(ds)
+
+    turned = {}
+
+    def products(item, p1, p2, s1, s2, kp, vp):
+        b, near, wide, cols, lines = spans(item)
+        qt1, qt2 = split2(stacked(q_ref[near, cols], fmasks).T)
+        mt1, mt2 = split2(stacked(m_ref[near, cols], fmasks).T)
+        both = nn(p1, cat(vp, 1))
+        o_ref[near, cols] = own_rows(both[:, :LANES] + both[:, LANES:] + nn(p2, vp[0]))
+        both = nn(s1, cat(kp[:2], 1))
+        dq_ref[near, cols] = own_rows(both[:, :LANES] + both[:, LANES:] + nn(s2, kp[0]))
+        both = nn(cat([qt1, qt2], 0), s1)
+        dkt = both[:LANES] + both[LANES:] + nn(qt1, s2)
+        both = nn(cat([mt1, mt2], 0), p1)
+        dvt = both[:LANES] + both[LANES:] + nn(mt1, p2)
+        turned.setdefault(b, []).append((dkt, dvt))
+        if len(turned[b]) == tiles:
+            flat = [a[0].T for a in turned[b]] + [a[1].T for a in turned[b]]
+            t1, t2 = split2(cat(flat, 1))
+            dyall[b] = nt(t1, b1) + nt(t1, b2) + nt(t2, b1)
+
+    count = n_seqs * tiles
+    ready, waiting = {}, {}
+    for item in range(-1, count + 1):
+        if 0 <= item + 1 < count:
+            ready[item + 1] = logits(item + 1)
+        if 0 <= item < count:
+            s, dp, kp, vp = ready.pop(item)
+            waiting[item] = weights(item, s, dp) + (kp, vp)
+        if 0 <= item - 1 < count:
+            products(item - 1, *waiting.pop(item - 1))
     for t, (ref, base) in enumerate(((r0_ref, 0), (r1_ref, 0), (r23_ref, 0), (r23_ref, n_seqs))):
         at = pl.multiple_of(lax.bitwise_xor(res, t) * own, own)
         for b in range(n_seqs):
@@ -785,12 +840,13 @@
 
     blocks = over_cores(first, over_chips(first, kept))
 
-    piece = lambda *s: pl.BlockSpec((1,) + s, lambda i: (i, 0, 0))
+    batch = 6 if rows % 6 == 0 else 1
+    piece = lambda *s: pl.BlockSpec((batch,) + s, lambda i: (i, 0, 0))
     whole = lambda *s: pl.BlockSpec(s, lambda i: (0,) * len(s))
     quarter = (chips, res_n, lines, length)
     ot, dqt, dk, dv, near, far = pl.pallas_call(
         functools.partial(pair_kernel, (rows, hp, seq_n, res_n)),
-        grid=(rows,),
+        grid=(rows // batch,),
         in_specs=[
             piece(length, 3 * feats), piece(length, 3 * feats),
             piece(length, 2 * feats), piece(length, 2 * feats),
@@ -818,13 +874,12 @@
     far_pair = swap(far, "seq", seq_n, 1)
     dn = pl.pallas_call(
         pair_back_kernel,
-        in_specs=vmem(8) + after * 2,
         out_shape=shape(rows, length, feats),
         compiler_params=params(32),
         name="pair_back",
         cost_estimate=pl.CostEstimate(flops=10**11, bytes_accessed=10**8, transcendentals=0),
     )(
-        ot, dqt, dk, dv, d_out, sig, gain, wb, r23, far_msa,
+        ot, dqt, dk, dv, d_out, sig, gain, wb,
     )
     sums = pl.pallas_call(
         core_sum_kernel,

time: 67.2 us -> 60.3 us (0.90)
  Pallas kernels: 27.4 us -> 20.5 us
    pallas_call x1, Pallas kernels: 13.3 us -> 7.4 us  [fused_on_device(): pl.pallas_call(functools.partial(pair_kernel, (rows, hp, seq_n, res_n)),...]
    pallas_call x1, Pallas kernels: 4.17 us -> 3.12 us  [fused_on_device(): pl.pallas_call(functools.partial(msa_kernel, (rows, hm, seq_n, res_n)), o...]
  transfers between devices with their start and end apart: 22 -> 22, of which waited for: 8 -> 8; matrix products, arithmetic and copies ran while one was open for 0% -> 0% of each run, Pallas kernels for 35% -> 27%
where the time goes in v5:
time: 60.3 us; the launch traced here: 59.9 us
  starting transfers between devices  22.5 us (37%)
  Pallas kernels  20.5 us (34%)
  waiting for transfers between devices  11.5 us (19%)
  local copies, waits for them, and re-layouts  4.49 us (7%)
  between operations  0.94 us (2%)
    ppermute x22, starting transfers between devices, swap(): return lax.ppermute(values, axis, [(i, i ^ offset) for i in range(size)])  22.5 us
    ppermute x22, waiting for transfers between devices, swap(): return lax.ppermute(values, axis, [(i, i ^ offset) for i in range(size)])  11.5 us
    pallas_call x1, Pallas kernels, fused_on_device(): pl.pallas_call(functools.partial(pair_kernel, (rows, hp, seq_n, res_n)),...  7.4 us
    unnamed x40, local copies, waits for them, and re-layouts  4.49 us
    pallas_call x1, Pallas kernels, fused_on_device(): pl.pallas_call(functools.partial(msa_kernel, (rows, hm, seq_n, res_n)), o...  3.12 us
    pallas_call x1, Pallas kernels, fused_on_device(): pl.pallas_call(functools.partial(bias_kernel, rows), out_shape=(shape(bas...  2.68 us
    pallas_call x1, Pallas kernels, fused_on_device(): pl.pallas_call(pair_project_kernel, out_shape=(bf(rows, length, 3 * feats...  1.65 us
    pallas_call x1, Pallas kernels, fused_on_device(): pl.pallas_call(pair_end_kernel, out_shape=shape(rows, length, feats), com...  1.44 us
  transfers between devices with their start and end apart: 22, of which 8 were waited for; matrix products, arithmetic and copies ran while one was open for 0% of the time, Pallas kernels for 27%

profile of v5, /device:TPU:0, one launch (start us, length us, event | category | flops | bytes accessed | tf_op | source)
XLA Modules:
  0.0 59.9 jit_solution(5135945528930097014)
XLA Ops:
  0.7 2.7 %bias_rows.1 = (f32[120,256]{1,0:T(8,128)}, f32[72,128]{1,0:T(8,128)}) custom-call(f32[6,192,128]{2,1,0:T(8,128)} %x_ref.3, f32[96,256]{1,0:T(8,128)} %bitcast.17, f32[1,128]{1,0:T(1,128)} %bitcast.14, f32[4,128]{1,0:T(4,128)} %bitcast.8, f32[1,128]{1,0:T(1,128)} %bitcast.12, f32[8,128]{1,0:T(8,128)} %bitcast.6), custom_call_target="tpu_custom_call" | custom-call | tf_op jit(solution)/shard_map/bias_rows/pallas_call | solution.py:755
  3.4 4.0 %collective-permute-start.5 = (f32[72,128]{1,0:T(8,128)}, f32[72,128]{1,0:T(8,128)S(1)}, u32[]{:S(2)}, u32[]{:S(2)}) collective-permute-start(f32[72,128]{1,0:T(8,128)} %get-tuple-element.55.b0_ref), channel_id=1, source_target_pairs={{0,24},{4,28},{8,16},{12,20},{16,8},{20,12},{24,0},{28,4},{1,25},{... | collective-permute-start | bytes 110600 | tf_op jit(solution)/shard_map/ppermute | solution.py:716
  7.3 0.5 collective-permute-start.4
  8.0 4.0 %collective-permute-start.2 = (f32[120,256]{1,0:T(8,128)}, f32[120,256]{1,0:T(8,128)S(1)}, u32[]{:S(2)}, u32[]{:S(2)}) collective-permute-start(f32[120,256]{1,0:T(8,128)} %get-tuple-element.54.p0_ref.y0_ref.y_ref), channel_id=1, source_target_pairs={{0,3},{1,2},{2,1},{3,0},{4,7},{5,6},{6,5},{7,4},{8,11},{9,10},{10,... | collective-permute-start | bytes 368648 | tf_op jit(solution)/shard_map/ppermute | solution.py:716
  12.0 0.6 collective-permute-start
  12.6 1.1 %copy-done.7 = f32[6,192,128]{2,1,0:T(8,128)S(1)} copy-done((f32[6,192,128]{2,1,0:T(8,128)S(1)}, f32[6,192,128]{2,1,0:T(8,128)}, u32[]{:S(2)}) %copy-start.7) | copy-done | bytes 589848
  13.6 0.8 %copy-done.15 = f32[128,128]{1,0:T(8,128)S(1)} copy-done((f32[128,128]{1,0:T(8,128)S(1)}, f32[128,128]{1,0:T(8,128)}, u32[]{:S(2)}) %copy-start.15) | copy-done | bytes 65560
  14.5 0.8 %copy-done.16 = f32[128,128]{1,0:T(8,128)S(1)} copy-done((f32[128,128]{1,0:T(8,128)S(1)}, f32[128,128]{1,0:T(8,128)}, u32[]{:S(2)}) %copy-start.16) | copy-done | bytes 65560
  15.3 0.8 %copy-done.17 = f32[128,128]{1,0:T(8,128)S(1)} copy-done((f32[128,128]{1,0:T(8,128)S(1)}, f32[128,128]{1,0:T(8,128)}, u32[]{:S(2)}) %copy-start.17) | copy-done | bytes 65560
  16.2 0.8 %copy-done.18 = f32[128,128]{1,0:T(8,128)S(1)} copy-done((f32[128,128]{1,0:T(8,128)S(1)}, f32[128,128]{1,0:T(8,128)}, u32[]{:S(2)}) %copy-start.18) | copy-done | bytes 65560
  17.0 1.6 %pair_project.1 = (bf16[6,192,384]{2,1,0:T(8,128)(2,1)S(1)}, bf16[6,192,384]{2,1,0:T(8,128)(2,1)S(1)}, bf16[6,192,256]{2,1,0:T(8,128)(2,1)S(1)}, bf16[6,192,256]...) custom-call(f32[6,192,128]{2,1,0:T(8,128)S(1)} %copy-done, ...), custom_call_target="tpu_custom_call" | custom-call | flops 2000000000 | bytes 10000000 | tf_op jit(solution)/shard_map/pair_project/pallas_call | solution.py:780
  19.3 2.4 %collective-permute-done.1.p2_ref.y2_ref = f32[120,256]{1,0:T(8,128)S(1)} collective-permute-done((f32[120,256]{1,0:T(8,128)}, f32[120,256]{1,0:T(8,128)S(1)}, u32[]{:S(2)}, u32[]{:S(2)}) %collective-permute-start.1) | collective-permute-done | bytes 122912 | tf_op jit(solution)/shard_map/ppermute | solution.py:716
  21.8 2.5 %collective-permute-start.8 = (f32[144,128]{1,0:T(8,128)S(1)}, f32[144,128]{1,0:T(8,128)S(1)}, u32[]{:S(2)}, u32[]{:S(2)}) collective-permute-start(f32[144,128]{1,0:T(8,128)S(1)} %stack_rows.1.b0_ref), channel_id=1, source_target_pairs={{0,24},{4,28},{8,16},{12,20},{16,8},{20,12},{24,0},{28,4},{1,25},{... | collective-permute-start | bytes 221192 | tf_op jit(solution)/shard_map/ppermute | solution.py:716
  24.3 0.5 collective-permute-start.7
  24.8 0.5 collective-permute-start.6
  25.4 1.3 %msa_project.1 = (f32[96,256]{1,0:T(8,128)S(1)}, f32[96,256]{1,0:T(8,128)S(1)}, f32[96,256]{1,0:T(8,128)S(1)}, f32[96,256]{1,0:T(8,128)S(1)}, f32[384,256]{1,0:T...) custom-call(f32[120,256]{1,0:T(8,128)S(1)} %copy-done.1, ...), custom_call_target="tpu_custom_call" | custom-call | flops 1000000000 | bytes 10000000 | tf_op jit(solution)/shard_map/msa_project/pallas_call | solution.py:810
  26.7 3.1 %msa_attention.1 = (f32[96,256]{1,0:T(8,128)S(1)}, f32[96,256]{1,0:T(8,128)S(1)}, f32[96,256]{1,0:T(8,128)S(1)}, f32[96,256]{1,0:T(8,128)S(1)}, f32[192,256]{1,0...) custom-call(f32[96,256]{1,0:T(8,128)S(1)} %get-tuple-element.56.q_ref, ...), custom_call_target="tpu_custom_call" | custom-call | flops 4000000000 | bytes 10000000 | tf_op jit(solution)/shard_map/msa_attention/pallas_call | solution.py:824
  30.8 0.7 %collective-permute-done.11.b2_ref = f32[144,128]{1,0:T(8,128)S(1)} collective-permute-done((f32[144,128]{1,0:T(8,128)S(1)}, f32[144,128]{1,0:T(8,128)S(1)}, u32[]{:S(2)}, u32[]{:S(2)}) %collective-permute-start.11) | collective-permute-done | bytes 73760 | tf_op jit(solution)/shard_map/ppermute | solution.py:716
  31.5 7.4 %pair_attention.1 = (f32[6,32,768]{2,1,0:T(8,128)S(1)}, f32[6,32,768]{2,1,0:T(8,128)S(1)}, f32[6,192,128]{2,1,0:T(8,128)S(1)}, f32[6,192,128]{2,1,0:T(8,128)S(1)...) custom-call(bf16[6,192,384]{2,1,0:T(8,128)(2,1)S(1)} %get-tuple-element.48.q_ref, ...), custom_call_target="tpu_custom_call" | custom-call | flops 10000000000 | bytes 10000000 | tf_op jit(solution)/shard_map/pair_attention/pallas_call | solution.py:847
  39.2 1.3 %pair_back.1.after_ref.dn_ref = f32[6,192,128]{2,1,0:T(8,128)S(1)} custom-call(f32[6,32,768]{2,1,0:T(8,128)S(1)} %get-tuple-element.62.ot_ref, f32[6,32,768]{2,1,0:T(8,128)S(1)} %get-tuple-element.63.dqt_ref, f32[6,192,128]{2,1,0:T(8,128)S(1)} %get-tuple-element.64.dk_ref, f32[6,192,128]{2,1,0:T(8,128)S(1)} %get-tuple-element.65.dv_ref, ...), custom_call_target="tpu_custom_call" | custom-call | flops 99999997952 | bytes 100000000 | tf_op jit(solution)/shard_map/pair_back/pallas_call | solution.py:875
  40.8 1.6 %collective-permute-start.15 = (f32[216,128]{1,0:T(8,128)S(1)}, f32[216,128]{1,0:T(8,128)S(1)}, u32[]{:S(2)}, u32[]{:S(2)}) collective-permute-start(f32[216,128]{1,0:T(8,128)S(1)} %get-tuple-element.74), channel_id=1, source_target_pairs={{0,8},{4,12},{8,0},{12,4},{16,24},{20,28},{24,16},{28,20},{1,9},{5... | collective-permute-start | bytes 331784 | tf_op jit(solution)/shard_map/ppermute | solution.py:716
  42.4 1.5 %collective-permute-start.16 = (f32[216,128]{1,0:T(8,128)S(1)}, f32[216,128]{1,0:T(8,128)S(1)}, u32[]{:S(2)}, u32[]{:S(2)}) collective-permute-start(f32[216,128]{1,0:T(8,128)S(1)} %get-tuple-element.75), channel_id=1, source_target_pairs={{0,16},{4,20},{8,24},{12,28},{16,0},{20,4},{24,8},{28,12},{1,17},{... | collective-permute-start | bytes 331784 | tf_op jit(solution)/shard_map/ppermute | solution.py:716
  44.8 1.3 %collective-permute-done.15.s1_ref = f32[216,128]{1,0:T(8,128)S(1)} collective-permute-done((f32[216,128]{1,0:T(8,128)S(1)}, f32[216,128]{1,0:T(8,128)S(1)}, u32[]{:S(2)}, u32[]{:S(2)}) %collective-permute-start.15) | collective-permute-done | bytes 110624 | tf_op jit(solution)/shard_map/ppermute | solution.py:716
  46.1 3.6 %collective-permute-done.16.s2_ref = f32[216,128]{1,0:T(8,128)S(1)} collective-permute-done((f32[216,128]{1,0:T(8,128)S(1)}, f32[216,128]{1,0:T(8,128)S(1)}, u32[]{:S(2)}, u32[]{:S(2)}) %collective-permute-start.16) | collective-permute-done | bytes 110624 | tf_op jit(solution)/shard_map/ppermute | solution.py:716
  49.8 2.0 %collective-permute-start.19 = (f32[120,256]{1,0:T(8,128)S(1)}, f32[120,256]{1,0:T(8,128)S(1)}, u32[]{:S(2)}, u32[]{:S(2)}) collective-permute-start(f32[120,256]{1,0:T(8,128)S(1)} %get-tuple-element.85), channel_id=1, source_target_pairs={{0,1},{1,0},{2,3},{3,2},{4,5},{5,4},{6,7},{7,6},{8,9},{9,8},{10,11... | collective-permute-start | bytes 368648 | tf_op jit(solution)/shard_map/ppermute | solution.py:716
  51.8 1.0 %collective-permute-start.20 = (f32[24,192]{1,0:T(8,128)S(1)}, f32[24,192]{1,0:T(8,128)S(1)}, u32[]{:S(2)}, u32[]{:S(2)}) collective-permute-start(f32[24,192]{1,0:T(8,128)S(1)} %get-tuple-element.86), channel_id=1, source_target_pairs={{0,2},{1,3},{2,0},{3,1},{4,6},{5,7},{6,4},{7,5},{8,10},{9,11},{10,... | collective-permute-start | bytes 55304 | tf_op jit(solution)/shard_map/ppermute | solution.py:716
  52.8 1.4 %collective-permute-start.21 = (f32[24,192]{1,0:T(8,128)S(1)}, f32[24,192]{1,0:T(8,128)S(1)}, u32[]{:S(2)}, u32[]{:S(2)}) collective-permute-start(f32[24,192]{1,0:T(8,128)S(1)} %get-tuple-element.87), channel_id=1, source_target_pairs={{0,3},{1,2},{2,1},{3,0},{4,7},{5,6},{6,5},{7,4},{8,11},{9,10},{10,... | collective-permute-start | bytes 55304 | tf_op jit(solution)/shard_map/ppermute | solution.py:716
  54.2 0.7 %collective-permute-done.19.p1_ref.r1_ref = f32[120,256]{1,0:T(8,128)S(1)} collective-permute-done((f32[120,256]{1,0:T(8,128)S(1)}, f32[120,256]{1,0:T(8,128)S(1)}, u32[]{:S(2)}, u32[]{:S(2)}) %collective-permute-start.19) | collective-permute-done | bytes 122912 | tf_op jit(solution)/shard_map/ppermute | solution.py:716
  54.9 0.9 %aligned_end.1 = f32[2,48,256]{2,1,0:T(8,128)} custom-call(f32[120,256]{1,0:T(8,128)S(1)} %copy-done.1, f32[1,256]{1,0:T(1,128)S(1)} %bitcast.11, f32[96,256]{1,0:T(8,128)S(1)} %aligned_back.1.after_ref.dy_ref, f32[192,256]{1,0:T(8,128)S(1)} %collective-permute-done.18.r23_ref, f32[120,256]{1,0:T(8,128)S(1)} %collective-permute-done.19.p1_ref.r1_ref), custom_call_target="tpu_custom_call" | custom-call | tf_op jit(solution)/shard_map/aligned_end/pallas_call | solution.py:910
  55.8 1.0 %collective-permute-done.20.p2_ref = f32[24,192]{1,0:T(8,128)S(1)} collective-permute-done((f32[24,192]{1,0:T(8,128)S(1)}, f32[24,192]{1,0:T(8,128)S(1)}, u32[]{:S(2)}, u32[]{:S(2)}) %collective-permute-start.20) | collective-permute-done | bytes 18464 | tf_op jit(solution)/shard_map/ppermute | solution.py:716
  56.8 1.7 %collective-permute-done.21.p3_ref = f32[24,192]{1,0:T(8,128)S(1)} collective-permute-done((f32[24,192]{1,0:T(8,128)S(1)}, f32[24,192]{1,0:T(8,128)S(1)}, u32[]{:S(2)}, u32[]{:S(2)}) %collective-permute-start.21) | collective-permute-done | bytes 18464 | tf_op jit(solution)/shard_map/ppermute | solution.py:716
  58.4 1.4 %pair_end.1 = f32[6,192,128]{2,1,0:T(8,128)} custom-call(f32[6,192,128]{2,1,0:T(8,128)S(1)} %get-tuple-element.46.after_ref.n_ref, f32[6,192,128]{2,1,0:T(8,128)S(1)} %get-tuple-element.47.scale_ref, f32[6,192,128]{2,1,0:T(8,128)S(1)} %pair_back.1.after_ref.dn_ref, f32[24,192]{1,0:T(8,128)S(1)} %get-tuple-element.84.p0_ref, ...), custom_call_target="tpu_custom_call" | custom-call | tf_op jit(solution)/shard_map/pair_end/pallas_call | solution.py:916
  (66 shorter events, 3.4 us)
Async XLA Ops:
  0.6 11.9 %copy-start = (f32[6,192,128]{2,1,0:T(8,128)S(1)}, f32[6,192,128]{2,1,0:T(8,128)}, u32[]{:S(2)}) copy-start(f32[6,192,128]{2,1,0:T(8,128)} %x_ref.3) | copy-start | bytes 1769476
  0.6 11.9 %copy-start.2 = (f32[128,8]{0,1:T(8,128)S(1)}, f32[128,8]{0,1:T(8,128)}, u32[]{:S(2)}) copy-start(f32[128,8]{0,1:T(8,128)} %param.36) | copy-start | bytes 12292
  0.7 11.9 %copy-start.14 = (f32[128,128]{1,0:T(8,128)S(1)}, f32[128,128]{1,0:T(8,128)}, u32[]{:S(2)}) copy-start(f32[128,128]{1,0:T(8,128)} %wq_ref.2) | copy-start | bytes 196612
  3.3 9.2 %copy-start.3 = (f32[128,4]{0,1:T(4,128)S(1)}, f32[128,4]{0,1:T(4,128)}, u32[]{:S(2)}) copy-start(f32[128,4]{0,1:T(4,128)} %param.28) | copy-start | bytes 6148
  3.3 9.2 %copy-start.5 = (f32[128]{0:T(128)S(1)}, f32[128]{0:T(128)}, u32[]{:S(2)}) copy-start(f32[128]{0:T(128)} %param.31) | copy-start | bytes 1540
  3.3 9.2 %copy-start.6 = (f32[128]{0:T(128)S(1)}, f32[128]{0:T(128)}, u32[]{:S(2)}) copy-start(f32[128]{0:T(128)} %param.23) | copy-start | bytes 1540
  3.4 8.6 %collective-permute-start.5 = (f32[72,128]{1,0:T(8,128)}, f32[72,128]{1,0:T(8,128)S(1)}, u32[]{:S(2)}, u32[]{:S(2)}) collective-permute-start(f32[72,128]{1,0:T(8,128)} %get-tuple-element.55.b0_ref), channel_id=1, source_target_pairs={{0,24},{4,28},{8,16},{12,20},{16,8},{20,12},{24,0},{28,4},{1,25},{... | collective-permute-start | bytes 110600 | tf_op jit(solution)/shard_map/ppermute | solution.py:716
  7.3 11.3 %collective-permute-start.4 = (f32[72,128]{1,0:T(8,128)}, f32[72,128]{1,0:T(8,128)S(1)}, u32[]{:S(2)}, u32[]{:S(2)}) collective-permute-start(f32[72,128]{1,0:T(8,128)} %get-tuple-element.55.b0_ref), channel_id=1, source_target_pairs={{0,16},{4,20},{8,24},{12,28},{16,0},{20,4},{24,8},{28,12},{1,17},{... | collective-permute-start | bytes 110600 | tf_op jit(solution)/shard_map/ppermute | solution.py:716
  7.8 10.8 %collective-permute-start.3 = (f32[72,128]{1,0:T(8,128)}, f32[72,128]{1,0:T(8,128)S(1)}, u32[]{:S(2)}, u32[]{:S(2)}) collective-permute-start(f32[72,128]{1,0:T(8,128)} %get-tuple-element.55.b0_ref), channel_id=1, source_target_pairs={{0,8},{4,12},{8,0},{12,4},{16,24},{20,28},{24,16},{28,20},{1,9},{5... | collective-permute-start | bytes 110600 | tf_op jit(solution)/shard_map/ppermute | solution.py:716
  8.0 11.4 %collective-permute-start.2 = (f32[120,256]{1,0:T(8,128)}, f32[120,256]{1,0:T(8,128)S(1)}, u32[]{:S(2)}, u32[]{:S(2)}) collective-permute-start(f32[120,256]{1,0:T(8,128)} %get-tuple-element.54.p0_ref.y0_ref.y_ref), channel_id=1, source_target_pairs={{0,3},{1,2},{2,1},{3,0},{4,7},{5,6},{6,5},{7,4},{8,11},{9,10},{10,... | collective-permute-start | bytes 368648 | tf_op jit(solution)/shard_map/ppermute | solution.py:716
  12.0 9.7 %collective-permute-start.1 = (f32[120,256]{1,0:T(8,128)}, f32[120,256]{1,0:T(8,128)S(1)}, u32[]{:S(2)}, u32[]{:S(2)}) collective-permute-start(f32[120,256]{1,0:T(8,128)} %get-tuple-element.54.p0_ref.y0_ref.y_ref), channel_id=1, source_target_pairs={{0,2},{1,3},{2,0},{3,1},{4,6},{5,7},{6,4},{7,5},{8,10},{9,11},{10,... | collective-permute-start | bytes 368648 | tf_op jit(solution)/shard_map/ppermute | solution.py:716
  12.0 9.7 %collective-permute-start = (f32[120,256]{1,0:T(8,128)}, f32[120,256]{1,0:T(8,128)S(1)}, u32[]{:S(2)}, u32[]{:S(2)}) collective-permute-start(f32[120,256]{1,0:T(8,128)} %get-tuple-element.54.p0_ref.y0_ref.y_ref), channel_id=1, source_target_pairs={{0,1},{1,0},{2,3},{3,2},{4,5},{5,4},{6,7},{7,6},{8,9},{9,8},{10,11... | collective-permute-start | bytes 368648 | tf_op jit(solution)/shard_map/ppermute | solution.py:716
  17.0 8.3 %copy-start.13 = (f32[2,48,256]{2,1,0:T(8,128)S(1)}, f32[2,48,256]{2,1,0:T(8,128)}, u32[]{:S(2)}) copy-start(f32[2,48,256]{2,1,0:T(8,128)} %adj_ref.3) | copy-start | bytes 294916
  18.7 6.6 %copy-start.10 = (f32[256,256]{1,0:T(8,128)S(1)}, f32[256,256]{1,0:T(8,128)}, u32[]{:S(2)}) copy-start(f32[256,256]{1,0:T(8,128)} %wv_ref.3) | copy-start | bytes 786436
  18.7 6.6 %copy-start.11 = (f32[256,256]{1,0:T(8,128)S(1)}, f32[256,256]{1,0:T(8,128)}, u32[]{:S(2)}) copy-start(f32[256,256]{1,0:T(8,128)} %wg_ref.3) | copy-start | bytes 786436
  18.7 6.6 %copy-start.12 = (f32[256,256]{1,0:T(8,128)S(1)}, f32[256,256]{1,0:T(8,128)}, u32[]{:S(2)}) copy-start(f32[256,256]{1,0:T(8,128)} %wo_ref.3) | copy-start | bytes 786436
  18.8 7.9 %collective-permute-start.10 = (f32[3,72,128]{2,1,0:T(8,128)S(1)}, f32[3,72,128]{2,1,0:T(8,128)S(1)}, u32[]{:S(2)}, u32[]{:S(2)}) collective-permute-start(f32[3,72,128]{2,1,0:T(8,128)S(1)} %stack_chips.2.after_ref.b1_ref), channel_id=1, source_target_pairs={{0,4},{4,0},{8,12},{12,8},{16,20},{20,16},{24,28},{28,24},{1,5},{5... | collective-permute-start | bytes 331784 | tf_op jit(solution)/shard_map/ppermute | solution.py:716
  18.9 7.8 %collective-permute-start.9 = (f32[72,128]{1,0:T(8,128)S(1)}, f32[72,128]{1,0:T(8,128)S(1)}, u32[]{:S(2)}, u32[]{:S(2)}) collective-permute-start(f32[72,128]{1,0:T(8,128)S(1)} %copy-done.19), channel_id=1, source_target_pairs={{0,4},{4,0},{8,12},{12,8},{16,20},{20,16},{24,28},{28,24},{1,5},{5... | collective-permute-start | bytes 110600 | tf_op jit(solution)/shard_map/ppermute | solution.py:716
  21.8 8.0 %collective-permute-start.8 = (f32[144,128]{1,0:T(8,128)S(1)}, f32[144,128]{1,0:T(8,128)S(1)}, u32[]{:S(2)}, u32[]{:S(2)}) collective-permute-start(f32[144,128]{1,0:T(8,128)S(1)} %stack_rows.1.b0_ref), channel_id=1, source_target_pairs={{0,24},{4,28},{8,16},{12,20},{16,8},{20,12},{24,0},{28,4},{1,25},{... | collective-permute-start | bytes 221192 | tf_op jit(solution)/shard_map/ppermute | solution.py:716
  24.3 5.5 %collective-permute-start.7 = (f32[144,128]{1,0:T(8,128)S(1)}, f32[144,128]{1,0:T(8,128)S(1)}, u32[]{:S(2)}, u32[]{:S(2)}) collective-permute-start(f32[144,128]{1,0:T(8,128)S(1)} %stack_rows.1.b0_ref), channel_id=1, source_target_pairs={{0,16},{4,20},{8,24},{12,28},{16,0},{20,4},{24,8},{28,12},{1,17},{... | collective-permute-start | bytes 221192 | tf_op jit(solution)/shard_map/ppermute | solution.py:716
  24.8 5.0 %collective-permute-start.6 = (f32[144,128]{1,0:T(8,128)S(1)}, f32[144,128]{1,0:T(8,128)S(1)}, u32[]{:S(2)}, u32[]{:S(2)}) collective-permute-start(f32[144,128]{1,0:T(8,128)S(1)} %stack_rows.1.b0_ref), channel_id=1, source_target_pairs={{0,8},{4,12},{8,0},{12,4},{16,24},{20,28},{24,16},{28,20},{1,9},{5... | collective-permute-start | bytes 221192 | tf_op jit(solution)/shard_map/ppermute | solution.py:716
  29.9 1.7 %collective-permute-start.12 = (f32[3,144,128]{2,1,0:T(8,128)S(1)}, f32[3,144,128]{2,1,0:T(8,128)S(1)}, u32[]{:S(2)}, u32[]{:S(2)}) collective-permute-start(f32[3,144,128]{2,1,0:T(8,128)S(1)} %stack_chips.3.b1_ref), channel_id=1, source_target_pairs={{0,4},{4,0},{8,12},{12,8},{16,20},{20,16},{24,28},{28,24},{1,5},{5... | collective-permute-start | bytes 663560 | tf_op jit(solution)/shard_map/ppermute | solution.py:716
  29.9 1.6 %collective-permute-start.11 = (f32[144,128]{1,0:T(8,128)S(1)}, f32[144,128]{1,0:T(8,128)S(1)}, u32[]{:S(2)}, u32[]{:S(2)}) collective-permute-start(f32[144,128]{1,0:T(8,128)S(1)} %stack_rows.1.b0_ref), channel_id=1, source_target_pairs={{0,4},{4,0},{8,12},{12,8},{16,20},{20,16},{24,28},{28,24},{1,5},{5... | collective-permute-start | bytes 221192 | tf_op jit(solution)/shard_map/ppermute | solution.py:716
  30.4 10.1 %collective-permute-start.14 = (f32[4,48,192]{2,1,0:T(8,128)S(1)}, f32[4,48,192]{2,1,0:T(8,128)S(1)}, u32[]{:S(2)}, u32[]{:S(2)}) collective-permute-start(f32[4,48,192]{2,1,0:T(8,128)S(1)} %get-tuple-element.72), channel_id=1, source_target_pairs={{0,4},{4,0},{8,12},{12,8},{16,20},{20,16},{24,28},{28,24},{1,5},{5... | collective-permute-start | bytes 442376 | tf_op jit(solution)/shard_map/ppermute | solution.py:716
  30.5 14.2 %collective-permute-start.18 = (f32[192,256]{1,0:T(8,128)S(1)}, f32[192,256]{1,0:T(8,128)S(1)}, u32[]{:S(2)}, u32[]{:S(2)}) collective-permute-start(f32[192,256]{1,0:T(8,128)S(1)} %get-tuple-element.78), channel_id=1, source_target_pairs={{0,2},{1,3},{2,0},{3,1},{4,6},{5,7},{6,4},{7,5},{8,10},{9,11},{10,... | collective-permute-start | bytes 589832 | tf_op jit(solution)/shard_map/ppermute | solution.py:716
  38.9 1.8 %collective-permute-start.13 = (f32[4,4,24,192]{3,2,1,0:T(8,128)S(1)}, f32[4,4,24,192]{3,2,1,0:T(8,128)S(1)}, u32[]{:S(2)}, u32[]{:S(2)}) collective-permute-start(f32[4,4,24,192]{3,2,1,0:T(8,128)S(1)} %get-tuple-element.70), channel_id=1, source_target_pairs={{0,4},{4,0},{8,12},{12,8},{16,20},{20,16},{24,28},{28,24},{1,5},{5... | collective-permute-start | bytes 884744 | tf_op jit(solution)/shard_map/ppermute | solution.py:716
  40.8 5.2 %collective-permute-start.15 = (f32[216,128]{1,0:T(8,128)S(1)}, f32[216,128]{1,0:T(8,128)S(1)}, u32[]{:S(2)}, u32[]{:S(2)}) collective-permute-start(f32[216,128]{1,0:T(8,128)S(1)} %get-tuple-element.74), channel_id=1, source_target_pairs={{0,8},{4,12},{8,0},{12,4},{16,24},{20,28},{24,16},{28,20},{1,9},{5... | collective-permute-start | bytes 331784 | tf_op jit(solution)/shard_map/ppermute | solution.py:716
  42.4 7.3 %collective-permute-start.16 = (f32[216,128]{1,0:T(8,128)S(1)}, f32[216,128]{1,0:T(8,128)S(1)}, u32[]{:S(2)}, u32[]{:S(2)}) collective-permute-start(f32[216,128]{1,0:T(8,128)S(1)} %get-tuple-element.75), channel_id=1, source_target_pairs={{0,16},{4,20},{8,24},{12,28},{16,0},{20,4},{24,8},{28,12},{1,17},{... | collective-permute-start | bytes 331784 | tf_op jit(solution)/shard_map/ppermute | solution.py:716
  43.9 5.7 %collective-permute-start.17 = (f32[216,128]{1,0:T(8,128)S(1)}, f32[216,128]{1,0:T(8,128)S(1)}, u32[]{:S(2)}, u32[]{:S(2)}) collective-permute-start(f32[216,128]{1,0:T(8,128)S(1)} %get-tuple-element.76), channel_id=1, source_target_pairs={{0,24},{4,28},{8,16},{12,20},{16,8},{20,12},{24,0},{28,4},{1,25},{... | collective-permute-start | bytes 331784 | tf_op jit(solution)/shard_map/ppermute | solution.py:716
  49.8 5.2 %collective-permute-start.19 = (f32[120,256]{1,0:T(8,128)S(1)}, f32[120,256]{1,0:T(8,128)S(1)}, u32[]{:S(2)}, u32[]{:S(2)}) collective-permute-start(f32[120,256]{1,0:T(8,128)S(1)} %get-tuple-element.85), channel_id=1, source_target_pairs={{0,1},{1,0},{2,3},{3,2},{4,5},{5,4},{6,7},{7,6},{8,9},{9,8},{10,11... | collective-permute-start | bytes 368648 | tf_op jit(solution)/shard_map/ppermute | solution.py:716
  51.8 5.0 %collective-permute-start.20 = (f32[24,192]{1,0:T(8,128)S(1)}, f32[24,192]{1,0:T(8,128)S(1)}, u32[]{:S(2)}, u32[]{:S(2)}) collective-permute-start(f32[24,192]{1,0:T(8,128)S(1)} %get-tuple-element.86), channel_id=1, source_target_pairs={{0,2},{1,3},{2,0},{3,1},{4,6},{5,7},{6,4},{7,5},{8,10},{9,11},{10,... | collective-permute-start | bytes 55304 | tf_op jit(solution)/shard_map/ppermute | solution.py:716
  52.8 5.6 %collective-permute-start.21 = (f32[24,192]{1,0:T(8,128)S(1)}, f32[24,192]{1,0:T(8,128)S(1)}, u32[]{:S(2)}, u32[]{:S(2)}) collective-permute-start(f32[24,192]{1,0:T(8,128)S(1)} %get-tuple-element.87), channel_id=1, source_target_pairs={{0,3},{1,2},{2,1},{3,0},{4,7},{5,6},{6,5},{7,4},{8,11},{9,10},{10,... | collective-permute-start | bytes 55304 | tf_op jit(solution)/shard_map/ppermute | solution.py:716
  (10 other events, 26.1 us)

commit v6 on v5

--- a/solution.py
+++ b/solution.py
@@ -450,19 +450,14 @@
         stack[...] = dbt[...].T
         for z in range(res_n):
             zi = lax.bitwise_xor(res, z)
-            for s in range(seq_n):
-                ci = lax.bitwise_xor(chip, s // 2)
-                d = z * seq_n + s
-                at = [h * n_keys + d * rows for h in range(heads)]
-                block = cat([stack[a : a + rows, :] for a in at], 0)
-
-                @pl.when(core == s % 2)
-                def _():
-                    near_ref[ci, zi] = block
-
-                @pl.when(core != s % 2)
-                def _():
-                    far_ref[ci, zi] = block
+            for pair in range(seq_n // 2):
+                ci = lax.bitwise_xor(chip, pair)
+                blocks = []
+                for s in (2 * pair, 2 * pair + 1):
+                    at = [h * n_keys + (z * seq_n + s) * rows for h in range(heads)]
+                    blocks.append(cat([stack[a : a + rows, :] for a in at], 0))
+                near_ref[ci, zi] = jnp.where(core == 0, blocks[0], blocks[1])
+                far_ref[ci, zi] = jnp.where(core == 0, blocks[1], blocks[0])
 
 
 def pair_back_kernel(
@@ -615,18 +610,14 @@
         for b in range(n_seqs):
             to = (base + b) * own
             ref[to : to + own, :] = dyall[b, pl.ds(at, own), :]
-    for s in range(seq_n):
-        ci = lax.bitwise_xor(chip, s // 2)
-        at = [h * own + s * rows for h in range(heads)]
-        block = cat([dbias[a : a + rows, :] for a in at], 0)
-
-        @pl.when(core == s % 2)
-        def _():
-            near_ref[ci] = block
-
-        @pl.when(core != s % 2)
-        def _():
-            far_ref[ci] = block
+    for pair in range(seq_n // 2):
+        ci = lax.bitwise_xor(chip, pair)
+        blocks = []
+        for s in (2 * pair, 2 * pair + 1):
+            at = [h * own + s * rows for h in range(heads)]
+            blocks.append(cat([dbias[a : a + rows, :] for a in at], 0))
+        near_ref[ci] = jnp.where(core == 0, blocks[0], blocks[1])
+        far_ref[ci] = jnp.where(core == 0, blocks[1], blocks[0])
 
 
 def aligned_back_kernel(o_ref, dq_ref, dout_ref, sig_ref, wqg_ref, r0_ref, dy_ref):

time: 60.3 us -> 59.9 us (level)
  no operation moved by 1% of the time
where the time goes in v6:
time: 59.9 us; the launch traced here: 59.6 us
  starting transfers between devices  22.5 us (38%)
  Pallas kernels  20.2 us (34%)
  waiting for transfers between devices  11.5 us (19%)
  local copies, waits for them, and re-layouts  4.49 us (7%)
  between operations  0.94 us (2%)
    ppermute x22, starting transfers between devices, swap(): return lax.ppermute(values, axis, [(i, i ^ offset) for i in range(size)])  22.5 us
    ppermute x22, waiting for transfers between devices, swap(): return lax.ppermute(values, axis, [(i, i ^ offset) for i in range(size)])  11.5 us
    pallas_call x1, Pallas kernels, fused_on_device(): pl.pallas_call(functools.partial(pair_kernel, (rows, hp, seq_n, res_n)),...  7.37 us
    unnamed x40, local copies, waits for them, and re-layouts  4.49 us
    pallas_call x1, Pallas kernels, fused_on_device(): pl.pallas_call(functools.partial(msa_kernel, (rows, hm, seq_n, res_n)), o...  2.85 us
    pallas_call x1, Pallas kernels, fused_on_device(): pl.pallas_call(functools.partial(bias_kernel, rows), out_shape=(shape(bas...  2.68 us
    pallas_call x1, Pallas kernels, fused_on_device(): pl.pallas_call(pair_project_kernel, out_shape=(bf(rows, length, 3 * feats...  1.65 us
    pallas_call x1, Pallas kernels, fused_on_device(): pl.pallas_call(pair_end_kernel, out_shape=shape(rows, length, feats), com...  1.45 us
  transfers between devices with their start and end apart: 22, of which 8 were waited for; matrix products, arithmetic and copies ran while one was open for 0% of the time, Pallas kernels for 27%

profile of v6, /device:TPU:0, one launch (start us, length us, event | category | flops | bytes accessed | tf_op | source)
XLA Modules:
  0.0 59.6 jit_solution(756281204421894968)
XLA Ops:
  0.7 2.7 %bias_rows.1 = (f32[120,256]{1,0:T(8,128)}, f32[72,128]{1,0:T(8,128)}) custom-call(f32[6,192,128]{2,1,0:T(8,128)} %x_ref.3, f32[96,256]{1,0:T(8,128)} %bitcast.17, f32[1,128]{1,0:T(1,128)} %bitcast.14, f32[4,128]{1,0:T(4,128)} %bitcast.8, f32[1,128]{1,0:T(1,128)} %bitcast.12, f32[8,128]{1,0:T(8,128)} %bitcast.6), custom_call_target="tpu_custom_call" | custom-call | tf_op jit(solution)/shard_map/bias_rows/pallas_call | solution.py:746
  3.4 4.0 %collective-permute-start.5 = (f32[72,128]{1,0:T(8,128)}, f32[72,128]{1,0:T(8,128)S(1)}, u32[]{:S(2)}, u32[]{:S(2)}) collective-permute-start(f32[72,128]{1,0:T(8,128)} %get-tuple-element.55.b0_ref), channel_id=1, source_target_pairs={{0,24},{4,28},{8,16},{12,20},{16,8},{20,12},{24,0},{28,4},{1,25},{... | collective-permute-start | bytes 110600 | tf_op jit(solution)/shard_map/ppermute | solution.py:707
  7.3 0.5 collective-permute-start.4
  8.0 4.0 %collective-permute-start.2 = (f32[120,256]{1,0:T(8,128)}, f32[120,256]{1,0:T(8,128)S(1)}, u32[]{:S(2)}, u32[]{:S(2)}) collective-permute-start(f32[120,256]{1,0:T(8,128)} %get-tuple-element.54.p0_ref.y0_ref.y_ref), channel_id=1, source_target_pairs={{0,3},{1,2},{2,1},{3,0},{4,7},{5,6},{6,5},{7,4},{8,11},{9,10},{10,... | collective-permute-start | bytes 368648 | tf_op jit(solution)/shard_map/ppermute | solution.py:707
  12.0 0.6 collective-permute-start
  12.6 1.1 %copy-done.7 = f32[6,192,128]{2,1,0:T(8,128)S(1)} copy-done((f32[6,192,128]{2,1,0:T(8,128)S(1)}, f32[6,192,128]{2,1,0:T(8,128)}, u32[]{:S(2)}) %copy-start.7) | copy-done | bytes 589848
  13.6 0.8 %copy-done.15 = f32[128,128]{1,0:T(8,128)S(1)} copy-done((f32[128,128]{1,0:T(8,128)S(1)}, f32[128,128]{1,0:T(8,128)}, u32[]{:S(2)}) %copy-start.15) | copy-done | bytes 65560
  14.5 0.8 %copy-done.16 = f32[128,128]{1,0:T(8,128)S(1)} copy-done((f32[128,128]{1,0:T(8,128)S(1)}, f32[128,128]{1,0:T(8,128)}, u32[]{:S(2)}) %copy-start.16) | copy-done | bytes 65560
  15.3 0.8 %copy-done.17 = f32[128,128]{1,0:T(8,128)S(1)} copy-done((f32[128,128]{1,0:T(8,128)S(1)}, f32[128,128]{1,0:T(8,128)}, u32[]{:S(2)}) %copy-start.17) | copy-done | bytes 65560
  16.2 0.8 %copy-done.18 = f32[128,128]{1,0:T(8,128)S(1)} copy-done((f32[128,128]{1,0:T(8,128)S(1)}, f32[128,128]{1,0:T(8,128)}, u32[]{:S(2)}) %copy-start.18) | copy-done | bytes 65560
  17.0 1.6 %pair_project.1 = (bf16[6,192,384]{2,1,0:T(8,128)(2,1)S(1)}, bf16[6,192,384]{2,1,0:T(8,128)(2,1)S(1)}, bf16[6,192,256]{2,1,0:T(8,128)(2,1)S(1)}, bf16[6,192,256]...) custom-call(f32[6,192,128]{2,1,0:T(8,128)S(1)} %copy-done, ...), custom_call_target="tpu_custom_call" | custom-call | flops 2000000000 | bytes 10000000 | tf_op jit(solution)/shard_map/pair_project/pallas_call | solution.py:771
  19.3 2.4 %collective-permute-done.1.p2_ref.y2_ref = f32[120,256]{1,0:T(8,128)S(1)} collective-permute-done((f32[120,256]{1,0:T(8,128)}, f32[120,256]{1,0:T(8,128)S(1)}, u32[]{:S(2)}, u32[]{:S(2)}) %collective-permute-start.1) | collective-permute-done | bytes 122912 | tf_op jit(solution)/shard_map/ppermute | solution.py:707
  21.8 2.5 %collective-permute-start.8 = (f32[144,128]{1,0:T(8,128)S(1)}, f32[144,128]{1,0:T(8,128)S(1)}, u32[]{:S(2)}, u32[]{:S(2)}) collective-permute-start(f32[144,128]{1,0:T(8,128)S(1)} %stack_rows.1.b0_ref), channel_id=1, source_target_pairs={{0,24},{4,28},{8,16},{12,20},{16,8},{20,12},{24,0},{28,4},{1,25},{... | collective-permute-start | bytes 221192 | tf_op jit(solution)/shard_map/ppermute | solution.py:707
  24.3 0.5 collective-permute-start.7
  24.8 0.5 collective-permute-start.6
  25.4 1.3 %msa_project.1 = (f32[96,256]{1,0:T(8,128)S(1)}, f32[96,256]{1,0:T(8,128)S(1)}, f32[96,256]{1,0:T(8,128)S(1)}, f32[96,256]{1,0:T(8,128)S(1)}, f32[384,256]{1,0:T...) custom-call(f32[120,256]{1,0:T(8,128)S(1)} %copy-done.1, ...), custom_call_target="tpu_custom_call" | custom-call | flops 1000000000 | bytes 10000000 | tf_op jit(solution)/shard_map/msa_project/pallas_call | solution.py:801
  26.7 2.9 %msa_attention.1 = (f32[96,256]{1,0:T(8,128)S(1)}, f32[96,256]{1,0:T(8,128)S(1)}, f32[96,256]{1,0:T(8,128)S(1)}, f32[96,256]{1,0:T(8,128)S(1)}, f32[192,256]{1,0...) custom-call(f32[96,256]{1,0:T(8,128)S(1)} %get-tuple-element.56.q_ref, ...), custom_call_target="tpu_custom_call" | custom-call | flops 4000000000 | bytes 10000000 | tf_op jit(solution)/shard_map/msa_attention/pallas_call | solution.py:815
  30.5 0.7 %collective-permute-done.11.b2_ref = f32[144,128]{1,0:T(8,128)S(1)} collective-permute-done((f32[144,128]{1,0:T(8,128)S(1)}, f32[144,128]{1,0:T(8,128)S(1)}, u32[]{:S(2)}, u32[]{:S(2)}) %collective-permute-start.11) | collective-permute-done | bytes 73760 | tf_op jit(solution)/shard_map/ppermute | solution.py:707
  31.3 7.4 %pair_attention.1 = (f32[6,32,768]{2,1,0:T(8,128)S(1)}, f32[6,32,768]{2,1,0:T(8,128)S(1)}, f32[6,192,128]{2,1,0:T(8,128)S(1)}, f32[6,192,128]{2,1,0:T(8,128)S(1)...) custom-call(bf16[6,192,384]{2,1,0:T(8,128)(2,1)S(1)} %get-tuple-element.48.q_ref, ...), custom_call_target="tpu_custom_call" | custom-call | flops 10000000000 | bytes 10000000 | tf_op jit(solution)/shard_map/pair_attention/pallas_call | solution.py:838
  38.9 1.3 %pair_back.1.after_ref.dn_ref = f32[6,192,128]{2,1,0:T(8,128)S(1)} custom-call(f32[6,32,768]{2,1,0:T(8,128)S(1)} %get-tuple-element.62.ot_ref, f32[6,32,768]{2,1,0:T(8,128)S(1)} %get-tuple-element.63.dqt_ref, f32[6,192,128]{2,1,0:T(8,128)S(1)} %get-tuple-element.64.dk_ref, f32[6,192,128]{2,1,0:T(8,128)S(1)} %get-tuple-element.65.dv_ref, ...), custom_call_target="tpu_custom_call" | custom-call | flops 99999997952 | bytes 100000000 | tf_op jit(solution)/shard_map/pair_back/pallas_call | solution.py:866
  40.5 1.6 %collective-permute-start.15 = (f32[216,128]{1,0:T(8,128)S(1)}, f32[216,128]{1,0:T(8,128)S(1)}, u32[]{:S(2)}, u32[]{:S(2)}) collective-permute-start(f32[216,128]{1,0:T(8,128)S(1)} %get-tuple-element.74), channel_id=1, source_target_pairs={{0,8},{4,12},{8,0},{12,4},{16,24},{20,28},{24,16},{28,20},{1,9},{5... | collective-permute-start | bytes 331784 | tf_op jit(solution)/shard_map/ppermute | solution.py:707
  42.1 1.5 %collective-permute-start.16 = (f32[216,128]{1,0:T(8,128)S(1)}, f32[216,128]{1,0:T(8,128)S(1)}, u32[]{:S(2)}, u32[]{:S(2)}) collective-permute-start(f32[216,128]{1,0:T(8,128)S(1)} %get-tuple-element.75), channel_id=1, source_target_pairs={{0,16},{4,20},{8,24},{12,28},{16,0},{20,4},{24,8},{28,12},{1,17},{... | collective-permute-start | bytes 331784 | tf_op jit(solution)/shard_map/ppermute | solution.py:707
  44.5 1.3 %collective-permute-done.15.s1_ref = f32[216,128]{1,0:T(8,128)S(1)} collective-permute-done((f32[216,128]{1,0:T(8,128)S(1)}, f32[216,128]{1,0:T(8,128)S(1)}, u32[]{:S(2)}, u32[]{:S(2)}) %collective-permute-start.15) | collective-permute-done | bytes 110624 | tf_op jit(solution)/shard_map/ppermute | solution.py:707
  45.8 3.6 %collective-permute-done.16.s2_ref = f32[216,128]{1,0:T(8,128)S(1)} collective-permute-done((f32[216,128]{1,0:T(8,128)S(1)}, f32[216,128]{1,0:T(8,128)S(1)}, u32[]{:S(2)}, u32[]{:S(2)}) %collective-permute-start.16) | collective-permute-done | bytes 110624 | tf_op jit(solution)/shard_map/ppermute | solution.py:707
  49.4 2.0 %collective-permute-start.19 = (f32[120,256]{1,0:T(8,128)S(1)}, f32[120,256]{1,0:T(8,128)S(1)}, u32[]{:S(2)}, u32[]{:S(2)}) collective-permute-start(f32[120,256]{1,0:T(8,128)S(1)} %get-tuple-element.85), channel_id=1, source_target_pairs={{0,1},{1,0},{2,3},{3,2},{4,5},{5,4},{6,7},{7,6},{8,9},{9,8},{10,11... | collective-permute-start | bytes 368648 | tf_op jit(solution)/shard_map/ppermute | solution.py:707
  51.5 1.0 %collective-permute-start.20 = (f32[24,192]{1,0:T(8,128)S(1)}, f32[24,192]{1,0:T(8,128)S(1)}, u32[]{:S(2)}, u32[]{:S(2)}) collective-permute-start(f32[24,192]{1,0:T(8,128)S(1)} %get-tuple-element.86), channel_id=1, source_target_pairs={{0,2},{1,3},{2,0},{3,1},{4,6},{5,7},{6,4},{7,5},{8,10},{9,11},{10,... | collective-permute-start | bytes 55304 | tf_op jit(solution)/shard_map/ppermute | solution.py:707
  52.5 1.4 %collective-permute-start.21 = (f32[24,192]{1,0:T(8,128)S(1)}, f32[24,192]{1,0:T(8,128)S(1)}, u32[]{:S(2)}, u32[]{:S(2)}) collective-permute-start(f32[24,192]{1,0:T(8,128)S(1)} %get-tuple-element.87), channel_id=1, source_target_pairs={{0,3},{1,2},{2,1},{3,0},{4,7},{5,6},{6,5},{7,4},{8,11},{9,10},{10,... | collective-permute-start | bytes 55304 | tf_op jit(solution)/shard_map/ppermute | solution.py:707
  53.9 0.7 %collective-permute-done.19.p1_ref.r1_ref = f32[120,256]{1,0:T(8,128)S(1)} collective-permute-done((f32[120,256]{1,0:T(8,128)S(1)}, f32[120,256]{1,0:T(8,128)S(1)}, u32[]{:S(2)}, u32[]{:S(2)}) %collective-permute-start.19) | collective-permute-done | bytes 122912 | tf_op jit(solution)/shard_map/ppermute | solution.py:707
  54.6 0.9 %aligned_end.1 = f32[2,48,256]{2,1,0:T(8,128)} custom-call(f32[120,256]{1,0:T(8,128)S(1)} %copy-done.1, f32[1,256]{1,0:T(1,128)S(1)} %bitcast.11, f32[96,256]{1,0:T(8,128)S(1)} %aligned_back.1.after_ref.dy_ref, f32[192,256]{1,0:T(8,128)S(1)} %collective-permute-done.18.r23_ref, f32[120,256]{1,0:T(8,128)S(1)} %collective-permute-done.19.p1_ref.r1_ref), custom_call_target="tpu_custom_call" | custom-call | tf_op jit(solution)/shard_map/aligned_end/pallas_call | solution.py:901
  55.5 1.0 %collective-permute-done.20.p2_ref = f32[24,192]{1,0:T(8,128)S(1)} collective-permute-done((f32[24,192]{1,0:T(8,128)S(1)}, f32[24,192]{1,0:T(8,128)S(1)}, u32[]{:S(2)}, u32[]{:S(2)}) %collective-permute-start.20) | collective-permute-done | bytes 18464 | tf_op jit(solution)/shard_map/ppermute | solution.py:707
  56.5 1.7 %collective-permute-done.21.p3_ref = f32[24,192]{1,0:T(8,128)S(1)} collective-permute-done((f32[24,192]{1,0:T(8,128)S(1)}, f32[24,192]{1,0:T(8,128)S(1)}, u32[]{:S(2)}, u32[]{:S(2)}) %collective-permute-start.21) | collective-permute-done | bytes 18464 | tf_op jit(solution)/shard_map/ppermute | solution.py:707
  58.1 1.4 %pair_end.1 = f32[6,192,128]{2,1,0:T(8,128)} custom-call(f32[6,192,128]{2,1,0:T(8,128)S(1)} %get-tuple-element.46.after_ref.n_ref, f32[6,192,128]{2,1,0:T(8,128)S(1)} %get-tuple-element.47.scale_ref, f32[6,192,128]{2,1,0:T(8,128)S(1)} %pair_back.1.after_ref.dn_ref, f32[24,192]{1,0:T(8,128)S(1)} %get-tuple-element.84.p0_ref, ...), custom_call_target="tpu_custom_call" | custom-call | tf_op jit(solution)/shard_map/pair_end/pallas_call | solution.py:907
  (66 shorter events, 3.4 us)
Async XLA Ops:
  0.6 11.9 %copy-start = (f32[6,192,128]{2,1,0:T(8,128)S(1)}, f32[6,192,128]{2,1,0:T(8,128)}, u32[]{:S(2)}) copy-start(f32[6,192,128]{2,1,0:T(8,128)} %x_ref.3) | copy-start | bytes 1769476
  0.6 11.9 %copy-start.2 = (f32[128,8]{0,1:T(8,128)S(1)}, f32[128,8]{0,1:T(8,128)}, u32[]{:S(2)}) copy-start(f32[128,8]{0,1:T(8,128)} %param.36) | copy-start | bytes 12292
  0.7 11.9 %copy-start.14 = (f32[128,128]{1,0:T(8,128)S(1)}, f32[128,128]{1,0:T(8,128)}, u32[]{:S(2)}) copy-start(f32[128,128]{1,0:T(8,128)} %wq_ref.2) | copy-start | bytes 196612
  3.3 9.2 %copy-start.3 = (f32[128,4]{0,1:T(4,128)S(1)}, f32[128,4]{0,1:T(4,128)}, u32[]{:S(2)}) copy-start(f32[128,4]{0,1:T(4,128)} %param.28) | copy-start | bytes 6148
  3.3 9.2 %copy-start.5 = (f32[128]{0:T(128)S(1)}, f32[128]{0:T(128)}, u32[]{:S(2)}) copy-start(f32[128]{0:T(128)} %param.31) | copy-start | bytes 1540
  3.3 9.2 %copy-start.6 = (f32[128]{0:T(128)S(1)}, f32[128]{0:T(128)}, u32[]{:S(2)}) copy-start(f32[128]{0:T(128)} %param.23) | copy-start | bytes 1540
  3.4 8.6 %collective-permute-start.5 = (f32[72,128]{1,0:T(8,128)}, f32[72,128]{1,0:T(8,128)S(1)}, u32[]{:S(2)}, u32[]{:S(2)}) collective-permute-start(f32[72,128]{1,0:T(8,128)} %get-tuple-element.55.b0_ref), channel_id=1, source_target_pairs={{0,24},{4,28},{8,16},{12,20},{16,8},{20,12},{24,0},{28,4},{1,25},{... | collective-permute-start | bytes 110600 | tf_op jit(solution)/shard_map/ppermute | solution.py:707
  7.3 11.3 %collective-permute-start.4 = (f32[72,128]{1,0:T(8,128)}, f32[72,128]{1,0:T(8,128)S(1)}, u32[]{:S(2)}, u32[]{:S(2)}) collective-permute-start(f32[72,128]{1,0:T(8,128)} %get-tuple-element.55.b0_ref), channel_id=1, source_target_pairs={{0,16},{4,20},{8,24},{12,28},{16,0},{20,4},{24,8},{28,12},{1,17},{... | collective-permute-start | bytes 110600 | tf_op jit(solution)/shard_map/ppermute | solution.py:707
  7.8 10.8 %collective-permute-start.3 = (f32[72,128]{1,0:T(8,128)}, f32[72,128]{1,0:T(8,128)S(1)}, u32[]{:S(2)}, u32[]{:S(2)}) collective-permute-start(f32[72,128]{1,0:T(8,128)} %get-tuple-element.55.b0_ref), channel_id=1, source_target_pairs={{0,8},{4,12},{8,0},{12,4},{16,24},{20,28},{24,16},{28,20},{1,9},{5... | collective-permute-start | bytes 110600 | tf_op jit(solution)/shard_map/ppermute | solution.py:707
  8.0 11.4 %collective-permute-start.2 = (f32[120,256]{1,0:T(8,128)}, f32[120,256]{1,0:T(8,128)S(1)}, u32[]{:S(2)}, u32[]{:S(2)}) collective-permute-start(f32[120,256]{1,0:T(8,128)} %get-tuple-element.54.p0_ref.y0_ref.y_ref), channel_id=1, source_target_pairs={{0,3},{1,2},{2,1},{3,0},{4,7},{5,6},{6,5},{7,4},{8,11},{9,10},{10,... | collective-permute-start | bytes 368648 | tf_op jit(solution)/shard_map/ppermute | solution.py:707
  12.0 9.7 %collective-permute-start.1 = (f32[120,256]{1,0:T(8,128)}, f32[120,256]{1,0:T(8,128)S(1)}, u32[]{:S(2)}, u32[]{:S(2)}) collective-permute-start(f32[120,256]{1,0:T(8,128)} %get-tuple-element.54.p0_ref.y0_ref.y_ref), channel_id=1, source_target_pairs={{0,2},{1,3},{2,0},{3,1},{4,6},{5,7},{6,4},{7,5},{8,10},{9,11},{10,... | collective-permute-start | bytes 368648 | tf_op jit(solution)/shard_map/ppermute | solution.py:707
  12.0 9.7 %collective-permute-start = (f32[120,256]{1,0:T(8,128)}, f32[120,256]{1,0:T(8,128)S(1)}, u32[]{:S(2)}, u32[]{:S(2)}) collective-permute-start(f32[120,256]{1,0:T(8,128)} %get-tuple-element.54.p0_ref.y0_ref.y_ref), channel_id=1, source_target_pairs={{0,1},{1,0},{2,3},{3,2},{4,5},{5,4},{6,7},{7,6},{8,9},{9,8},{10,11... | collective-permute-start | bytes 368648 | tf_op jit(solution)/shard_map/ppermute | solution.py:707
  17.0 8.3 %copy-start.13 = (f32[2,48,256]{2,1,0:T(8,128)S(1)}, f32[2,48,256]{2,1,0:T(8,128)}, u32[]{:S(2)}) copy-start(f32[2,48,256]{2,1,0:T(8,128)} %adj_ref.3) | copy-start | bytes 294916
  18.7 6.6 %copy-start.10 = (f32[256,256]{1,0:T(8,128)S(1)}, f32[256,256]{1,0:T(8,128)}, u32[]{:S(2)}) copy-start(f32[256,256]{1,0:T(8,128)} %wv_ref.3) | copy-start | bytes 786436
  18.7 6.6 %copy-start.11 = (f32[256,256]{1,0:T(8,128)S(1)}, f32[256,256]{1,0:T(8,128)}, u32[]{:S(2)}) copy-start(f32[256,256]{1,0:T(8,128)} %wg_ref.3) | copy-start | bytes 786436
  18.7 6.6 %copy-start.12 = (f32[256,256]{1,0:T(8,128)S(1)}, f32[256,256]{1,0:T(8,128)}, u32[]{:S(2)}) copy-start(f32[256,256]{1,0:T(8,128)} %wo_ref.3) | copy-start | bytes 786436
  18.8 7.9 %collective-permute-start.10 = (f32[3,72,128]{2,1,0:T(8,128)S(1)}, f32[3,72,128]{2,1,0:T(8,128)S(1)}, u32[]{:S(2)}, u32[]{:S(2)}) collective-permute-start(f32[3,72,128]{2,1,0:T(8,128)S(1)} %stack_chips.2.after_ref.b1_ref), channel_id=1, source_target_pairs={{0,4},{4,0},{8,12},{12,8},{16,20},{20,16},{24,28},{28,24},{1,5},{5... | collective-permute-start | bytes 331784 | tf_op jit(solution)/shard_map/ppermute | solution.py:707
  18.9 7.8 %collective-permute-start.9 = (f32[72,128]{1,0:T(8,128)S(1)}, f32[72,128]{1,0:T(8,128)S(1)}, u32[]{:S(2)}, u32[]{:S(2)}) collective-permute-start(f32[72,128]{1,0:T(8,128)S(1)} %copy-done.19), channel_id=1, source_target_pairs={{0,4},{4,0},{8,12},{12,8},{16,20},{20,16},{24,28},{28,24},{1,5},{5... | collective-permute-start | bytes 110600 | tf_op jit(solution)/shard_map/ppermute | solution.py:707
  21.8 7.8 %collective-permute-start.8 = (f32[144,128]{1,0:T(8,128)S(1)}, f32[144,128]{1,0:T(8,128)S(1)}, u32[]{:S(2)}, u32[]{:S(2)}) collective-permute-start(f32[144,128]{1,0:T(8,128)S(1)} %stack_rows.1.b0_ref), channel_id=1, source_target_pairs={{0,24},{4,28},{8,16},{12,20},{16,8},{20,12},{24,0},{28,4},{1,25},{... | collective-permute-start | bytes 221192 | tf_op jit(solution)/shard_map/ppermute | solution.py:707
  24.3 5.3 %collective-permute-start.7 = (f32[144,128]{1,0:T(8,128)S(1)}, f32[144,128]{1,0:T(8,128)S(1)}, u32[]{:S(2)}, u32[]{:S(2)}) collective-permute-start(f32[144,128]{1,0:T(8,128)S(1)} %stack_rows.1.b0_ref), channel_id=1, source_target_pairs={{0,16},{4,20},{8,24},{12,28},{16,0},{20,4},{24,8},{28,12},{1,17},{... | collective-permute-start | bytes 221192 | tf_op jit(solution)/shard_map/ppermute | solution.py:707
  24.8 4.8 %collective-permute-start.6 = (f32[144,128]{1,0:T(8,128)S(1)}, f32[144,128]{1,0:T(8,128)S(1)}, u32[]{:S(2)}, u32[]{:S(2)}) collective-permute-start(f32[144,128]{1,0:T(8,128)S(1)} %stack_rows.1.b0_ref), channel_id=1, source_target_pairs={{0,8},{4,12},{8,0},{12,4},{16,24},{20,28},{24,16},{28,20},{1,9},{5... | collective-permute-start | bytes 221192 | tf_op jit(solution)/shard_map/ppermute | solution.py:707
  29.6 1.7 %collective-permute-start.12 = (f32[3,144,128]{2,1,0:T(8,128)S(1)}, f32[3,144,128]{2,1,0:T(8,128)S(1)}, u32[]{:S(2)}, u32[]{:S(2)}) collective-permute-start(f32[3,144,128]{2,1,0:T(8,128)S(1)} %stack_chips.3.b1_ref), channel_id=1, source_target_pairs={{0,4},{4,0},{8,12},{12,8},{16,20},{20,16},{24,28},{28,24},{1,5},{5... | collective-permute-start | bytes 663560 | tf_op jit(solution)/shard_map/ppermute | solution.py:707
  29.7 1.6 %collective-permute-start.11 = (f32[144,128]{1,0:T(8,128)S(1)}, f32[144,128]{1,0:T(8,128)S(1)}, u32[]{:S(2)}, u32[]{:S(2)}) collective-permute-start(f32[144,128]{1,0:T(8,128)S(1)} %stack_rows.1.b0_ref), channel_id=1, source_target_pairs={{0,4},{4,0},{8,12},{12,8},{16,20},{20,16},{24,28},{28,24},{1,5},{5... | collective-permute-start | bytes 221192 | tf_op jit(solution)/shard_map/ppermute | solution.py:707
  30.2 10.0 %collective-permute-start.14 = (f32[4,48,192]{2,1,0:T(8,128)S(1)}, f32[4,48,192]{2,1,0:T(8,128)S(1)}, u32[]{:S(2)}, u32[]{:S(2)}) collective-permute-start(f32[4,48,192]{2,1,0:T(8,128)S(1)} %get-tuple-element.72), channel_id=1, source_target_pairs={{0,4},{4,0},{8,12},{12,8},{16,20},{20,16},{24,28},{28,24},{1,5},{5... | collective-permute-start | bytes 442376 | tf_op jit(solution)/shard_map/ppermute | solution.py:707
  30.3 14.2 %collective-permute-start.18 = (f32[192,256]{1,0:T(8,128)S(1)}, f32[192,256]{1,0:T(8,128)S(1)}, u32[]{:S(2)}, u32[]{:S(2)}) collective-permute-start(f32[192,256]{1,0:T(8,128)S(1)} %get-tuple-element.78), channel_id=1, source_target_pairs={{0,2},{1,3},{2,0},{3,1},{4,6},{5,7},{6,4},{7,5},{8,10},{9,11},{10,... | collective-permute-start | bytes 589832 | tf_op jit(solution)/shard_map/ppermute | solution.py:707
  38.6 1.8 %collective-permute-start.13 = (f32[4,4,24,192]{3,2,1,0:T(8,128)S(1)}, f32[4,4,24,192]{3,2,1,0:T(8,128)S(1)}, u32[]{:S(2)}, u32[]{:S(2)}) collective-permute-start(f32[4,4,24,192]{3,2,1,0:T(8,128)S(1)} %get-tuple-element.70), channel_id=1, source_target_pairs={{0,4},{4,0},{8,12},{12,8},{16,20},{20,16},{24,28},{28,24},{1,5},{5... | collective-permute-start | bytes 884744 | tf_op jit(solution)/shard_map/ppermute | solution.py:707
  40.5 5.2 %collective-permute-start.15 = (f32[216,128]{1,0:T(8,128)S(1)}, f32[216,128]{1,0:T(8,128)S(1)}, u32[]{:S(2)}, u32[]{:S(2)}) collective-permute-start(f32[216,128]{1,0:T(8,128)S(1)} %get-tuple-element.74), channel_id=1, source_target_pairs={{0,8},{4,12},{8,0},{12,4},{16,24},{20,28},{24,16},{28,20},{1,9},{5... | collective-permute-start | bytes 331784 | tf_op jit(solution)/shard_map/ppermute | solution.py:707
  42.1 7.2 %collective-permute-start.16 = (f32[216,128]{1,0:T(8,128)S(1)}, f32[216,128]{1,0:T(8,128)S(1)}, u32[]{:S(2)}, u32[]{:S(2)}) collective-permute-start(f32[216,128]{1,0:T(8,128)S(1)} %get-tuple-element.75), channel_id=1, source_target_pairs={{0,16},{4,20},{8,24},{12,28},{16,0},{20,4},{24,8},{28,12},{1,17},{... | collective-permute-start | bytes 331784 | tf_op jit(solution)/shard_map/ppermute | solution.py:707
  43.6 5.7 %collective-permute-start.17 = (f32[216,128]{1,0:T(8,128)S(1)}, f32[216,128]{1,0:T(8,128)S(1)}, u32[]{:S(2)}, u32[]{:S(2)}) collective-permute-start(f32[216,128]{1,0:T(8,128)S(1)} %get-tuple-element.76), channel_id=1, source_target_pairs={{0,24},{4,28},{8,16},{12,20},{16,8},{20,12},{24,0},{28,4},{1,25},{... | collective-permute-start | bytes 331784 | tf_op jit(solution)/shard_map/ppermute | solution.py:707
  49.4 5.2 %collective-permute-start.19 = (f32[120,256]{1,0:T(8,128)S(1)}, f32[120,256]{1,0:T(8,128)S(1)}, u32[]{:S(2)}, u32[]{:S(2)}) collective-permute-start(f32[120,256]{1,0:T(8,128)S(1)} %get-tuple-element.85), channel_id=1, source_target_pairs={{0,1},{1,0},{2,3},{3,2},{4,5},{5,4},{6,7},{7,6},{8,9},{9,8},{10,11... | collective-permute-start | bytes 368648 | tf_op jit(solution)/shard_map/ppermute | solution.py:707
  51.5 5.0 %collective-permute-start.20 = (f32[24,192]{1,0:T(8,128)S(1)}, f32[24,192]{1,0:T(8,128)S(1)}, u32[]{:S(2)}, u32[]{:S(2)}) collective-permute-start(f32[24,192]{1,0:T(8,128)S(1)} %get-tuple-element.86), channel_id=1, source_target_pairs={{0,2},{1,3},{2,0},{3,1},{4,6},{5,7},{6,4},{7,5},{8,10},{9,11},{10,... | collective-permute-start | bytes 55304 | tf_op jit(solution)/shard_map/ppermute | solution.py:707
  52.5 5.6 %collective-permute-start.21 = (f32[24,192]{1,0:T(8,128)S(1)}, f32[24,192]{1,0:T(8,128)S(1)}, u32[]{:S(2)}, u32[]{:S(2)}) collective-permute-start(f32[24,192]{1,0:T(8,128)S(1)} %get-tuple-element.87), channel_id=1, source_target_pairs={{0,3},{1,2},{2,1},{3,0},{4,7},{5,6},{6,5},{7,4},{8,11},{9,10},{10,... | collective-permute-start | bytes 55304 | tf_op jit(solution)/shard_map/ppermute | solution.py:707
  (10 other events, 26.1 us)

commit v7 on v6

--- a/solution.py
+++ b/solution.py
@@ -677,7 +677,7 @@
 
 
 def pair_end_kernel(
-    n_ref, scale_ref, dn_ref, p0_ref, p1_ref, p2_ref, p3_ref, m_ref, wj_ref, out_ref
+    n_ref, scale_ref, dn_ref, p0_ref, p1_ref, p2_ref, p3_ref, m_ref, wj_ref, out_hbm, out_ref, sem
 ):
     rows, length, feats = n_ref.shape
     lines = p0_ref.shape[0]
@@ -687,9 +687,16 @@
     pad = jnp.zeros((LANES - pair.shape[0] - msa.shape[0], length), F32)
     b = cat([pair, msa, pad], 0).T
     more = nn(cat(left3(split2(b)), 1), wj_ref[...])
+    copies = []
     for j in range(rows):
         dn = dn_ref[j] + more[:, j * feats : (j + 1) * feats]
         out_ref[j] = normed_back(n_ref[j], scale_ref[j], dn)
+        if j % 2 == 1 or j == rows - 1:
+            span = pl.ds(j - j % 2, j % 2 + 1)
+            copies.append(pltpu.make_async_copy(out_ref.at[span], out_hbm.at[span], sem.at[j // 2]))
+            copies[-1].start()
+    for copy in copies:
+        copy.wait()
 
 
 MIB = 1 << 20
@@ -906,7 +913,12 @@
     )(mixed_rows, wide_gain, dy, r23, mixed_sum)
     coupled_out = pl.pallas_call(
         pair_end_kernel,
+        in_specs=vmem(9),
+        out_specs=pl.BlockSpec(memory_space=pl.ANY),
         out_shape=shape(rows, length, feats),
+        scratch_shapes=[
+            pltpu.VMEM((rows, length, feats), F32), pltpu.SemaphoreType.DMA((-(-rows // 2),)),
+        ],
         compiler_params=params(16),
         name="pair_end",
     )(n, scale, dn, c0, mixed_sum, c2, c3, msa_sum, wj)

time: 59.9 us -> 60 us (level)
  no operation moved by 1% of the time
where the time goes in v7:
time: 60 us; the launch traced here: 59.7 us
  starting transfers between devices  22.5 us (38%)
  Pallas kernels  20.1 us (34%)
  waiting for transfers between devices  11.5 us (19%)
  local copies, waits for them, and re-layouts  4.49 us (7%)
  between operations  1.1 us (2%)
    ppermute x22, starting transfers between devices, swap(): return lax.ppermute(values, axis, [(i, i ^ offset) for i in range(size)])  22.5 us
    ppermute x22, waiting for transfers between devices, swap(): return lax.ppermute(values, axis, [(i, i ^ offset) for i in range(size)])  11.5 us
    pallas_call x1, Pallas kernels, fused_on_device(): pl.pallas_call(functools.partial(pair_kernel, (rows, hp, seq_n, res_n)),...  7.37 us
    unnamed x40, local copies, waits for them, and re-layouts  4.49 us
    pallas_call x1, Pallas kernels, fused_on_device(): pl.pallas_call(functools.partial(msa_kernel, (rows, hm, seq_n, res_n)), o...  2.85 us
    pallas_call x1, Pallas kernels, fused_on_device(): pl.pallas_call(functools.partial(bias_kernel, rows), out_shape=(shape(bas...  2.68 us
    pallas_call x1, Pallas kernels, fused_on_device(): pl.pallas_call(pair_project_kernel, out_shape=(bf(rows, length, 3 * feats...  1.65 us
    pallas_call x1, Pallas kernels, fused_on_device(): pl.pallas_call(pair_end_kernel, in_specs=vmem(9), out_specs=pl.BlockSpec(...  1.37 us
  transfers between devices with their start and end apart: 22, of which 8 were waited for; matrix products, arithmetic and copies ran while one was open for 0% of the time, Pallas kernels for 27%

profile of v7, /device:TPU:0, one launch (start us, length us, event | category | flops | bytes accessed | tf_op | source)
XLA Modules:
  0.0 59.7 jit_solution(14360196616443663139)
XLA Ops:
  0.7 2.7 %bias_rows.1 = (f32[120,256]{1,0:T(8,128)}, f32[72,128]{1,0:T(8,128)}) custom-call(f32[6,192,128]{2,1,0:T(8,128)} %x_ref.3, f32[96,256]{1,0:T(8,128)} %bitcast.17, f32[1,128]{1,0:T(1,128)} %bitcast.14, f32[4,128]{1,0:T(4,128)} %bitcast.8, f32[1,128]{1,0:T(1,128)} %bitcast.12, f32[8,128]{1,0:T(8,128)} %bitcast.6), custom_call_target="tpu_custom_call" | custom-call | tf_op jit(solution)/shard_map/bias_rows/pallas_call | solution.py:753
  3.4 4.0 %collective-permute-start.5 = (f32[72,128]{1,0:T(8,128)}, f32[72,128]{1,0:T(8,128)S(1)}, u32[]{:S(2)}, u32[]{:S(2)}) collective-permute-start(f32[72,128]{1,0:T(8,128)} %get-tuple-element.55.b0_ref), channel_id=1, source_target_pairs={{0,24},{4,28},{8,16},{12,20},{16,8},{20,12},{24,0},{28,4},{1,25},{... | collective-permute-start | bytes 110600 | tf_op jit(solution)/shard_map/ppermute | solution.py:714
  7.3 0.5 collective-permute-start.4
  8.0 4.0 %collective-permute-start.2 = (f32[120,256]{1,0:T(8,128)}, f32[120,256]{1,0:T(8,128)S(1)}, u32[]{:S(2)}, u32[]{:S(2)}) collective-permute-start(f32[120,256]{1,0:T(8,128)} %get-tuple-element.54.p0_ref.y0_ref.y_ref), channel_id=1, source_target_pairs={{0,3},{1,2},{2,1},{3,0},{4,7},{5,6},{6,5},{7,4},{8,11},{9,10},{10,... | collective-permute-start | bytes 368648 | tf_op jit(solution)/shard_map/ppermute | solution.py:714
  12.0 0.6 collective-permute-start
  12.6 1.1 %copy-done.7 = f32[6,192,128]{2,1,0:T(8,128)S(1)} copy-done((f32[6,192,128]{2,1,0:T(8,128)S(1)}, f32[6,192,128]{2,1,0:T(8,128)}, u32[]{:S(2)}) %copy-start.7) | copy-done | bytes 589848
  13.6 0.8 %copy-done.15 = f32[128,128]{1,0:T(8,128)S(1)} copy-done((f32[128,128]{1,0:T(8,128)S(1)}, f32[128,128]{1,0:T(8,128)}, u32[]{:S(2)}) %copy-start.15) | copy-done | bytes 65560
  14.5 0.8 %copy-done.16 = f32[128,128]{1,0:T(8,128)S(1)} copy-done((f32[128,128]{1,0:T(8,128)S(1)}, f32[128,128]{1,0:T(8,128)}, u32[]{:S(2)}) %copy-start.16) | copy-done | bytes 65560
  15.3 0.8 %copy-done.17 = f32[128,128]{1,0:T(8,128)S(1)} copy-done((f32[128,128]{1,0:T(8,128)S(1)}, f32[128,128]{1,0:T(8,128)}, u32[]{:S(2)}) %copy-start.17) | copy-done | bytes 65560
  16.2 0.8 %copy-done.18 = f32[128,128]{1,0:T(8,128)S(1)} copy-done((f32[128,128]{1,0:T(8,128)S(1)}, f32[128,128]{1,0:T(8,128)}, u32[]{:S(2)}) %copy-start.18) | copy-done | bytes 65560
  17.0 1.6 %pair_project.1 = (bf16[6,192,384]{2,1,0:T(8,128)(2,1)S(1)}, bf16[6,192,384]{2,1,0:T(8,128)(2,1)S(1)}, bf16[6,192,256]{2,1,0:T(8,128)(2,1)S(1)}, bf16[6,192,256]...) custom-call(f32[6,192,128]{2,1,0:T(8,128)S(1)} %copy-done, ...), custom_call_target="tpu_custom_call" | custom-call | flops 2000000000 | bytes 10000000 | tf_op jit(solution)/shard_map/pair_project/pallas_call | solution.py:778
  19.3 2.4 %collective-permute-done.1.p2_ref.y2_ref = f32[120,256]{1,0:T(8,128)S(1)} collective-permute-done((f32[120,256]{1,0:T(8,128)}, f32[120,256]{1,0:T(8,128)S(1)}, u32[]{:S(2)}, u32[]{:S(2)}) %collective-permute-start.1) | collective-permute-done | bytes 122912 | tf_op jit(solution)/shard_map/ppermute | solution.py:714
  21.8 2.5 %collective-permute-start.8 = (f32[144,128]{1,0:T(8,128)S(1)}, f32[144,128]{1,0:T(8,128)S(1)}, u32[]{:S(2)}, u32[]{:S(2)}) collective-permute-start(f32[144,128]{1,0:T(8,128)S(1)} %stack_rows.1.b0_ref), channel_id=1, source_target_pairs={{0,24},{4,28},{8,16},{12,20},{16,8},{20,12},{24,0},{28,4},{1,25},{... | collective-permute-start | bytes 221192 | tf_op jit(solution)/shard_map/ppermute | solution.py:714
  24.3 0.5 collective-permute-start.7
  24.8 0.5 collective-permute-start.6
  25.4 1.3 %msa_project.1 = (f32[96,256]{1,0:T(8,128)S(1)}, f32[96,256]{1,0:T(8,128)S(1)}, f32[96,256]{1,0:T(8,128)S(1)}, f32[96,256]{1,0:T(8,128)S(1)}, f32[384,256]{1,0:T...) custom-call(f32[120,256]{1,0:T(8,128)S(1)} %copy-done.1, ...), custom_call_target="tpu_custom_call" | custom-call | flops 1000000000 | bytes 10000000 | tf_op jit(solution)/shard_map/msa_project/pallas_call | solution.py:808
  26.7 2.9 %msa_attention.1 = (f32[96,256]{1,0:T(8,128)S(1)}, f32[96,256]{1,0:T(8,128)S(1)}, f32[96,256]{1,0:T(8,128)S(1)}, f32[96,256]{1,0:T(8,128)S(1)}, f32[192,256]{1,0...) custom-call(f32[96,256]{1,0:T(8,128)S(1)} %get-tuple-element.56.q_ref, ...), custom_call_target="tpu_custom_call" | custom-call | flops 4000000000 | bytes 10000000 | tf_op jit(solution)/shard_map/msa_attention/pallas_call | solution.py:822
  30.5 0.7 %collective-permute-done.11.b2_ref = f32[144,128]{1,0:T(8,128)S(1)} collective-permute-done((f32[144,128]{1,0:T(8,128)S(1)}, f32[144,128]{1,0:T(8,128)S(1)}, u32[]{:S(2)}, u32[]{:S(2)}) %collective-permute-start.11) | collective-permute-done | bytes 73760 | tf_op jit(solution)/shard_map/ppermute | solution.py:714
  31.3 7.4 %pair_attention.1 = (f32[6,32,768]{2,1,0:T(8,128)S(1)}, f32[6,32,768]{2,1,0:T(8,128)S(1)}, f32[6,192,128]{2,1,0:T(8,128)S(1)}, f32[6,192,128]{2,1,0:T(8,128)S(1)...) custom-call(bf16[6,192,384]{2,1,0:T(8,128)(2,1)S(1)} %get-tuple-element.48.q_ref, ...), custom_call_target="tpu_custom_call" | custom-call | flops 10000000000 | bytes 10000000 | tf_op jit(solution)/shard_map/pair_attention/pallas_call | solution.py:845
  38.9 1.3 %pair_back.1.after_ref.dn_ref = f32[6,192,128]{2,1,0:T(8,128)S(1)} custom-call(f32[6,32,768]{2,1,0:T(8,128)S(1)} %get-tuple-element.62.ot_ref, f32[6,32,768]{2,1,0:T(8,128)S(1)} %get-tuple-element.63.dqt_ref, f32[6,192,128]{2,1,0:T(8,128)S(1)} %get-tuple-element.64.dk_ref, f32[6,192,128]{2,1,0:T(8,128)S(1)} %get-tuple-element.65.dv_ref, ...), custom_call_target="tpu_custom_call" | custom-call | flops 99999997952 | bytes 100000000 | tf_op jit(solution)/shard_map/pair_back/pallas_call | solution.py:873
  40.5 1.6 %collective-permute-start.15 = (f32[216,128]{1,0:T(8,128)S(1)}, f32[216,128]{1,0:T(8,128)S(1)}, u32[]{:S(2)}, u32[]{:S(2)}) collective-permute-start(f32[216,128]{1,0:T(8,128)S(1)} %get-tuple-element.74), channel_id=1, source_target_pairs={{0,8},{4,12},{8,0},{12,4},{16,24},{20,28},{24,16},{28,20},{1,9},{5... | collective-permute-start | bytes 331784 | tf_op jit(solution)/shard_map/ppermute | solution.py:714
  42.1 1.5 %collective-permute-start.16 = (f32[216,128]{1,0:T(8,128)S(1)}, f32[216,128]{1,0:T(8,128)S(1)}, u32[]{:S(2)}, u32[]{:S(2)}) collective-permute-start(f32[216,128]{1,0:T(8,128)S(1)} %get-tuple-element.75), channel_id=1, source_target_pairs={{0,16},{4,20},{8,24},{12,28},{16,0},{20,4},{24,8},{28,12},{1,17},{... | collective-permute-start | bytes 331784 | tf_op jit(solution)/shard_map/ppermute | solution.py:714
  44.5 1.3 %collective-permute-done.15.s1_ref = f32[216,128]{1,0:T(8,128)S(1)} collective-permute-done((f32[216,128]{1,0:T(8,128)S(1)}, f32[216,128]{1,0:T(8,128)S(1)}, u32[]{:S(2)}, u32[]{:S(2)}) %collective-permute-start.15) | collective-permute-done | bytes 110624 | tf_op jit(solution)/shard_map/ppermute | solution.py:714
  45.8 3.6 %collective-permute-done.16.s2_ref = f32[216,128]{1,0:T(8,128)S(1)} collective-permute-done((f32[216,128]{1,0:T(8,128)S(1)}, f32[216,128]{1,0:T(8,128)S(1)}, u32[]{:S(2)}, u32[]{:S(2)}) %collective-permute-start.16) | collective-permute-done | bytes 110624 | tf_op jit(solution)/shard_map/ppermute | solution.py:714
  49.4 2.0 %collective-permute-start.19 = (f32[120,256]{1,0:T(8,128)S(1)}, f32[120,256]{1,0:T(8,128)S(1)}, u32[]{:S(2)}, u32[]{:S(2)}) collective-permute-start(f32[120,256]{1,0:T(8,128)S(1)} %get-tuple-element.85), channel_id=1, source_target_pairs={{0,1},{1,0},{2,3},{3,2},{4,5},{5,4},{6,7},{7,6},{8,9},{9,8},{10,11... | collective-permute-start | bytes 368648 | tf_op jit(solution)/shard_map/ppermute | solution.py:714
  51.5 1.0 %collective-permute-start.20 = (f32[24,192]{1,0:T(8,128)S(1)}, f32[24,192]{1,0:T(8,128)S(1)}, u32[]{:S(2)}, u32[]{:S(2)}) collective-permute-start(f32[24,192]{1,0:T(8,128)S(1)} %get-tuple-element.86), channel_id=1, source_target_pairs={{0,2},{1,3},{2,0},{3,1},{4,6},{5,7},{6,4},{7,5},{8,10},{9,11},{10,... | collective-permute-start | bytes 55304 | tf_op jit(solution)/shard_map/ppermute | solution.py:714
  52.5 1.4 %collective-permute-start.21 = (f32[24,192]{1,0:T(8,128)S(1)}, f32[24,192]{1,0:T(8,128)S(1)}, u32[]{:S(2)}, u32[]{:S(2)}) collective-permute-start(f32[24,192]{1,0:T(8,128)S(1)} %get-tuple-element.87), channel_id=1, source_target_pairs={{0,3},{1,2},{2,1},{3,0},{4,7},{5,6},{6,5},{7,4},{8,11},{9,10},{10,... | collective-permute-start | bytes 55304 | tf_op jit(solution)/shard_map/ppermute | solution.py:714
  53.9 0.7 %collective-permute-done.19.p1_ref.r1_ref = f32[120,256]{1,0:T(8,128)S(1)} collective-permute-done((f32[120,256]{1,0:T(8,128)S(1)}, f32[120,256]{1,0:T(8,128)S(1)}, u32[]{:S(2)}, u32[]{:S(2)}) %collective-permute-start.19) | collective-permute-done | bytes 122912 | tf_op jit(solution)/shard_map/ppermute | solution.py:714
  54.6 0.9 %aligned_end.1 = f32[2,48,256]{2,1,0:T(8,128)} custom-call(f32[120,256]{1,0:T(8,128)S(1)} %copy-done.1, f32[1,256]{1,0:T(1,128)S(1)} %bitcast.11, f32[96,256]{1,0:T(8,128)S(1)} %aligned_back.1.after_ref.dy_ref, f32[192,256]{1,0:T(8,128)S(1)} %collective-permute-done.18.r23_ref, f32[120,256]{1,0:T(8,128)S(1)} %collective-permute-done.19.p1_ref.r1_ref), custom_call_target="tpu_custom_call" | custom-call | tf_op jit(solution)/shard_map/aligned_end/pallas_call | solution.py:908
  55.5 1.0 %collective-permute-done.20.p2_ref = f32[24,192]{1,0:T(8,128)S(1)} collective-permute-done((f32[24,192]{1,0:T(8,128)S(1)}, f32[24,192]{1,0:T(8,128)S(1)}, u32[]{:S(2)}, u32[]{:S(2)}) %collective-permute-start.20) | collective-permute-done | bytes 18464 | tf_op jit(solution)/shard_map/ppermute | solution.py:714
  56.5 1.7 %collective-permute-done.21.p3_ref = f32[24,192]{1,0:T(8,128)S(1)} collective-permute-done((f32[24,192]{1,0:T(8,128)S(1)}, f32[24,192]{1,0:T(8,128)S(1)}, u32[]{:S(2)}, u32[]{:S(2)}) %collective-permute-start.21) | collective-permute-done | bytes 18464 | tf_op jit(solution)/shard_map/ppermute | solution.py:714
  58.1 1.4 %pair_end.1 = f32[6,192,128]{2,1,0:T(8,128)} custom-call(f32[6,192,128]{2,1,0:T(8,128)S(1)} %get-tuple-element.46.after_ref.n_ref, f32[6,192,128]{2,1,0:T(8,128)S(1)} %get-tuple-element.47.scale_ref, f32[6,192,128]{2,1,0:T(8,128)S(1)} %pair_back.1.after_ref.dn_ref, f32[24,192]{1,0:T(8,128)S(1)} %get-tuple-element.84.p0_ref, ...), custom_call_target="tpu_custom_call" | custom-call | tf_op jit(solution)/shard_map/pair_end/pallas_call | solution.py:914
  (66 shorter events, 3.4 us)
Async XLA Ops:
  0.6 11.9 %copy-start = (f32[6,192,128]{2,1,0:T(8,128)S(1)}, f32[6,192,128]{2,1,0:T(8,128)}, u32[]{:S(2)}) copy-start(f32[6,192,128]{2,1,0:T(8,128)} %x_ref.3) | copy-start | bytes 1769476
  0.6 11.9 %copy-start.2 = (f32[128,8]{0,1:T(8,128)S(1)}, f32[128,8]{0,1:T(8,128)}, u32[]{:S(2)}) copy-start(f32[128,8]{0,1:T(8,128)} %param.36) | copy-start | bytes 12292
  0.7 11.9 %copy-start.14 = (f32[128,128]{1,0:T(8,128)S(1)}, f32[128,128]{1,0:T(8,128)}, u32[]{:S(2)}) copy-start(f32[128,128]{1,0:T(8,128)} %wq_ref.2) | copy-start | bytes 196612
  3.3 9.2 %copy-start.3 = (f32[128,4]{0,1:T(4,128)S(1)}, f32[128,4]{0,1:T(4,128)}, u32[]{:S(2)}) copy-start(f32[128,4]{0,1:T(4,128)} %param.28) | copy-start | bytes 6148
  3.3 9.2 %copy-start.5 = (f32[128]{0:T(128)S(1)}, f32[128]{0:T(128)}, u32[]{:S(2)}) copy-start(f32[128]{0:T(128)} %param.31) | copy-start | bytes 1540
  3.3 9.2 %copy-start.6 = (f32[128]{0:T(128)S(1)}, f32[128]{0:T(128)}, u32[]{:S(2)}) copy-start(f32[128]{0:T(128)} %param.23) | copy-start | bytes 1540
  3.4 8.6 %collective-permute-start.5 = (f32[72,128]{1,0:T(8,128)}, f32[72,128]{1,0:T(8,128)S(1)}, u32[]{:S(2)}, u32[]{:S(2)}) collective-permute-start(f32[72,128]{1,0:T(8,128)} %get-tuple-element.55.b0_ref), channel_id=1, source_target_pairs={{0,24},{4,28},{8,16},{12,20},{16,8},{20,12},{24,0},{28,4},{1,25},{... | collective-permute-start | bytes 110600 | tf_op jit(solution)/shard_map/ppermute | solution.py:714
  7.3 11.3 %collective-permute-start.4 = (f32[72,128]{1,0:T(8,128)}, f32[72,128]{1,0:T(8,128)S(1)}, u32[]{:S(2)}, u32[]{:S(2)}) collective-permute-start(f32[72,128]{1,0:T(8,128)} %get-tuple-element.55.b0_ref), channel_id=1, source_target_pairs={{0,16},{4,20},{8,24},{12,28},{16,0},{20,4},{24,8},{28,12},{1,17},{... | collective-permute-start | bytes 110600 | tf_op jit(solution)/shard_map/ppermute | solution.py:714
  7.8 10.8 %collective-permute-start.3 = (f32[72,128]{1,0:T(8,128)}, f32[72,128]{1,0:T(8,128)S(1)}, u32[]{:S(2)}, u32[]{:S(2)}) collective-permute-start(f32[72,128]{1,0:T(8,128)} %get-tuple-element.55.b0_ref), channel_id=1, source_target_pairs={{0,8},{4,12},{8,0},{12,4},{16,24},{20,28},{24,16},{28,20},{1,9},{5... | collective-permute-start | bytes 110600 | tf_op jit(solution)/shard_map/ppermute | solution.py:714
  8.0 11.4 %collective-permute-start.2 = (f32[120,256]{1,0:T(8,128)}, f32[120,256]{1,0:T(8,128)S(1)}, u32[]{:S(2)}, u32[]{:S(2)}) collective-permute-start(f32[120,256]{1,0:T(8,128)} %get-tuple-element.54.p0_ref.y0_ref.y_ref), channel_id=1, source_target_pairs={{0,3},{1,2},{2,1},{3,0},{4,7},{5,6},{6,5},{7,4},{8,11},{9,10},{10,... | collective-permute-start | bytes 368648 | tf_op jit(solution)/shard_map/ppermute | solution.py:714
  12.0 9.7 %collective-permute-start.1 = (f32[120,256]{1,0:T(8,128)}, f32[120,256]{1,0:T(8,128)S(1)}, u32[]{:S(2)}, u32[]{:S(2)}) collective-permute-start(f32[120,256]{1,0:T(8,128)} %get-tuple-element.54.p0_ref.y0_ref.y_ref), channel_id=1, source_target_pairs={{0,2},{1,3},{2,0},{3,1},{4,6},{5,7},{6,4},{7,5},{8,10},{9,11},{10,... | collective-permute-start | bytes 368648 | tf_op jit(solution)/shard_map/ppermute | solution.py:714
  12.0 9.7 %collective-permute-start = (f32[120,256]{1,0:T(8,128)}, f32[120,256]{1,0:T(8,128)S(1)}, u32[]{:S(2)}, u32[]{:S(2)}) collective-permute-start(f32[120,256]{1,0:T(8,128)} %get-tuple-element.54.p0_ref.y0_ref.y_ref), channel_id=1, source_target_pairs={{0,1},{1,0},{2,3},{3,2},{4,5},{5,4},{6,7},{7,6},{8,9},{9,8},{10,11... | collective-permute-start | bytes 368648 | tf_op jit(solution)/shard_map/ppermute | solution.py:714
  17.0 8.3 %copy-start.13 = (f32[2,48,256]{2,1,0:T(8,128)S(1)}, f32[2,48,256]{2,1,0:T(8,128)}, u32[]{:S(2)}) copy-start(f32[2,48,256]{2,1,0:T(8,128)} %adj_ref.3) | copy-start | bytes 294916
  18.7 6.6 %copy-start.10 = (f32[256,256]{1,0:T(8,128)S(1)}, f32[256,256]{1,0:T(8,128)}, u32[]{:S(2)}) copy-start(f32[256,256]{1,0:T(8,128)} %wv_ref.3) | copy-start | bytes 786436
  18.7 6.6 %copy-start.11 = (f32[256,256]{1,0:T(8,128)S(1)}, f32[256,256]{1,0:T(8,128)}, u32[]{:S(2)}) copy-start(f32[256,256]{1,0:T(8,128)} %wg_ref.3) | copy-start | bytes 786436
  18.7 6.6 %copy-start.12 = (f32[256,256]{1,0:T(8,128)S(1)}, f32[256,256]{1,0:T(8,128)}, u32[]{:S(2)}) copy-start(f32[256,256]{1,0:T(8,128)} %wo_ref.3) | copy-start | bytes 786436
  18.8 7.9 %collective-permute-start.10 = (f32[3,72,128]{2,1,0:T(8,128)S(1)}, f32[3,72,128]{2,1,0:T(8,128)S(1)}, u32[]{:S(2)}, u32[]{:S(2)}) collective-permute-start(f32[3,72,128]{2,1,0:T(8,128)S(1)} %stack_chips.2.after_ref.b1_ref), channel_id=1, source_target_pairs={{0,4},{4,0},{8,12},{12,8},{16,20},{20,16},{24,28},{28,24},{1,5},{5... | collective-permute-start | bytes 331784 | tf_op jit(solution)/shard_map/ppermute | solution.py:714
  18.9 7.8 %collective-permute-start.9 = (f32[72,128]{1,0:T(8,128)S(1)}, f32[72,128]{1,0:T(8,128)S(1)}, u32[]{:S(2)}, u32[]{:S(2)}) collective-permute-start(f32[72,128]{1,0:T(8,128)S(1)} %copy-done.19), channel_id=1, source_target_pairs={{0,4},{4,0},{8,12},{12,8},{16,20},{20,16},{24,28},{28,24},{1,5},{5... | collective-permute-start | bytes 110600 | tf_op jit(solution)/shard_map/ppermute | solution.py:714
  21.8 7.8 %collective-permute-start.8 = (f32[144,128]{1,0:T(8,128)S(1)}, f32[144,128]{1,0:T(8,128)S(1)}, u32[]{:S(2)}, u32[]{:S(2)}) collective-permute-start(f32[144,128]{1,0:T(8,128)S(1)} %stack_rows.1.b0_ref), channel_id=1, source_target_pairs={{0,24},{4,28},{8,16},{12,20},{16,8},{20,12},{24,0},{28,4},{1,25},{... | collective-permute-start | bytes 221192 | tf_op jit(solution)/shard_map/ppermute | solution.py:714
  24.3 5.3 %collective-permute-start.7 = (f32[144,128]{1,0:T(8,128)S(1)}, f32[144,128]{1,0:T(8,128)S(1)}, u32[]{:S(2)}, u32[]{:S(2)}) collective-permute-start(f32[144,128]{1,0:T(8,128)S(1)} %stack_rows.1.b0_ref), channel_id=1, source_target_pairs={{0,16},{4,20},{8,24},{12,28},{16,0},{20,4},{24,8},{28,12},{1,17},{... | collective-permute-start | bytes 221192 | tf_op jit(solution)/shard_map/ppermute | solution.py:714
  24.8 4.8 %collective-permute-start.6 = (f32[144,128]{1,0:T(8,128)S(1)}, f32[144,128]{1,0:T(8,128)S(1)}, u32[]{:S(2)}, u32[]{:S(2)}) collective-permute-start(f32[144,128]{1,0:T(8,128)S(1)} %stack_rows.1.b0_ref), channel_id=1, source_target_pairs={{0,8},{4,12},{8,0},{12,4},{16,24},{20,28},{24,16},{28,20},{1,9},{5... | collective-permute-start | bytes 221192 | tf_op jit(solution)/shard_map/ppermute | solution.py:714
  29.6 1.7 %collective-permute-start.12 = (f32[3,144,128]{2,1,0:T(8,128)S(1)}, f32[3,144,128]{2,1,0:T(8,128)S(1)}, u32[]{:S(2)}, u32[]{:S(2)}) collective-permute-start(f32[3,144,128]{2,1,0:T(8,128)S(1)} %stack_chips.3.b1_ref), channel_id=1, source_target_pairs={{0,4},{4,0},{8,12},{12,8},{16,20},{20,16},{24,28},{28,24},{1,5},{5... | collective-permute-start | bytes 663560 | tf_op jit(solution)/shard_map/ppermute | solution.py:714
  29.7 1.6 %collective-permute-start.11 = (f32[144,128]{1,0:T(8,128)S(1)}, f32[144,128]{1,0:T(8,128)S(1)}, u32[]{:S(2)}, u32[]{:S(2)}) collective-permute-start(f32[144,128]{1,0:T(8,128)S(1)} %stack_rows.1.b0_ref), channel_id=1, source_target_pairs={{0,4},{4,0},{8,12},{12,8},{16,20},{20,16},{24,28},{28,24},{1,5},{5... | collective-permute-start | bytes 221192 | tf_op jit(solution)/shard_map/ppermute | solution.py:714
  30.2 10.0 %collective-permute-start.14 = (f32[4,48,192]{2,1,0:T(8,128)S(1)}, f32[4,48,192]{2,1,0:T(8,128)S(1)}, u32[]{:S(2)}, u32[]{:S(2)}) collective-permute-start(f32[4,48,192]{2,1,0:T(8,128)S(1)} %get-tuple-element.72), channel_id=1, source_target_pairs={{0,4},{4,0},{8,12},{12,8},{16,20},{20,16},{24,28},{28,24},{1,5},{5... | collective-permute-start | bytes 442376 | tf_op jit(solution)/shard_map/ppermute | solution.py:714
  30.3 14.2 %collective-permute-start.18 = (f32[192,256]{1,0:T(8,128)S(1)}, f32[192,256]{1,0:T(8,128)S(1)}, u32[]{:S(2)}, u32[]{:S(2)}) collective-permute-start(f32[192,256]{1,0:T(8,128)S(1)} %get-tuple-element.78), channel_id=1, source_target_pairs={{0,2},{1,3},{2,0},{3,1},{4,6},{5,7},{6,4},{7,5},{8,10},{9,11},{10,... | collective-permute-start | bytes 589832 | tf_op jit(solution)/shard_map/ppermute | solution.py:714
  38.6 1.8 %collective-permute-start.13 = (f32[4,4,24,192]{3,2,1,0:T(8,128)S(1)}, f32[4,4,24,192]{3,2,1,0:T(8,128)S(1)}, u32[]{:S(2)}, u32[]{:S(2)}) collective-permute-start(f32[4,4,24,192]{3,2,1,0:T(8,128)S(1)} %get-tuple-element.70), channel_id=1, source_target_pairs={{0,4},{4,0},{8,12},{12,8},{16,20},{20,16},{24,28},{28,24},{1,5},{5... | collective-permute-start | bytes 884744 | tf_op jit(solution)/shard_map/ppermute | solution.py:714
  40.5 5.2 %collective-permute-start.15 = (f32[216,128]{1,0:T(8,128)S(1)}, f32[216,128]{1,0:T(8,128)S(1)}, u32[]{:S(2)}, u32[]{:S(2)}) collective-permute-start(f32[216,128]{1,0:T(8,128)S(1)} %get-tuple-element.74), channel_id=1, source_target_pairs={{0,8},{4,12},{8,0},{12,4},{16,24},{20,28},{24,16},{28,20},{1,9},{5... | collective-permute-start | bytes 331784 | tf_op jit(solution)/shard_map/ppermute | solution.py:714
  42.1 7.2 %collective-permute-start.16 = (f32[216,128]{1,0:T(8,128)S(1)}, f32[216,128]{1,0:T(8,128)S(1)}, u32[]{:S(2)}, u32[]{:S(2)}) collective-permute-start(f32[216,128]{1,0:T(8,128)S(1)} %get-tuple-element.75), channel_id=1, source_target_pairs={{0,16},{4,20},{8,24},{12,28},{16,0},{20,4},{24,8},{28,12},{1,17},{... | collective-permute-start | bytes 331784 | tf_op jit(solution)/shard_map/ppermute | solution.py:714
  43.6 5.7 %collective-permute-start.17 = (f32[216,128]{1,0:T(8,128)S(1)}, f32[216,128]{1,0:T(8,128)S(1)}, u32[]{:S(2)}, u32[]{:S(2)}) collective-permute-start(f32[216,128]{1,0:T(8,128)S(1)} %get-tuple-element.76), channel_id=1, source_target_pairs={{0,24},{4,28},{8,16},{12,20},{16,8},{20,12},{24,0},{28,4},{1,25},{... | collective-permute-start | bytes 331784 | tf_op jit(solution)/shard_map/ppermute | solution.py:714
  49.4 5.2 %collective-permute-start.19 = (f32[120,256]{1,0:T(8,128)S(1)}, f32[120,256]{1,0:T(8,128)S(1)}, u32[]{:S(2)}, u32[]{:S(2)}) collective-permute-start(f32[120,256]{1,0:T(8,128)S(1)} %get-tuple-element.85), channel_id=1, source_target_pairs={{0,1},{1,0},{2,3},{3,2},{4,5},{5,4},{6,7},{7,6},{8,9},{9,8},{10,11... | collective-permute-start | bytes 368648 | tf_op jit(solution)/shard_map/ppermute | solution.py:714
  51.5 5.0 %collective-permute-start.20 = (f32[24,192]{1,0:T(8,128)S(1)}, f32[24,192]{1,0:T(8,128)S(1)}, u32[]{:S(2)}, u32[]{:S(2)}) collective-permute-start(f32[24,192]{1,0:T(8,128)S(1)} %get-tuple-element.86), channel_id=1, source_target_pairs={{0,2},{1,3},{2,0},{3,1},{4,6},{5,7},{6,4},{7,5},{8,10},{9,11},{10,... | collective-permute-start | bytes 55304 | tf_op jit(solution)/shard_map/ppermute | solution.py:714
  52.5 5.6 %collective-permute-start.21 = (f32[24,192]{1,0:T(8,128)S(1)}, f32[24,192]{1,0:T(8,128)S(1)}, u32[]{:S(2)}, u32[]{:S(2)}) collective-permute-start(f32[24,192]{1,0:T(8,128)S(1)} %get-tuple-element.87), channel_id=1, source_target_pairs={{0,3},{1,2},{2,1},{3,0},{4,7},{5,6},{6,5},{7,4},{8,11},{9,10},{10,... | collective-permute-start | bytes 55304 | tf_op jit(solution)/shard_map/ppermute | solution.py:714
  (10 other events, 26.1 us)
